TPU v7x, 32 devices: a whole 2x2x4 slice. The times are simulated.
32 devices in a mesh: dp: 4 (over z), fsdp: 8 (over y, x, core).
Axes of the slice: x: 2, y: 2, z: 4, core: 2. Of those that a mesh axis runs over, the one named last changes fastest.
Arguments:
- tokens: bfloat16 [8192, 2048], P(('dp', 'fsdp')), may hold values from -6 to 6
- cotangent: bfloat16 [8192, 2048], P(('dp', 'fsdp')), may hold values from -6 to 6
- query_weight: bfloat16 [2048, 2048], P(('dp', 'fsdp')), may hold values from -0.5 to 0.5
- key_weight: bfloat16 [2048, 512], P(('dp', 'fsdp')), may hold values from -0.5 to 0.5
- value_weight: bfloat16 [2048, 512], P(('dp', 'fsdp')), may hold values from -0.125 to 0.125
- output_weight: bfloat16 [2048, 2048], P(('dp', 'fsdp')), may hold values from -1.5 to 1.5
- gate_weight: bfloat16 [2048, 8192], P(('dp', 'fsdp')), may hold values from -0.125 to 0.125
- up_weight: bfloat16 [2048, 8192], P(('dp', 'fsdp')), may hold values from -0.125 to 0.125
- down_weight: bfloat16 [8192, 2048], P(('dp', 'fsdp')), may hold values from -0.375 to 0.375
- attention_gain: bfloat16 [2048], P(('dp', 'fsdp')), may hold values from 0.099609375 to 1.8984375
- feedforward_gain: bfloat16 [2048], P(('dp', 'fsdp')), may hold values from 0.099609375 to 1.8984375
- lengths: int32 [4, 4], P('dp'), may hold values from 1 to 1024, as said below
Outputs:
- output: bfloat16 [8192, 2048], P(('dp', 'fsdp'))
- grad_input: bfloat16 [8192, 2048], P(('dp', 'fsdp'))
- grad_query: float32 [2048, 2048], P(('dp', 'fsdp'))
- grad_key: float32 [2048, 512], P(('dp', 'fsdp'))
- grad_value: float32 [2048, 512], P(('dp', 'fsdp'))
- grad_out: float32 [2048, 2048], P(('dp', 'fsdp'))
- grad_gate: float32 [2048, 8192], P(('dp', 'fsdp'))
- grad_up: float32 [2048, 8192], P(('dp', 'fsdp'))
- grad_down: float32 [8192, 2048], P(('dp', 'fsdp'))
- grad_attention_gain: float32 [2048], P(('dp', 'fsdp'))
- grad_feedforward_gain: float32 [2048], P(('dp', 'fsdp'))
Inputs may be any that keep to these rules, and one draw needn't show every extreme that they name: Row g gives the lengths of the 4 sequences that fill group g's 2048 tokens one after another; every row sums to 2048, and its longest sequence has exactly 1024 tokens.
All inputs are finite; a program needn't handle non-finite values.
Results may differ from a plain program's by a relative error of at most 0.023.
Values may be sent and summed in bfloat16 or wider, within the bound.
A program may use at most 640 MiB of HBM per device.

v0:
```python
import jax
import jax.numpy as jnp
from jax import lax
from jax.sharding import PartitionSpec as P

D = 2048
NH = 32
KVH = 8
HD = 64
FF = 8192


EPSILON = 1e-05
RESIDUAL_SCALE = 0.22
ATTENTION_SCALE = 0.015625
ROPE_BASE = 10000000.0
MASKED = -1e30
block_limit = 256


def plain_product(left, right):
    return jnp.dot(left, right, preferred_element_type=jnp.float32)


def product_transposed(left, right):
    return lax.dot_general(
        left, right, (((1,), (1,)), ((), ())), preferred_element_type=jnp.float32
    )


def product_leading(left, right):
    return lax.dot_general(
        left, right, (((0,), (0,)), ((), ())), preferred_element_type=jnp.float32
    )


def block_size(length):
    chosen = 1
    for candidate in range(1, min(length, block_limit) + 1):
        if length % candidate == 0:
            chosen = candidate
    return chosen


def rotate(values, positions, head_count, direction):
    row_count = values.shape[0]
    head_width = values.shape[1] // head_count
    half_width = head_width // 2
    frequency = ROPE_BASE ** (-(2.0 * jnp.arange(half_width, dtype=jnp.float32)) / head_width)
    angles = positions.astype(jnp.float32)[:, None] * frequency[None, :]
    cosine = jnp.cos(angles)[:, None, :]
    sine_part = direction * jnp.sin(angles)[:, None, :]
    reshaped_rows = values.reshape(row_count, head_count, head_width)
    first_half = reshaped_rows[:, :, :half_width]
    second_half = reshaped_rows[:, :, half_width:]
    turned = jnp.concatenate(
        [
            first_half * cosine - second_half * sine_part,
            second_half * cosine + first_half * sine_part,
        ],
        axis=2,
    )
    return turned.reshape(row_count, head_count * head_width)


def sequence_tables(lengths_row, group_tokens):
    sequence_count = lengths_row.shape[0]
    finish = jnp.cumsum(lengths_row)
    opening = finish - lengths_row
    token_place = jnp.arange(group_tokens, dtype=jnp.int32)
    segment = jnp.sum((token_place[:, None] >= finish[None, :]).astype(jnp.int32), axis=1)
    member = segment[:, None] == jnp.arange(sequence_count, dtype=jnp.int32)[None, :]
    first_place = jnp.sum(jnp.where(member, opening[None, :], 0), axis=1)
    return (segment, token_place - first_place)


def body(
    tokens,
    cotangent,
    query_weight,
    key_weight,
    value_weight,
    output_weight,
    gate_weight,
    up_weight,
    down_weight,
    attention_gain,
    feedforward_gain,
    lengths,
):
    tok_rows = tokens.shape[0]
    model_width = tokens.shape[1]
    kv_width = key_weight.shape[1]
    weight_rows = query_weight.shape[0]
    member_count = lax.axis_size("fsdp")
    group_tokens = tok_rows * member_count
    member_index = lax.axis_index("fsdp")
    group_size = NH // KVH
    down_ratio = FF // D
    segment, position = sequence_tables(lengths[0], group_tokens)
    own_start = member_index * tok_rows
    share_rows = tok_rows // member_count
    holder_ids = jnp.arange(member_count, dtype=jnp.int32)[:, None, None]
    sender_ids = jnp.arange(member_count, dtype=jnp.int32)[None, :, None]
    row_ids = jnp.arange(share_rows, dtype=jnp.int32)[None, None, :]
    source = (sender_ids * tok_rows + holder_ids * share_rows + row_ids).reshape(group_tokens)
    tokens_here, cotangent_here = (
        lax.all_to_all(tokens, "fsdp", split_axis=0, concat_axis=0, tiled=True),
        lax.all_to_all(cotangent, "fsdp", split_axis=0, concat_axis=0, tiled=True),
    )
    key_segment = segment[source]
    key_position = position[source]
    query_segment = lax.dynamic_slice_in_dim(key_segment, own_start, tok_rows)
    query_position = lax.dynamic_slice_in_dim(key_position, own_start, tok_rows)
    inputs = tokens_here.astype(jnp.float32)
    inverse_one = lax.rsqrt(jnp.mean(inputs * inputs, axis=1, keepdims=True) + EPSILON)
    query_piece = lax.all_gather(query_weight, ("dp", "fsdp"), axis=0, tiled=True)
    key_piece = lax.all_gather(key_weight, ("dp", "fsdp"), axis=0, tiled=True)
    value_piece = lax.all_gather(value_weight, ("dp", "fsdp"), axis=0, tiled=True)
    out_piece = lax.all_gather(output_weight, ("dp", "fsdp"), axis=0, tiled=True)
    gain_piece = lax.all_gather(attention_gain, ("dp", "fsdp"), axis=0, tiled=True)
    columns = inputs
    gain_float = gain_piece.astype(jnp.float32)
    scaled = (columns * inverse_one * gain_float[None, :]).astype(jnp.bfloat16)
    query_sum = plain_product(scaled, query_piece)
    key_sum = plain_product(scaled, key_piece)
    value_sum = plain_product(scaled, value_piece)
    normed_one = scaled
    gain_one = gain_float
    query_low = rotate(query_sum, query_position, NH, 1.0).astype(jnp.bfloat16)
    key_low = rotate(key_sum, query_position, KVH, 1.0).astype(jnp.bfloat16)
    value_low = value_sum.astype(jnp.bfloat16)
    both_kv = jnp.concatenate([key_low, value_low], axis=1)
    all_kv = lax.all_gather(both_kv, "fsdp", axis=0, tiled=True)
    query_split_heads = query_low.reshape(tok_rows, KVH, group_size, HD)
    key_step = block_size(group_tokens)

    def visible_at(key_start, key_count):
        block_segment = lax.dynamic_slice_in_dim(key_segment, key_start, key_count)
        block_place = lax.dynamic_slice_in_dim(key_position, key_start, key_count)
        return (query_segment[:, None] == block_segment[None, :]) & (
            block_place[None, :] <= query_position[:, None]
        )

    def scores_at(key_start, key_count):
        kv_rows = lax.dynamic_slice_in_dim(all_kv, key_start, key_count, 0)
        key_section = kv_rows[:, :kv_width].reshape(key_count, KVH, HD)
        value_section = kv_rows[:, kv_width:].reshape(key_count, KVH, HD)
        scores = (
            jnp.einsum(
                "akzv,ikv->kzai", query_split_heads, key_section, preferred_element_type=jnp.float32
            )
            * ATTENTION_SCALE
        )
        return (scores, key_section, value_section)

    def forward_block(block_index, carried):
        key_start = block_index * key_step
        visible = visible_at(key_start, key_step)

        def forward_compute(current):
            running_max, running_sum, gathered = current
            scores, key_section, value_section = scores_at(key_start, key_step)
            masked = jnp.where(visible[None, None], scores, MASKED)
            new_max = jnp.maximum(running_max, jnp.max(masked, axis=3))
            weights = jnp.where(visible[None, None], jnp.exp(masked - new_max[..., None]), 0.0)
            rescale = jnp.exp(running_max - new_max)
            new_sum = running_sum * rescale + jnp.sum(weights, axis=3)
            new_gathered = gathered * jnp.transpose(rescale, (2, 0, 1))[..., None] + jnp.einsum(
                "ymqp,pyj->qymj",
                weights.astype(jnp.bfloat16),
                value_section,
                preferred_element_type=jnp.float32,
            )
            return (new_max, new_sum, new_gathered)

        return lax.cond(jnp.any(visible), forward_compute, lambda current: current, carried)

    forward_start = (
        jnp.full((KVH, group_size, tok_rows), MASKED, jnp.float32),
        jnp.zeros((KVH, group_size, tok_rows), jnp.float32),
        jnp.zeros((tok_rows, KVH, group_size, HD), jnp.float32),
    )
    running_max, running_sum, gathered = lax.fori_loop(
        0, group_tokens // key_step, forward_block, forward_start
    )
    log_total = running_max + jnp.log(running_sum)
    attn_out = (gathered / jnp.transpose(running_sum, (2, 0, 1))[..., None]).reshape(
        tok_rows, model_width
    )
    out_low = attn_out.astype(jnp.bfloat16)
    mixed = inputs + RESIDUAL_SCALE * plain_product(out_low, out_piece)
    inverse_two = lax.rsqrt(jnp.mean(mixed * mixed, axis=1, keepdims=True) + EPSILON)
    gate_piece = lax.all_gather(gate_weight, ("dp", "fsdp"), axis=0, tiled=True)
    up_piece = lax.all_gather(up_weight, ("dp", "fsdp"), axis=0, tiled=True)
    gain_piece = lax.all_gather(feedforward_gain, ("dp", "fsdp"), axis=0, tiled=True)
    columns = mixed
    gain_float = gain_piece.astype(jnp.float32)
    scaled = (columns * inverse_two * gain_float[None, :]).astype(jnp.bfloat16)
    gate_sum = plain_product(scaled, gate_piece)
    up_sum = plain_product(scaled, up_piece)
    sigmoid_gate = jax.nn.sigmoid(gate_sum)
    activated = gate_sum * sigmoid_gate
    hidden_low = (jax.nn.silu(gate_sum) * up_sum).astype(jnp.bfloat16)
    columns = hidden_low
    down_sum = plain_product(
        columns, lax.all_gather(down_weight, ("dp", "fsdp"), axis=0, tiled=True)
    )
    output_low = (mixed + RESIDUAL_SCALE * down_sum).astype(jnp.bfloat16)
    upstream = cotangent_here.astype(jnp.float32)
    grad_two = (RESIDUAL_SCALE * upstream).astype(jnp.bfloat16)
    grad_hidden = product_transposed(
        grad_two, lax.all_gather(down_weight, ("dp", "fsdp"), axis=0, tiled=True)
    )
    grad_gate_low = (
        grad_hidden * up_sum * sigmoid_gate * (1.0 + gate_sum * (1.0 - sigmoid_gate))
    ).astype(jnp.bfloat16)
    grad_up_low = (grad_hidden * activated).astype(jnp.bfloat16)
    gate_piece = lax.all_gather(gate_weight, ("dp", "fsdp"), axis=0, tiled=True)
    up_piece = lax.all_gather(up_weight, ("dp", "fsdp"), axis=0, tiled=True)
    column_part = product_transposed(grad_gate_low, gate_piece) + product_transposed(
        grad_up_low, up_piece
    )
    grad_normed_two = column_part
    weighted_two = grad_normed_two * gain_float[None, :]
    grad_mixed = (
        upstream
        + inverse_two * weighted_two
        - mixed * inverse_two**3 * jnp.mean(weighted_two * mixed, axis=1, keepdims=True)
    )
    gain_term_two = jnp.sum(grad_normed_two * mixed * inverse_two, axis=0)
    grad_one = (RESIDUAL_SCALE * grad_mixed).astype(jnp.bfloat16)
    grad_attn_low = product_transposed(grad_one, out_piece).astype(jnp.bfloat16)
    gradient_split_heads = grad_attn_low.reshape(tok_rows, KVH, group_size, HD)
    correction = jnp.transpose(
        jnp.sum(
            (grad_attn_low.astype(jnp.float32) * attn_out).reshape(tok_rows, KVH, group_size, HD),
            axis=3,
        ),
        (1, 2, 0),
    )

    def score_grads(key_start, key_count, visible):
        scores, key_section, value_section = scores_at(key_start, key_count)
        probabilities = jnp.where(visible[None, None], jnp.exp(scores - log_total[..., None]), 0.0)
        pressure = jnp.einsum(
            "akzv,ikv->kzai",
            gradient_split_heads,
            value_section,
            preferred_element_type=jnp.float32,
        )
        gradient_logits = (probabilities * (pressure - correction[..., None])).astype(jnp.bfloat16)
        return (probabilities, gradient_logits, key_section)

    def query_back(block_index, carried):
        key_start = block_index * key_step
        visible = visible_at(key_start, key_step)

        def query_compute(current):
            probabilities, gradient_logits, key_section = score_grads(key_start, key_step, visible)
            return (
                current
                + jnp.einsum(
                    "ymqp,pyj->qymj",
                    gradient_logits,
                    key_section,
                    preferred_element_type=jnp.float32,
                )
                * ATTENTION_SCALE
            )

        return lax.cond(jnp.any(visible), query_compute, lambda current: current, carried)

    grad_query_turned = lax.fori_loop(
        0,
        group_tokens // key_step,
        query_back,
        jnp.zeros((tok_rows, KVH, group_size, HD), jnp.float32),
    )
    first_row = jnp.int32(0)
    sub_step = block_size(tok_rows * lax.axis_size("fsdp"))

    def one_block(block_index, buffer):
        key_start = first_row + block_index * sub_step
        visible = visible_at(key_start, sub_step)

        def one_compute(ignored):
            probabilities, gradient_logits, key_section = score_grads(key_start, sub_step, visible)
            grad_keys = (
                jnp.einsum(
                    "mlpe,pmlj->emj",
                    gradient_logits,
                    query_split_heads,
                    preferred_element_type=jnp.float32,
                )
                * ATTENTION_SCALE
            )
            grad_values = jnp.einsum(
                "mlpe,pmlj->emj",
                probabilities.astype(jnp.bfloat16),
                gradient_split_heads,
                preferred_element_type=jnp.float32,
            )
            return jnp.concatenate(
                [grad_keys.reshape(sub_step, kv_width), grad_values.reshape(sub_step, kv_width)],
                axis=1,
            )

        piece_terms = lax.cond(
            jnp.any(visible),
            one_compute,
            lambda ignored: jnp.zeros((sub_step, 2 * kv_width), jnp.float32),
            None,
        )
        return lax.dynamic_update_slice_in_dim(buffer, piece_terms, block_index * sub_step, 0)

    kv_summed = lax.psum_scatter(
        lax.fori_loop(
            0,
            tok_rows * lax.axis_size("fsdp") // sub_step,
            one_block,
            jnp.zeros((tok_rows * lax.axis_size("fsdp"), 2 * kv_width), jnp.float32),
        ).astype(jnp.bfloat16),
        "fsdp",
        scatter_dimension=0,
        tiled=True,
    ).astype(jnp.float32)
    grad_query_low = rotate(
        grad_query_turned.reshape(tok_rows, model_width), query_position, NH, -1.0
    ).astype(jnp.bfloat16)
    grad_key_low = rotate(kv_summed[:, :kv_width], query_position, KVH, -1.0).astype(jnp.bfloat16)
    grad_value_low = kv_summed[:, kv_width:].astype(jnp.bfloat16)
    query_piece = lax.all_gather(query_weight, ("dp", "fsdp"), axis=0, tiled=True)
    key_piece = lax.all_gather(key_weight, ("dp", "fsdp"), axis=0, tiled=True)
    value_piece = lax.all_gather(value_weight, ("dp", "fsdp"), axis=0, tiled=True)
    column_part = (
        product_transposed(grad_query_low, query_piece)
        + product_transposed(grad_key_low, key_piece)
        + product_transposed(grad_value_low, value_piece)
    )
    weighted_one = column_part * gain_one[None, :]
    grad_inputs = (
        grad_mixed
        + inverse_one * weighted_one
        - inputs * inverse_one**3 * jnp.mean(weighted_one * inputs, axis=1, keepdims=True)
    )
    gain_term_one = jnp.sum(column_part * inputs * inverse_one, axis=0)
    attention_width = 2 * model_width + 2 * kv_width + 128
    down_terms = product_leading(hidden_low, grad_two).reshape(
        weight_rows * lax.axis_size(("dp", "fsdp")), down_ratio * model_width
    )
    joined = lax.psum_scatter(
        jnp.concatenate(
            [
                jnp.concatenate(
                    [
                        product_leading(normed_one, grad_query_low),
                        product_leading(normed_one, grad_key_low),
                        product_leading(normed_one, grad_value_low),
                        product_leading(out_low, grad_one),
                        jnp.broadcast_to(
                            gain_term_one[:, None],
                            (weight_rows * lax.axis_size(("dp", "fsdp")), 128),
                        ),
                    ],
                    axis=1,
                ),
                jnp.concatenate(
                    [
                        product_leading(scaled, grad_gate_low),
                        product_leading(scaled, grad_up_low),
                        down_terms,
                        jnp.broadcast_to(
                            gain_term_two[:, None],
                            (weight_rows * lax.axis_size(("dp", "fsdp")), 128),
                        ),
                    ],
                    axis=1,
                ),
            ],
            axis=1,
        ),
        ("dp", "fsdp"),
        scatter_dimension=0,
        tiled=True,
    )
    attention_summed = joined[:, :attention_width]
    feedforward_summed = joined[:, attention_width:]
    both_low = jnp.concatenate([output_low, grad_inputs.astype(jnp.bfloat16)], axis=1)
    returned_low = lax.all_to_all(both_low, "fsdp", split_axis=0, concat_axis=0, tiled=True)
    grad_query = attention_summed[:, :model_width]
    grad_key = attention_summed[:, model_width : model_width + kv_width]
    grad_value = attention_summed[:, model_width + kv_width : model_width + 2 * kv_width]
    grad_out = attention_summed[:, model_width + 2 * kv_width : 2 * model_width + 2 * kv_width]
    grad_attention_gain = attention_summed[:, 2 * model_width + 2 * kv_width]
    grad_gate = feedforward_summed[:, :FF]
    grad_up = feedforward_summed[:, FF : 2 * FF]
    grad_down = feedforward_summed[:, 2 * FF : 3 * FF].reshape(
        weight_rows * down_ratio, model_width
    )
    grad_feedforward_gain = feedforward_summed[:, 3 * FF]
    return (
        returned_low[:, :model_width],
        returned_low[:, model_width:],
        grad_query,
        grad_key,
        grad_value,
        grad_out,
        grad_gate,
        grad_up,
        grad_down,
        grad_attention_gain,
        grad_feedforward_gain,
    )


def solution(mesh):
    placed = (
        P(("dp", "fsdp"), None),
        P(("dp", "fsdp"), None),
        P(("dp", "fsdp"), None),
        P(("dp", "fsdp"), None),
        P(("dp", "fsdp"), None),
        P(("dp", "fsdp"), None),
        P(("dp", "fsdp"), None),
        P(("dp", "fsdp"), None),
        P(("dp", "fsdp"), None),
        P(("dp", "fsdp")),
        P(("dp", "fsdp")),
        P("dp", None),
    )
    return jax.shard_map(
        body,
        mesh=mesh,
        in_specs=placed,
        out_specs=(
            P(("dp", "fsdp"), None),
            P(("dp", "fsdp"), None),
            P(("dp", "fsdp"), None),
            P(("dp", "fsdp"), None),
            P(("dp", "fsdp"), None),
            P(("dp", "fsdp"), None),
            P(("dp", "fsdp"), None),
            P(("dp", "fsdp"), None),
            P(("dp", "fsdp"), None),
            P(("dp", "fsdp")),
            P(("dp", "fsdp")),
        ),
        check_vma=False,
    )
```

profile of v0, /device:TPU:0, one launch (start us, length us, event | category | flops | bytes accessed | tf_op | source)
XLA Modules:
  0.0 3392.1 jit_solution(7854924041151168897)
XLA Ops:
  17.6 45.2 %all-reduce.2 = (bf16[2048]{0:T(1024)(128)(2,1)S(1)}, bf16[2048]{0:T(1024)(128)(2,1)S(1)}) all-reduce(bf16[2048]{0:T(1024)(128)(2,1)S(1)} %dynamic-update-slice, bf16[2048]{0:T(1024)(128)(2,1)S(1)} %dynamic-update-slice.1), channel_id=1, replica_groups=mesh['dp'=4,'fsdp'=8] {'dp','fsdp'}, use_global_device_ids=true, to_apply=%add | all-reduce | flops 4096 | bytes 16384
  84.4 44.3 %all-gather.11.cloned.1.call-done = bf16[2048,512]{1,0:T(8,128)(2,1)} async-done(((bf16[64,512]{1,0:T(8,128)(2,1)}), bf16[2048,512]{1,0:T(8,128)(2,1)}) %all-gather.11.cloned.1.call-update) | async-done | bytes 2097168 | tf_op jit(solution)/shard_map/all_gather | solution.py:119
  139.9 20.4 gather_fusion
  163.5 15.7 all-gather.13.cloned.1.call-done
  185.7 73.7 %all-gather.15.cloned.1.call-done = bf16[2048,2048]{1,0:T(8,128)(2,1)} async-done(((bf16[64,2048]{1,0:T(8,128)(2,1)}), bf16[2048,2048]{1,0:T(8,128)(2,1)}) %all-gather.15.cloned.1.call-update) | async-done | bytes 8388624 | tf_op jit(solution)/shard_map/all_gather | solution.py:117
  279.5 84.4 %while.46 = (s32[]{:T(128)}, f32[8,4,256]{2,1,0:T(4,128)S(1)}, f32[8,4,256]{2,1,0:T(4,128)S(1)}, f32[256,8,4,64]{0,3,2,1:T(8,128)}, s32[256]{0:T(256)S(1)}, /*in...) while((s32[]{:T(128)}, f32[8,4,256]{2,1,0:T(4,128)S(1)}, ...), condition=%wide.region_10.11_spmd, body=%wide.region_4.10_spmd.sunk | while | flops 565469184 | bytes 49553828 | solution.py:184
  378.2 156.1 %all-gather.23.cloned.1.call-done = bf16[8192,2048]{1,0:T(8,128)(2,1)} async-done(((bf16[256,2048]{1,0:T(8,128)(2,1)}), bf16[8192,2048]{1,0:T(8,128)(2,1)}) %all-gather.23.cloned.1.call-update) | async-done | bytes 33554448 | tf_op jit(solution)/shard_map/all_gather | solution.py:207
  534.3 18.8 fusion.88
  553.1 177.1 %all-gather.19.cloned.1.call-done = bf16[2048,8192]{1,0:T(8,128)(2,1)} async-done(((bf16[64,8192]{1,0:T(8,128)(2,1)}), bf16[2048,8192]{1,0:T(8,128)(2,1)}) %all-gather.19.cloned.1.call-update) | async-done | bytes 33554448 | tf_op jit(solution)/shard_map/all_gather | solution.py:194
  730.1 17.8 fusion.87
  748.0 178.0 %all-gather.21.cloned.1.call-done = bf16[2048,8192]{1,0:T(8,128)(2,1)} async-done(((bf16[64,8192]{1,0:T(8,128)(2,1)}), bf16[2048,8192]{1,0:T(8,128)(2,1)}) %all-gather.21.cloned.1.call-update) | async-done | bytes 33554448 | tf_op jit(solution)/shard_map/all_gather | solution.py:195
  926.0 28.2 multiply_convert_fusion.2
  954.2 17.0 fusion.89
  971.3 18.9 multiply_reduce_fusion
  1004.7 126.3 %while.48 = (s32[]{:T(128)}, bf16[2048,1024]{0,1:T(8,128)(2,1)}, s32[256]{0:T(256)S(1)}, s32[2048]{0:T(1024)}, s32[2048]{0:T(1024)S(1)}, /*index=5*/s32[256]{0:T...) while((s32[]{:T(128)}, bf16[2048,1024]{0,1:T(8,128)(2,1)}, ...), condition=%wide.region_23.24_spmd, body=%wide.region_19.23_spmd.sunk | while | flops 1096286208 | bytes 67412320 | solution.py:318
  1132.2 27.6 fusion.91
  1159.9 79.4 %reshape.383 = f32[2048,8192]{1,0:T(8,128)} reshape(f32[8192,2048]{1,0:T(8,128)} %fusion.91) | data formatting | bytes 134217728 | tf_op jit(solution)/shard_map/reshape | solution.py:349
  1239.5 127.0 %while.47 = (s32[]{:T(128)}, f32[256,8,4,64]{0,3,2,1:T(8,128)S(1)}, s32[256]{0:T(256)S(1)}, s32[2048]{0:T(1024)}, s32[2048]{0:T(1024)S(1)}, /*index=5*/s32[256]{...) while((s32[]{:T(128)}, f32[256,8,4,64]{0,3,2,1:T(8,128)S(1)}, ...), condition=%wide.region_18.19_spmd, body=%wide.region_14.18_spmd.sunk | while | flops 819200000 | bytes 25108816 | solution.py:274
  1400.4 23.6 convolution_dynamic-update-slice_fusion.1
  1423.9 23.2 convolution_dynamic-update-slice_fusion
  1447.2 44.2 %constant_dynamic-update-slice_fusion.1 = f32[2048,29952]{1,0:T(8,128)} fusion(f32[2048,29952]{1,0:T(8,128)} %convolution_dynamic-update-slice_fusion, f32[2048,8192]{1,0:T(8,128)} %reshape.383), kind=kLoop, calls=%fused_computation.135 | loop fusion | bytes 134217728
  1494.4 23.8 fusion.51
  1519.0 29.2 all_to_all.30
  1549.7 1822.9 %reduce-scatter.5.cloned.1.call-done = f32[64,29952]{1,0:T(8,128)} async-done(((f32[2048,29952]{1,0:T(8,128)}), f32[64,29952]{1,0:T(8,128)}) %reduce-scatter.5.cloned.1.call-update) | async-done | bytes 7667728 | tf_op jit(solution)/shard_map/reduce_scatter | solution.py:352
  (465 shorter events, 750.7 us)
Async XLA Ops:
  7.2 70.3 %all-gather.9.cloned.1.call-start = ((), (), s32[]{:S(2)}) async-start(), calls=%async_computation.5 | async-start | bytes 2162688 | tf_op jit(solution)/shard_map/all_gather | solution.py:118
  7.9 67.6 %all-to-all-start = ((bf16[8,32,2048]{2,1,0:T(8,128)(2,1)}), bf16[8,32,2048]{2,1,0:T(8,128)(2,1)S(1)}, u32[]{:S(2)}, u32[]{:S(2)}) async-start(bf16[8,32,2048]{2,1,0:T(8,128)(2,1)} %bitcast.269), calls=%async_computation | async-start | bytes 2097152 | tf_op jit(solution)/shard_map/all_to_all | solution.py:108
  13.1 115.6 %all-gather.11.cloned.1.call-start = ((), (), s32[]{:S(2)}) async-start(), calls=%async_computation.6 | async-start | bytes 2162688 | tf_op jit(solution)/shard_map/all_gather | solution.py:119
  13.8 165.3 %all-gather.13.cloned.1.call-start = ((), (), s32[]{:S(2)}) async-start(), calls=%async_computation.7 | async-start | bytes 4718592 | tf_op jit(solution)/shard_map/all_gather | solution.py:134
  75.5 202.0 %copy-start.28 = (f32[256,32]{0,1:T(8,128)}, f32[256,32]{0,1:T(8,128)S(1)}, u32[]{:S(2)}) copy-start(f32[256,32]{0,1:T(8,128)S(1)} %get-tuple-element.859) | copy-start | bytes 98308
  75.5 294.5 %copy-start.1 = (bf16[8,32,2048]{2,1,0:T(8,128)(2,1)}, bf16[8,32,2048]{2,1,0:T(8,128)(2,1)S(1)}, u32[]{:S(2)}) copy-start(bf16[8,32,2048]{2,1,0:T(8,128)(2,1)S(1)} %all-to-all-done) | copy-start | bytes 3145732
  77.5 194.2 %copy-start.11 = (bf16[8,32,2048]{2,1,0:T(8,128)(2,1)}, bf16[8,32,2048]{2,1,0:T(8,128)(2,1)S(1)}, u32[]{:S(2)}) copy-start(bf16[8,32,2048]{2,1,0:T(8,128)(2,1)S(1)} %fusion.56) | copy-start | bytes 3145732
  132.2 127.1 %all-gather.15.cloned.1.call-start = ((), (), s32[]{:S(2)}) async-start(), calls=%async_computation.8 | async-start | bytes 8650752 | tf_op jit(solution)/shard_map/all_gather | solution.py:117
  132.8 237.2 %all-gather.17.cloned.1.call-start = ((), (), s32[]{:S(2)}) async-start(), calls=%async_computation.9 | async-start | bytes 8650752 | tf_op jit(solution)/shard_map/all_gather | solution.py:120
  133.4 400.9 %all-gather.23.cloned.1.call-start = ((), (), s32[]{:S(2)}) async-start(), calls=%async_computation.12 | async-start | bytes 34603008 | tf_op jit(solution)/shard_map/all_gather | solution.py:207
  134.0 596.2 %all-gather.19.cloned.1.call-start = ((), (), s32[]{:S(2)}) async-start(), calls=%async_computation.10 | async-start | bytes 34603008 | tf_op jit(solution)/shard_map/all_gather | solution.py:194
  134.7 791.3 %all-gather.21.cloned.1.call-start = ((), (), s32[]{:S(2)}) async-start(), calls=%async_computation.11 | async-start | bytes 34603008 | tf_op jit(solution)/shard_map/all_gather | solution.py:195
  135.5 25.6 all-to-all-start.1
  139.7 1238.7 %reduce-scatter.3.cloned.1.call-start = ((), (), s32[]{:S(2)}) async-start(), calls=%async_computation.13 | async-start | bytes 4718592 | tf_op jit(solution)/shard_map/reduce_scatter | solution.py:317
  370.0 164.3 %copy-start.21 = (bf16[256,2048]{1,0:T(8,128)(2,1)S(1)}, bf16[256,2048]{1,0:T(8,128)(2,1)}, u32[]{:S(2)}) copy-start(bf16[256,2048]{1,0:T(8,128)(2,1)} %fusion.52) | copy-start | bytes 3145732
  378.2 547.8 %copy-start.13 = (bf16[256,2048]{1,0:T(8,128)(2,1)}, bf16[256,2048]{1,0:T(8,128)(2,1)S(1)}, u32[]{:S(2)}) copy-start(bf16[256,2048]{1,0:T(8,128)(2,1)S(1)} %multiply_convert_fusion.4) | copy-start | bytes 3145732
  1131.0 28.9 copy-start.34
  1131.0 28.9 copy-start.35
  1131.0 2241.6 %reduce-scatter.5.cloned.1.call-start = ((), (), s32[]{:S(2)}) async-start(), calls=%async_computation.14 | async-start | bytes 253034496 | tf_op jit(solution)/shard_map/reduce_scatter | solution.py:352
  1239.5 127.1 %copy-start.29 = (f32[256,32]{0,1:T(8,128)S(1)}, f32[256,32]{0,1:T(8,128)}, u32[]{:S(2)}) copy-start(f32[256,32]{0,1:T(8,128)} %copy-done.28) | copy-start | bytes 98308
  1239.5 127.1 %copy-start.30 = (f32[256,32]{0,1:T(8,128)S(1)}, f32[256,32]{0,1:T(8,128)}, u32[]{:S(2)}) copy-start(f32[256,32]{0,1:T(8,128)} %get-tuple-element.857) | copy-start | bytes 98308
  1447.2 44.2 %copy-start.38 = (f32[2048]{0:T(1024)S(1)}, f32[2048]{0:T(1024)}, u32[]{:S(2)}) copy-start(f32[2048]{0:T(1024)} %get-tuple-element.749) | copy-start | bytes 24580
  1494.4 23.8 copy-start.17
  1494.4 23.8 copy-start.33
  (53 other events, 299.5 us)
Sparse Core Ops, SparseCore 0:
  10.9 59.6 all-gather.8
  73.4 55.2 all-gather.10
  132.3 46.7 all-gather.12
  181.9 77.4 all-gather.14
  262.1 76.0 all-gather.16
  340.9 193.3 all-gather.22
  537.2 192.9 all-gather.18
  733.0 192.9 all-gather.20
  1131.1 49.4 reduce-scatter.2
  1493.0 1879.5 reduce-scatter.4
where the time goes:
time: 3400 us; the launch traced here: 3390 us
  waiting for transfers between devices  2470 us (73%)
  matrix products  450 us (13%)
  local copies, waits for them, and re-layouts  299 us (9%)
  blocking collectives  74.4 us (2%)
  other arithmetic  54 us (2%)
    reduce_scatter x1, waiting for transfers between devices, body(): lax.psum_scatter(jnp.concatenate([jnp.concatenate([product_leading(normed...  1820 us
    all_gather x1, waiting for transfers between devices, body(): up_piece = lax.all_gather(up_weight, ('dp', 'fsdp'), axis=0, tiled=True)  178 us
    all_gather x1, waiting for transfers between devices, body(): gate_piece = lax.all_gather(gate_weight, ('dp', 'fsdp'), axis=0, tiled=True)  177 us
    all_gather x1, waiting for transfers between devices, body(): lax.all_gather(down_weight, ('dp', 'fsdp'), axis=0, tiled=True)  156 us
    dot_general x7, matrix products, product_leading(): lax.dot_general(left, right, (((0,), (0,)), ((), ())), preferred_element_...  96.6 us
    dot_general x7, matrix products, plain_product(): return jnp.dot(left, right, preferred_element_type=jnp.float32)  87.2 us
    reshape x1, local copies, waits for them, and re-layouts, body(): product_leading(hidden_low, grad_two)  79.4 us
    all_gather x1, waiting for transfers between devices, body(): lax.all_gather(query_weight, ('dp', 'fsdp'), axis=0, tiled=True)  73.7 us
  transfers between devices with their start and end apart: 12, of which 7 were waited for; matrix products, arithmetic and copies ran while one was open for 14% of the time, Pallas kernels for 0%

commit v1 on v0

v1 whole, which is shorter than its diff:
```python
import functools

import jax
import jax.numpy as jnp
from jax import lax
from jax.experimental import pallas as pl
from jax.experimental.pallas import tpu as pltpu
from jax.sharding import PartitionSpec as P

NH = 32
KVH = 8
HD = 64
HALF = HD // 2

EPSILON = 1e-05
RESIDUAL_SCALE = 0.22
ATTENTION_SCALE = 0.015625
ROPE_BASE = 10000000.0
MASKED = -1e30
BLOCK = 256
CHUNKS = 2
PIECES = 4
VMEM_BYTES = 58 * 1024 * 1024
MESH = pl.DeviceIdType.MESH
BF16 = jnp.bfloat16
F32 = jnp.float32


def dot_nn(left, right):
    return jnp.dot(left, right, preferred_element_type=F32)


def dot_nt(left, right):
    return lax.dot_general(left, right, (((1,), (1,)), ((), ())), preferred_element_type=F32)


def dot_tn(left, right):
    return lax.dot_general(left, right, (((0,), (0,)), ((), ())), preferred_element_type=F32)


def flip(index, mask):
    return index + mask * (1 - 2 * ((index // mask) % 2))


def plane_masks(member_count):
    masks = []
    mask = 2
    while mask < member_count:
        masks.append(mask)
        mask *= 2
    return masks


def hop(index, step, masks):
    core = index % 2
    return (1 - core) * flip(index, masks[step]) + core * flip(index, masks[-1 - step])


def walk(index, subset, masks):
    for step in range(len(masks)):
        if (subset >> step) & 1:
            index = hop(index, step, masks)
    return index


def greet(group, member, masks):
    barrier = pltpu.get_barrier_semaphore()
    partners = [hop(member, step, masks) for step in range(len(masks))] + [flip(member, 1)]
    for partner in partners:
        pl.semaphore_signal(barrier, inc=1, device_id=(group, partner), device_id_type=MESH)
    pl.semaphore_wait(barrier, len(partners))


def gather_kernel(
    member_count, own_ref, all_ref, link_send, link_recv, core_send, core_recv, local_sem
):
    group = lax.axis_index("dp")
    member = lax.axis_index("fsdp")
    masks = plane_masks(member_count)
    steps = len(masks)
    rows = own_ref.shape[0]
    piece = rows // PIECES
    greet(group, member, masks)

    def place(block, part):
        return all_ref.at[pl.ds(pl.multiple_of(block * rows + part * piece, piece), piece)]

    def link_copy(step, subset, part):
        number = (1 << step) - 1 + subset
        block = walk(member, subset, masks)
        source = own_ref.at[pl.ds(part * piece, piece)] if subset == 0 else place(block, part)
        return pltpu.make_async_remote_copy(
            source,
            place(block, part),
            link_send.at[number, part],
            link_recv.at[number, part],
            device_id=(group, hop(member, step, masks)),
            device_id_type=MESH,
        )

    def core_copy(subset, part):
        block = walk(member, subset, masks)
        source = own_ref.at[pl.ds(part * piece, piece)] if subset == 0 else place(block, part)
        return pltpu.make_async_remote_copy(
            source,
            place(block, part),
            core_send.at[subset, part],
            core_recv.at[subset, part],
            device_id=(group, flip(member, 1)),
            device_id_type=MESH,
        )

    for part in range(PIECES):
        for step in range(steps):
            link_copy(step, 0, part).start()
    keep = pltpu.make_async_copy(
        own_ref, all_ref.at[pl.ds(pl.multiple_of(member * rows, rows), rows)], local_sem
    )
    keep.start()
    for part in range(PIECES):
        core_copy(0, part).start()
    for step in range(steps):
        for part in range(PIECES):
            for subset in range(1 << step):
                link_copy(step, subset, part).wait_recv()
                arrived = subset | (1 << step)
                for later in range(step + 1, steps):
                    link_copy(later, arrived, part).start()
                core_copy(arrived, part).start()
    for part in range(PIECES):
        for subset in range(1 << steps):
            core_copy(subset, part).wait()
    for part in range(PIECES):
        for step in range(steps):
            for subset in range(1 << step):
                link_copy(step, subset, part).wait_send()
    keep.wait()


def plane_gather(own, member_count, collective_id):
    rows, width = own.shape
    steps = len(plane_masks(member_count))
    blocks = 1 << steps
    total = member_count * rows
    return pl.pallas_call(
        functools.partial(gather_kernel, member_count),
        out_shape=jax.ShapeDtypeStruct((total, width), own.dtype),
        in_specs=[pl.BlockSpec(memory_space=pl.ANY)],
        out_specs=pl.BlockSpec(memory_space=pl.ANY),
        scratch_shapes=[
            pltpu.SemaphoreType.DMA((blocks - 1, PIECES)),
            pltpu.SemaphoreType.DMA((blocks - 1, PIECES)),
            pltpu.SemaphoreType.DMA((blocks, PIECES)),
            pltpu.SemaphoreType.DMA((blocks, PIECES)),
            pltpu.SemaphoreType.DMA,
        ],
        compiler_params=pltpu.CompilerParams(collective_id=collective_id, has_side_effects=True),
        cost_estimate=pl.CostEstimate(
            flops=0, bytes_accessed=60 * total * width, transcendentals=0
        ),
        name="plane_gather",
    )(own)


def scatter_kernel(
    member_count,
    part_ref,
    sum_ref,
    core_buffer,
    link_buffer,
    held,
    link_send,
    link_recv,
    core_send,
    core_recv,
):
    group = lax.axis_index("dp")
    member = lax.axis_index("fsdp")
    sibling = flip(member, 1)
    masks = plane_masks(member_count)
    steps = len(masks)
    blocks = 1 << steps
    rows = sum_ref.shape[0]
    piece = rows // PIECES
    greet(group, member, masks)

    def source_rows(block, part):
        return pl.ds(pl.multiple_of(block * rows + part * piece, piece), piece)

    def core_copy(subset, part):
        block = walk(sibling, subset, masks)
        return pltpu.make_async_remote_copy(
            part_ref.at[source_rows(block, part)],
            core_buffer.at[subset, pl.ds(part * piece, piece)],
            core_send.at[subset, part],
            core_recv.at[subset, part],
            device_id=(group, sibling),
            device_id_type=MESH,
        )

    def slot(step, kept):
        return sum(blocks >> (s + 1) for s in range(step)) + (kept >> (step + 1))

    def link_copy(step, subset, part):
        kept = subset & ~(1 << step)
        number = slot(step, kept)
        return pltpu.make_async_remote_copy(
            held.at[subset, pl.ds(part * piece, piece)],
            link_buffer.at[number, pl.ds(part * piece, piece)],
            link_send.at[number, part],
            link_recv.at[number, part],
            device_id=(group, hop(member, step, masks)),
            device_id_type=MESH,
        )

    order = sorted(range(blocks), key=lambda s: (-(s & 1), -s))
    for part in range(PIECES):
        for subset in order:
            core_copy(subset, part).start()
    for part in range(PIECES):
        where = pl.ds(part * piece, piece)
        for subset in order:
            core_copy(subset, part).wait_recv()
            block = walk(member, subset, masks)
            total = part_ref[source_rows(block, part), :].astype(F32) + core_buffer[
                subset, where, :
            ].astype(F32)
            held[subset, where, :] = total.astype(BF16)
            if subset & 1:
                link_copy(0, subset, part).start()
    for step in range(steps):
        for part in range(PIECES):
            where = pl.ds(part * piece, piece)
            for kept in sorted(range(0, blocks, 2 << step), reverse=True):
                link_copy(step, kept | (1 << step), part).wait_recv()
                total = held[kept, where, :].astype(F32) + link_buffer[
                    slot(step, kept), where, :
                ].astype(F32)
                if kept == 0 and step == steps - 1:
                    sum_ref[where, :] = total
                else:
                    held[kept, where, :] = total.astype(BF16)
                if kept and (kept & (kept - 1)) != kept and (kept >> (step + 1)) & 1:
                    link_copy(step + 1, kept, part).start()
    for part in range(PIECES):
        for subset in range(blocks):
            core_copy(subset, part).wait_send()
        for step in range(steps):
            for kept in range(0, blocks, 2 << step):
                link_copy(step, kept | (1 << step), part).wait_send()


def plane_scatter(parts, member_count, collective_id):
    total, width = parts.shape
    rows = total // member_count
    steps = len(plane_masks(member_count))
    blocks = 1 << steps
    return pl.pallas_call(
        functools.partial(scatter_kernel, member_count),
        out_shape=jax.ShapeDtypeStruct((rows, width), F32),
        in_specs=[pl.BlockSpec(memory_space=pltpu.VMEM)],
        out_specs=pl.BlockSpec(memory_space=pltpu.VMEM),
        scratch_shapes=[
            pltpu.VMEM((blocks, rows, width), BF16),
            pltpu.VMEM((blocks - 1, rows, width), BF16),
            pltpu.VMEM((blocks, rows, width), BF16),
            pltpu.SemaphoreType.DMA((blocks - 1, PIECES)),
            pltpu.SemaphoreType.DMA((blocks - 1, PIECES)),
            pltpu.SemaphoreType.DMA((blocks, PIECES)),
            pltpu.SemaphoreType.DMA((blocks, PIECES)),
        ],
        compiler_params=pltpu.CompilerParams(
            collective_id=collective_id, has_side_effects=True, vmem_limit_bytes=VMEM_BYTES
        ),
        cost_estimate=pl.CostEstimate(
            flops=0, bytes_accessed=60 * total * width, transcendentals=0
        ),
        name="plane_scatter",
    )(parts)


def half_group(shape, heads):
    return (lax.broadcasted_iota(jnp.int32, shape, 1) // HALF) % heads


def full_group(shape):
    return lax.broadcasted_iota(jnp.int32, shape, 1) // HD


def forward_kernel(
    heads, first_ref, query_ref, key_ref, value_ref, start_ref, mixed_ref, lse_ref, top, total, acc
):
    step = pl.program_id(0)
    query = query_ref[...]
    start = start_ref[...]
    token = step * BLOCK + lax.broadcasted_iota(jnp.int32, (BLOCK, BLOCK), 1)
    within = lax.broadcasted_iota(jnp.int32, (BLOCK, BLOCK), 0)
    lane_head = half_group((BLOCK, query.shape[1]), heads)
    top[...] = jnp.full_like(top, MASKED)
    total[...] = jnp.zeros_like(total)
    acc[...] = jnp.zeros_like(acc)

    def one_block(block, carried):
        offset = pl.multiple_of(block * BLOCK, BLOCK)
        keys = key_ref[pl.ds(offset, BLOCK), :]
        values = value_ref[:, pl.ds(offset, BLOCK)]
        place = offset + within
        visible = (place >= start) & (place <= token)
        for head in range(heads):
            own_keys = jnp.where(lane_head == head, keys, jnp.zeros_like(keys))
            scores = jnp.where(visible, dot_nt(own_keys, query) * ATTENTION_SCALE, MASKED)
            old = top[head : head + 1, :]
            new = jnp.maximum(old, jnp.max(scores, axis=0, keepdims=True))
            weights = jnp.exp(scores - new)
            fade = jnp.exp(old - new)
            top[head : head + 1, :] = new
            total[head : head + 1, :] = total[head : head + 1, :] * fade + jnp.sum(
                weights, axis=0, keepdims=True
            )
            acc[head * HD : (head + 1) * HD, :] = acc[
                head * HD : (head + 1) * HD, :
            ] * fade + dot_nn(values, weights.astype(BF16))
        return carried

    lax.fori_loop(first_ref[step], step + 1, one_block, 0)
    for head in range(heads):
        acc[head * HD : (head + 1) * HD, :] = (
            acc[head * HD : (head + 1) * HD, :] / total[head : head + 1, :]
        )
    mixed_ref[...] = jnp.transpose(acc[...]).astype(BF16)
    lse_ref[...] = top[...] + jnp.log(total[...])


def attention_forward(first, query, keys, values, start):
    tokens, width = query.shape
    heads = width // HD
    return pl.pallas_call(
        functools.partial(forward_kernel, heads),
        grid_spec=pltpu.PrefetchScalarGridSpec(
            num_scalar_prefetch=1,
            grid=(tokens // BLOCK,),
            in_specs=[
                pl.BlockSpec((BLOCK, width), lambda i, first: (i, 0)),
                pl.BlockSpec((tokens, width), lambda i, first: (0, 0)),
                pl.BlockSpec((HD, tokens), lambda i, first: (0, 0)),
                pl.BlockSpec((1, BLOCK), lambda i, first: (0, i)),
            ],
            out_specs=[
                pl.BlockSpec((BLOCK, width), lambda i, first: (i, 0)),
                pl.BlockSpec((heads, BLOCK), lambda i, first: (0, i)),
            ],
            scratch_shapes=[
                pltpu.VMEM((heads, BLOCK), F32),
                pltpu.VMEM((heads, BLOCK), F32),
                pltpu.VMEM((width, BLOCK), F32),
            ],
        ),
        out_shape=[
            jax.ShapeDtypeStruct((tokens, width), BF16),
            jax.ShapeDtypeStruct((heads, tokens), F32),
        ],
        compiler_params=pltpu.CompilerParams(vmem_limit_bytes=VMEM_BYTES),
        cost_estimate=pl.CostEstimate(
            flops=8 * tokens * BLOCK * width * 8, bytes_accessed=8 * tokens * width, transcendentals=0
        ),
        name="attention_forward",
    )(first, query, keys, values, start)


def backward_kernel(
    heads,
    first_ref,
    query_ref,
    key_ref,
    value_ref,
    mixed_ref,
    grad_ref,
    lse_ref,
    start_ref,
    dquery_ref,
    dkey_ref,
    dvalue_ref,
):
    step = pl.program_id(0)
    query = query_ref[...]
    grad = grad_ref[...]
    start = start_ref[...]
    width = query.shape[1]
    token = step * BLOCK + lax.broadcasted_iota(jnp.int32, (BLOCK, BLOCK), 1)
    within = lax.broadcasted_iota(jnp.int32, (BLOCK, BLOCK), 0)
    half_head = half_group((BLOCK, width), heads)
    full_head = full_group((BLOCK, width))
    zero = jnp.zeros((BLOCK, width), BF16)
    product = grad.astype(F32) * mixed_ref[...].astype(F32)
    chooser = (
        lax.broadcasted_iota(jnp.int32, (8, width), 0)
        == lax.broadcasted_iota(jnp.int32, (8, width), 1) // HD
    ).astype(F32)
    correction = lax.dot_general(
        chooser,
        product,
        (((1,), (1,)), ((), ())),
        precision=lax.Precision.HIGHEST,
        preferred_element_type=F32,
    )

    @pl.when(step == 0)
    def _():
        dkey_ref[...] = jnp.zeros_like(dkey_ref)
        dvalue_ref[...] = jnp.zeros_like(dvalue_ref)

    dquery_ref[...] = jnp.zeros_like(dquery_ref)

    def one_block(block, carried):
        offset = pl.multiple_of(block * BLOCK, BLOCK)
        rows = pl.ds(offset, BLOCK)
        keys = key_ref[rows, :]
        values = value_ref[rows, :]
        place = offset + within
        visible = (place >= start) & (place <= token)
        dquery = dquery_ref[...]
        dkey = dkey_ref[rows, :]
        dvalue = dvalue_ref[rows, :]
        for head in range(heads):
            own_keys = jnp.where(half_head == head, keys, zero)
            own_values = jnp.where(full_head == head, values, zero)
            scores = dot_nt(own_keys, query) * ATTENTION_SCALE
            probs = jnp.where(visible, jnp.exp(scores - lse_ref[head : head + 1, :]), 0.0)
            pressure = dot_nt(own_values, grad)
            dscores = (probs * (pressure - correction[head : head + 1, :])).astype(BF16)
            dvalue = dvalue + dot_nn(probs.astype(BF16), jnp.where(full_head == head, grad, zero))
            dkey = dkey + dot_nn(dscores, jnp.where(half_head == head, query, zero))
            dquery = dquery + dot_tn(dscores, own_keys)
        dquery_ref[...] = dquery
        dkey_ref[rows, :] = dkey
        dvalue_ref[rows, :] = dvalue
        return carried

    lax.fori_loop(first_ref[step], step + 1, one_block, 0)


def attention_backward(first, query, keys, values, mixed, grad, lse, start):
    tokens, width = query.shape
    heads = width // HD
    by_block = pl.BlockSpec((BLOCK, width), lambda i, first: (i, 0))
    whole = pl.BlockSpec((tokens, width), lambda i, first: (0, 0))
    return pl.pallas_call(
        functools.partial(backward_kernel, heads),
        grid_spec=pltpu.PrefetchScalarGridSpec(
            num_scalar_prefetch=1,
            grid=(tokens // BLOCK,),
            in_specs=[
                by_block,
                whole,
                whole,
                by_block,
                by_block,
                pl.BlockSpec((heads, BLOCK), lambda i, first: (0, i)),
                pl.BlockSpec((1, BLOCK), lambda i, first: (0, i)),
            ],
            out_specs=[by_block, whole, whole],
        ),
        out_shape=[jax.ShapeDtypeStruct((tokens, width), F32)] * 3,
        compiler_params=pltpu.CompilerParams(vmem_limit_bytes=VMEM_BYTES),
        cost_estimate=pl.CostEstimate(
            flops=20 * tokens * BLOCK * width * 8,
            bytes_accessed=24 * tokens * width,
            transcendentals=0,
        ),
        name="attention_backward",
    )(first, query, keys, values, mixed, grad, lse, start)


def token_starts(lengths_row, group_tokens):
    count = lengths_row.shape[0]
    order = jnp.arange(count, dtype=jnp.int32)
    finish = jnp.sum(jnp.where(order[None, :] <= order[:, None], lengths_row[None, :], 0), axis=1)
    place = jnp.arange(group_tokens, dtype=jnp.int32)
    passed = place[:, None] >= finish[None, :]
    return jnp.max(jnp.where(passed, finish[None, :], 0), axis=1), place


def turn(values, cosine, sine):
    width = cosine.shape[1]
    first = values[:, :width]
    second = values[:, width:]
    return jnp.concatenate(
        [first * cosine - second * sine, second * cosine + first * sine], axis=1
    )


def inverse_norm(values):
    return lax.rsqrt(jnp.mean(values * values, axis=1, keepdims=True) + EPSILON)


def body(
    tokens,
    cotangent,
    query_weight,
    key_weight,
    value_weight,
    output_weight,
    gate_weight,
    up_weight,
    down_weight,
    attention_gain,
    feedforward_gain,
    lengths,
):
    members = lax.axis_size("fsdp")
    groups = lax.axis_size("dp")
    rows, model = tokens.shape
    group_tokens = rows * members
    shard = query_weight.shape[0]
    heads = NH // members
    width = heads * HD
    copies = members // KVH
    out_columns = model // members
    down_rows = down_weight.shape[0]
    chunk_rows = down_rows // CHUNKS
    gain_one = attention_gain.astype(F32)[:, None]
    gain_two = feedforward_gain.astype(F32)[:, None]

    scaled_query = (query_weight * gain_one).astype(BF16)
    scaled_key = (key_weight * gain_one).astype(BF16)
    scaled_value = (value_weight * gain_one).astype(BF16)
    packed = jnp.concatenate(
        [
            scaled_query.reshape(shard, members, heads, 2, HALF)
            .transpose(0, 1, 3, 2, 4)
            .reshape(shard, members, width),
            jnp.repeat(scaled_key.reshape(shard, KVH, HD), copies, axis=1),
            jnp.repeat(scaled_value.reshape(shard, KVH, HD), copies, axis=1),
            output_weight.reshape(shard, members, out_columns),
        ],
        axis=2,
    )
    packed = lax.all_to_all(packed, "fsdp", split_axis=1, concat_axis=0, tiled=True)
    packed = packed.reshape(members * shard, width + 2 * HD + out_columns)
    packed = lax.all_gather(packed, "dp", axis=0, tiled=True)

    gate_up = jnp.stack(
        [
            (weight * gain_two)
            .astype(BF16)
            .reshape(shard, groups, members, CHUNKS, chunk_rows)
            .transpose(0, 2, 3, 1, 4)
            for weight in (gate_weight, up_weight)
        ],
        axis=3,
    ).reshape(shard, members, CHUNKS * 2 * groups * chunk_rows)
    gate_up = lax.all_to_all(gate_up, "fsdp", split_axis=1, concat_axis=0, tiled=True)
    gate_up = gate_up.reshape(members * shard, CHUNKS, 2 * groups * chunk_rows)
    gate_up_chunks = []
    down_chunks = []
    for chunk in range(CHUNKS):
        gate_up_chunks.append(lax.all_gather(gate_up[:, chunk], "dp", axis=0, tiled=True))
        down_chunks.append(
            lax.all_gather(
                down_weight[chunk * chunk_rows : (chunk + 1) * chunk_rows], "dp", axis=0, tiled=True
            )
        )

    start, place = token_starts(lengths[0], group_tokens)
    first = start[::BLOCK] // BLOCK
    frequency = ROPE_BASE ** (-(2.0 * jnp.arange(HALF, dtype=F32)) / HD)
    angles = (place - start).astype(F32)[:, None] * frequency[None, :]
    cosine = jnp.tile(jnp.cos(angles), (1, heads))
    sine = jnp.tile(jnp.sin(angles), (1, heads))
    start = start[None, :]

    inputs = tokens.astype(F32)
    inverse_one = inverse_norm(inputs)
    normed_one = plane_gather((inputs * inverse_one).astype(BF16), members, 0)
    upstream = cotangent.astype(F32)
    grad_two = plane_gather((RESIDUAL_SCALE * upstream).astype(BF16), members, 1)

    key_part = packed[:, width : width + HD]
    value_part = packed[:, width + HD : width + 2 * HD]
    projection = jnp.concatenate(
        [
            packed[:, :width],
            jnp.tile(key_part[:, :HALF], (1, heads)),
            jnp.tile(key_part[:, HALF:], (1, heads)),
            jnp.tile(value_part, (1, heads)),
        ],
        axis=1,
    )
    out_piece = lax.all_to_all(
        packed[:, width + 2 * HD :], "fsdp", split_axis=0, concat_axis=1, tiled=True
    )
    projected = dot_nn(normed_one, projection)
    query = turn(projected[:, :width], cosine, sine).astype(BF16)
    keys = turn(projected[:, width : 2 * width], cosine, sine).astype(BF16)
    values = projected[:, 2 * width :].astype(BF16)
    mixed, lse = attention_forward(first, query, keys, values[:, :HD].T, start)
    branch_one = plane_scatter(dot_nn(mixed, out_piece).astype(BF16), members, 2)
    residual = inputs + RESIDUAL_SCALE * branch_one

    inverse_two = inverse_norm(residual)
    normed_two = plane_gather((residual * inverse_two).astype(BF16), members, 3)
    down_sum = 0.0
    grad_normed = 0.0
    down_grads = []
    gate_up_grads = []
    for chunk in range(CHUNKS):
        both_weight = gate_up_chunks[chunk]
        down_piece = down_chunks[chunk]
        units = down_piece.shape[0]
        both = dot_nn(normed_two, both_weight)
        gate = both[:, :units]
        up = both[:, units:]
        sigmoid = jax.nn.sigmoid(gate)
        hidden = (gate * sigmoid * up).astype(BF16)
        down_sum = down_sum + dot_nn(hidden, down_piece)
        grad_hidden = dot_nt(grad_two, down_piece)
        grad_both = jnp.concatenate(
            [
                (grad_hidden * up * sigmoid * (1.0 + gate * (1.0 - sigmoid))).astype(BF16),
                (grad_hidden * gate * sigmoid).astype(BF16),
            ],
            axis=1,
        )
        grad_normed = grad_normed + dot_nt(grad_both, both_weight)
        down_grads.append(
            lax.psum_scatter(
                dot_tn(hidden, grad_two).astype(BF16), "dp", scatter_dimension=0, tiled=True
            )
        )
        gate_up_grads.append(
            lax.psum_scatter(
                dot_tn(normed_two, grad_both).astype(BF16), "dp", scatter_dimension=0, tiled=True
            )
        )
    weighted_two = plane_scatter(grad_normed.astype(BF16), members, 4)
    grad_residual = (
        upstream
        + inverse_two * weighted_two
        - residual * inverse_two**3 * jnp.mean(weighted_two * residual, axis=1, keepdims=True)
    )
    gain_term_two = jnp.sum(weighted_two * residual * inverse_two, axis=0)

    grad_one = plane_gather((RESIDUAL_SCALE * grad_residual).astype(BF16), members, 5)
    grad_mixed = dot_nt(grad_one, out_piece).astype(BF16)
    out_grad = dot_tn(mixed, grad_one).astype(BF16)
    out_grad = lax.all_to_all(out_grad, "fsdp", split_axis=1, concat_axis=0, tiled=True)
    dquery, dkeys, dvalues = attention_backward(
        first, query, keys, values, mixed, grad_mixed, lse, start
    )
    grad_projected = jnp.concatenate(
        [
            (turn(dquery, cosine, -sine) * ATTENTION_SCALE).astype(BF16),
            (turn(dkeys, cosine, -sine) * ATTENTION_SCALE).astype(BF16),
            dvalues.astype(BF16),
        ],
        axis=1,
    )
    projection_grad = dot_tn(normed_one, grad_projected)
    key_grad = projection_grad[:, width : 2 * width].reshape(model, 2, heads, HALF).sum(axis=2)
    value_grad = projection_grad[:, 2 * width :].reshape(model, heads, HD).sum(axis=1)
    packed_grad = jnp.concatenate(
        [
            projection_grad[:, :width].astype(BF16),
            key_grad.reshape(model, HD).astype(BF16),
            value_grad.astype(BF16),
            out_grad,
        ],
        axis=1,
    )
    packed_grad = lax.psum_scatter(packed_grad, "dp", scatter_dimension=0, tiled=True)
    weighted_one = plane_scatter(dot_nt(grad_projected, projection).astype(BF16), members, 6)
    grad_inputs = (
        grad_residual
        + inverse_one * weighted_one
        - inputs * inverse_one**3 * jnp.mean(weighted_one * inputs, axis=1, keepdims=True)
    )
    gain_term_one = jnp.sum(weighted_one * inputs * inverse_one, axis=0)

    down_sum, _ = lax.optimization_barrier((down_sum.astype(BF16), weighted_one))
    branch_two = plane_scatter(down_sum, members, 7)
    output = residual + RESIDUAL_SCALE * branch_two

    both_grad = jnp.stack(gate_up_grads, axis=1).reshape(members, shard, -1)
    both_grad = lax.all_to_all(both_grad, "fsdp", split_axis=0, concat_axis=0, tiled=True)
    both_grad = (
        both_grad.reshape(members, shard, CHUNKS, 2, groups, chunk_rows)
        .transpose(3, 1, 4, 0, 2, 5)
        .reshape(2, shard, -1)
        .astype(F32)
    )
    packed_grad = lax.all_to_all(
        packed_grad.reshape(members, shard, -1), "fsdp", split_axis=0, concat_axis=0, tiled=True
    ).astype(F32)
    grad_query = (
        packed_grad[:, :, :width]
        .reshape(members, shard, 2, heads, HALF)
        .transpose(1, 0, 3, 2, 4)
        .reshape(shard, -1)
    )

    def folded(part):
        return (
            part.reshape(KVH, copies, shard, HD).sum(axis=1).transpose(1, 0, 2).reshape(shard, -1)
        )

    gains = jnp.stack([gain_term_one, gain_term_two], axis=1).reshape(-1, 2 * shard)
    gains = lax.psum_scatter(gains, ("dp", "fsdp"), scatter_dimension=0, tiled=True)
    gains = gains.reshape(shard, 2)
    return (
        output.astype(BF16),
        grad_inputs.astype(BF16),
        grad_query * gain_one,
        folded(packed_grad[:, :, width : width + HD]) * gain_one,
        folded(packed_grad[:, :, width + HD : width + 2 * HD]) * gain_one,
        packed_grad[:, :, width + 2 * HD :].transpose(1, 0, 2).reshape(shard, -1),
        both_grad[0] * gain_two,
        both_grad[1] * gain_two,
        jnp.concatenate(down_grads, axis=0).astype(F32),
        gains[:, 0] / gain_one[:, 0],
        gains[:, 1] / gain_two[:, 0],
    )


def solution(mesh):
    by_rows = P(("dp", "fsdp"), None)
    by_entries = P(("dp", "fsdp"))
    return jax.shard_map(
        body,
        mesh=mesh,
        in_specs=(by_rows,) * 9 + (by_entries,) * 2 + (P("dp", None),),
        out_specs=(by_rows,) * 9 + (by_entries,) * 2,
        check_vma=False,
    )
```

time: 3400 us -> 948 us (0.28)
  waiting for transfers between devices: 2470 us -> 73.8 us
  Pallas kernels: 0 us -> 406 us
  matrix products: 450 us -> 206 us
  local copies, waits for them, and re-layouts: 299 us -> 91.6 us
    reduce_scatter x2 -> x5, waiting for transfers between devices: 1820 us -> 60.7 us  [the longest x2 60.7 us: body(): lax.psum_scatter(dot_tn(hidden, grad_two).astype(BF16), 'dp', scatter_dim...]
    all_gather x8 -> x5, waiting for transfers between devices: 645 us -> 0.07 us  [the longest x2 0.02 us: body(): lax.all_gather(gate_up[:, chunk], 'dp', axis=0, tiled=True)]
    pallas_call x0 -> x10, Pallas kernels: none -> 406 us  [the longest x4 178 us: plane_scatter(): pl.pallas_call(functools.partial(scatter_kernel, member_count), out_shape...]
    dot_general x77 -> x18, matrix products: 450 us -> 206 us  [the longest x6 75.7 us: dot_nt(): lax.dot_general(left, right, (((1,), (1,)), ((), ())), preferred_element_...]
    reshape x3 -> x10, local copies, waits for them, and re-layouts: 83.9 us -> 10.4 us  [the longest x1 3.3 us: body(): gate_up = gate_up.reshape(members * shard, CHUNKS, 2 * groups * chunk_rows)]
    unnamed x88 -> x99, local copies, waits for them, and re-layouts: 53.9 us -> 11.9 us
  transfers between devices with their start and end apart: 12 -> 15, of which waited for: 7 -> 4; matrix products, arithmetic and copies ran while one was open for 14% -> 27% of each run, Pallas kernels for 0% -> 34%
where the time goes in v1:
time: 948 us; the launch traced here: 938 us
  Pallas kernels  406 us (43%)
  matrix products  206 us (22%)
  local copies, waits for them, and re-layouts  91.6 us (10%)
  waiting for transfers between devices  73.8 us (8%)
  blocking collectives  70.9 us (7%)
  other arithmetic  52.8 us (6%)
  starting transfers between devices  21.9 us (2%)
  between operations  15.6 us (2%)
    pallas_call x4, Pallas kernels, plane_scatter(): pl.pallas_call(functools.partial(scatter_kernel, member_count), out_shape...  178 us
    pallas_call x4, Pallas kernels, plane_gather(): pl.pallas_call(functools.partial(gather_kernel, member_count), out_shape=...  155 us
    dot_general x6, matrix products, dot_nt(): lax.dot_general(left, right, (((1,), (1,)), ((), ())), preferred_element_...  75.7 us
    dot_general x6, matrix products, dot_nn(): return jnp.dot(left, right, preferred_element_type=F32)  70.5 us
    reduce_scatter x2, waiting for transfers between devices, body(): lax.psum_scatter(dot_tn(hidden, grad_two).astype(BF16), 'dp', scatter_dim...  60.7 us
    dot_general x6, matrix products, dot_tn(): lax.dot_general(left, right, (((0,), (0,)), ((), ())), preferred_element_...  59.5 us
    pallas_call x1, Pallas kernels, attention_backward(): pl.pallas_call(functools.partial(backward_kernel, heads), grid_spec=pltpu...  42.1 us
    unnamed x1, blocking collectives  41.1 us
  transfers between devices with their start and end apart: 15, of which 4 were waited for; matrix products, arithmetic and copies ran while one was open for 27% of the time, Pallas kernels for 34%

profile of v1, /device:TPU:0, one launch (start us, length us, event | category | flops | bytes accessed | tf_op | source)
XLA Modules:
  0.0 937.9 jit_solution(13264998588993660978)
XLA Ops:
  17.6 11.1 %all-to-all-done = bf16[64,8,640]{2,0,1:T(8,128)(2,1)S(1)} async-done(((bf16[64,8,640]{2,0,1:T(8,128)(2,1)}), bf16[64,8,640]{2,0,1:T(8,128)(2,1)S(1)}, u32[]{:S(2)}, u32[]{:S(2)}) %all-to-all-start) | async-done | bytes 655392 | tf_op jit(solution)/shard_map/all_to_all | solution.py:538
  37.6 29.8 %all_to_all.78 = bf16[64,8,2048]{2,0,1:T(8,128)(2,1)} all-to-all(bf16[64,8,2048]{2,0,1:T(8,128)(2,1)S(1)} %copy.196), channel_id=1, replica_groups=mesh['dp'=4,'fsdp'=8] {'fsdp'}, dimensions={1} | all-to-all | bytes 4194304 | tf_op jit(solution)/shard_map/all_to_all | solution.py:552
  88.7 38.0 %plane_gather.6 = bf16[2048,2048]{1,0:T(8,128)(2,1)} custom-call(bf16[256,2048]{1,0:T(8,128)(2,1)} %fusion.7.own_ref), custom_call_target="tpu_custom_call" | custom-call | bytes 251658240 | tf_op jit(solution)/shard_map/plane_gather/pallas_call | solution.py:145
  126.6 39.1 %plane_gather.4 = bf16[2048,2048]{1,0:T(8,128)(2,1)} custom-call(bf16[256,2048]{1,0:T(8,128)(2,1)} %fusion.10.own_ref), custom_call_target="tpu_custom_call" | custom-call | bytes 251658240 | tf_op jit(solution)/shard_map/plane_gather/pallas_call | solution.py:145
  207.9 31.1 %attention_forward.1 = (bf16[2048,256]{1,0:T(8,128)(2,1)}, f32[4,2048]{1,0:T(4,128)}) custom-call(s32[8]{0:T(128)} %and_select_fusion.first_ref, bf16[2048,256]{1,0:T(8,128)(2,1)} %get-tuple-element.123.query_ref, bf16[2048,256]{1,0:T(8,128)(2,1)} %get-tuple-element.124.key_ref, bf16[64,2048]{1,0:T(8,128)(2,1)} %copy.193.value_ref, s32[1,2048]{1,0:T(1,128)} %bitcast.126), custom_call_target="tpu_custom_call" | custom-call | flops 8589934592 | bytes 4194304 | tf_op jit(solution)/shard_map/attention_forward/pallas_call | solution.py:337
  246.2 44.8 %plane_scatter.4 = f32[256,2048]{1,0:T(8,128)} custom-call(bf16[2048,2048]{1,0:T(8,128)(2,1)} %convolution_convert_fusion.1.part_ref), custom_call_target="tpu_custom_call" | custom-call | bytes 251658240 | tf_op jit(solution)/shard_map/plane_scatter/pallas_call | solution.py:258
  294.4 38.9 %plane_gather.5 = bf16[2048,2048]{1,0:T(8,128)(2,1)} custom-call(bf16[256,2048]{1,0:T(8,128)(2,1)} %multiply_convert_fusion.9.own_ref), custom_call_target="tpu_custom_call" | custom-call | bytes 251658240 | tf_op jit(solution)/shard_map/plane_gather/pallas_call | solution.py:145
  333.4 14.9 %fusion.1 = f32[2048,1024]{0,1:T(8,128)} fusion(bf16[2048,2048]{1,0:T(8,128)(2,1)} %plane_gather.5, bf16[2048,1,1024]{2,0,1:T(8,128)(2,1)} %all-gather.16.cloned.1.call-done), kind=kOutput, calls=%fused_computation.7 | convolution fusion | flops 8589934592 | bytes 20971520 | tf_op jit(solution)/shard_map/dot_general | solution.py:30
  348.4 15.0 %fusion.5 = f32[2048,1024]{0,1:T(8,128)} fusion(bf16[2048,2048]{1,0:T(8,128)(2,1)} %plane_gather.5, bf16[2048,1,1024]{2,0,1:T(8,128)(2,1)} %all-gather.14.cloned.1.call-done), kind=kOutput, calls=%fused_computation.11 | convolution fusion | flops 8589934592 | bytes 20971520 | tf_op jit(solution)/shard_map/dot_general | solution.py:30
  363.4 15.0 %multiply_convert_fusion.1 = (bf16[2048,512]{0,1:T(8,128)(2,1)}, bf16[2048,512]{0,1:T(8,128)(2,1)}, bf16[2048,512]{0,1:T(8,128)(2,1)}) fusion(f32[2048,1024]{0,1:T(8,128)} %fusion.1, bf16[2048,2048]{1,0:T(8,128)(2,1)} %plane_gather.6, bf16[512,2048]{1,0:T(8,128)(2,1)} %all-gather.12.cloned.1.call-done), kind=kOutput, calls=%fused_computation.14 | convolution fusion | flops 4311744512 | bytes 25165824 | tf_op jit(solution)/shard_map/dot_general | solution.py:34
  378.4 13.8 %multiply_convert_fusion.3 = (bf16[2048,512]{0,1:T(8,128)(2,1)S(1)}, bf16[2048,512]{0,1:T(8,128)(2,1)S(1)}, bf16[2048,512]{0,1:T(8,128)(2,1)}) fusion(f32[2048,1024]{0,1:T(8,128)} %fusion.5, bf16[2048,2048]{1,0:T(8,128)(2,1)} %plane_gather.6, bf16[512,2048]{1,0:T(8,128)(2,1)} %all-gather.10.cloned.1.call-done), kind=kOutput, calls=%fused_computation.16 | convolution fusion | flops 4311744512 | bytes 25165824 | tf_op jit(solution)/shard_map/dot_general | solution.py:34
  392.2 12.2 %fusion.3 = f32[2048,2048]{1,0:T(8,128)} fusion(bf16[2048,1,1024]{2,0,1:T(8,128)(2,1)S(1)} %copy-done.36, bf16[2048,512]{0,1:T(8,128)(2,1)S(1)} %get-tuple-element.80, bf16[2048,512]{0,1:T(8,128)(2,1)S(1)} %get-tuple-element.79), kind=kOutput, calls=%fused_computation.9 | convolution fusion | flops 8598323200 | bytes 25165824 | tf_op jit(solution)/shard_map/dot_general | solution.py:34
  404.4 16.7 %add_convert_fusion.part_ref = bf16[2048,2048]{1,0:T(8,128)(2,1)} fusion(f32[2048,2048]{1,0:T(8,128)} %fusion.3, bf16[2048,1,1024]{2,0,1:T(8,128)(2,1)} %all-gather.16.cloned.1.call-done, bf16[2048,512]{0,1:T(8,128)(2,1)} %get-tuple-element.78, bf16[2048,512]{0,1:T(8,128)(2,1)} %get-tuple-element.77), kind=kOutput, calls=%fused_computation | convolution fusion | flops 8606711808 | bytes 33554432 | tf_op jit(solution)/shard_map/dot_general | solution.py:34
  421.1 43.5 %plane_scatter.5 = f32[256,2048]{1,0:T(8,128)} custom-call(bf16[2048,2048]{1,0:T(8,128)(2,1)} %add_convert_fusion.part_ref), custom_call_target="tpu_custom_call" | custom-call | bytes 251658240 | tf_op jit(solution)/shard_map/plane_scatter/pallas_call | solution.py:258
  469.4 38.8 %plane_gather.7 = bf16[2048,2048]{1,0:T(8,128)(2,1)} custom-call(bf16[256,2048]{1,0:T(8,128)(2,1)} %get-tuple-element.73.own_ref), custom_call_target="tpu_custom_call" | custom-call | bytes 251658240 | tf_op jit(solution)/shard_map/plane_gather/pallas_call | solution.py:145
  523.3 42.1 %attention_backward.1 = (f32[2048,256]{1,0:T(8,128)}, f32[2048,256]{1,0:T(8,128)}, f32[2048,256]{1,0:T(8,128)}) custom-call(s32[8]{0:T(128)} %and_select_fusion.first_ref, bf16[2048,256]{1,0:T(8,128)(2,1)} %get-tuple-element.123.query_ref, bf16[2048,256]{1,0:T(8,128)(2,1)} %get-tuple-element.124.key_ref, bf16[2048,256]{1,0:T(8,128)(2,1)} %slice.170.value_ref, ...), custom_call_target="tpu_custom_call" | custom-call | flops 21474836480 | bytes 12582912 | tf_op jit(solution)/shard_map/attention_backward/pallas_call | solution.py:447
  593.1 14.0 %convolution_convert_fusion.2 = bf16[2048,1024]{1,0:T(8,128)(2,1)} fusion(bf16[2048,2048]{1,0:T(8,128)(2,1)} %plane_gather.5, bf16[2048,512]{0,1:T(8,128)(2,1)} %get-tuple-element.78, bf16[2048,512]{0,1:T(8,128)(2,1)S(1)} %copy-done.43), kind=kOutput, calls=%fused_computation.26 | convolution fusion | flops 8600420352 | bytes 16777216 | tf_op jit(solution)/shard_map/dot_general | solution.py:38
  608.7 13.3 %convolution_convert_fusion.3 = bf16[2048,1024]{1,0:T(8,128)(2,1)} fusion(bf16[2048,2048]{1,0:T(8,128)(2,1)} %plane_gather.5, bf16[2048,512]{0,1:T(8,128)(2,1)} %copy-done.46, bf16[2048,512]{0,1:T(8,128)(2,1)S(1)} %copy-done.45), kind=kOutput, calls=%fused_computation.27 | convolution fusion | flops 8600420352 | bytes 16777216 | tf_op jit(solution)/shard_map/dot_general | solution.py:38
  643.3 44.9 %plane_scatter.6 = f32[256,2048]{1,0:T(8,128)} custom-call(bf16[2048,2048]{1,0:T(8,128)(2,1)} %convolution_convert_fusion.part_ref), custom_call_target="tpu_custom_call" | custom-call | bytes 251658240 | tf_op jit(solution)/shard_map/plane_scatter/pallas_call | solution.py:258
  691.0 41.1 %all-reduce = f32[32,128]{1,0:T(8,128)S(1)} all-reduce(f32[32,128]{1,0:T(8,128)S(1)} %reshape.245), channel_id=9, replica_groups=mesh['dp'=4,'fsdp'=8] {'dp','fsdp'}, use_global_device_ids=true, to_apply=%region_15.16.clone | all-reduce | flops 4096 | bytes 32768
  742.2 12.7 %fusion.34 = f32[2048,2048]{1,0:T(8,128)} fusion(bf16[2048,512]{0,1:T(8,128)(2,1)} %get-tuple-element.82, bf16[512,2048]{1,0:T(8,128)(2,1)} %all-gather.10.cloned.1.call-done), kind=kOutput, calls=%fused_computation.125 | convolution fusion | flops 4294967296 | bytes 20971520 | tf_op jit(solution)/shard_map/dot_general | solution.py:30
  765.6 44.6 %plane_scatter.7 = f32[256,2048]{1,0:T(8,128)} custom-call(bf16[2048,2048]{1,0:T(8,128)(2,1)} %add_convert_fusion.1.part_ref), custom_call_target="tpu_custom_call" | custom-call | bytes 251658240 | tf_op jit(solution)/shard_map/plane_scatter/pallas_call | solution.py:258
  833.8 15.2 %reduce-scatter.14.cloned.1.call-done = bf16[128,2048]{1,0:T(8,128)(2,1)} async-done(((bf16[512,2048]{1,0:T(8,128)(2,1)}), bf16[128,2048]{1,0:T(8,128)(2,1)}) %reduce-scatter.14.cloned.1.call-update) | async-done | bytes 524304 | tf_op jit(solution)/shard_map/reduce_scatter | solution.py:626
  849.1 45.4 %reduce-scatter.12.cloned.1.call-done = bf16[128,2048]{1,0:T(8,128)(2,1)} async-done(((bf16[512,2048]{1,0:T(8,128)(2,1)}), bf16[128,2048]{1,0:T(8,128)(2,1)}) %reduce-scatter.12.cloned.1.call-update) | async-done | bytes 524304 | tf_op jit(solution)/shard_map/reduce_scatter | solution.py:626
  (250 shorter events, 246.2 us)
Async XLA Ops:
  11.1 18.5 %copy-start.19 = (bf16[64,8192]{1,0:T(8,128)(2,1)S(1)}, bf16[64,8192]{1,0:T(8,128)(2,1)}, u32[]{:S(2)}) copy-start(bf16[64,8192]{1,0:T(8,128)(2,1)} %param.18) | copy-start | bytes 3145732
  12.4 16.3 %all-to-all-start = ((bf16[64,8,640]{2,0,1:T(8,128)(2,1)}), bf16[64,8,640]{2,0,1:T(8,128)(2,1)S(1)}, u32[]{:S(2)}, u32[]{:S(2)}) async-start(bf16[64,8,640]{2,0,1:T(8,128)(2,1)} %copy.173), calls=%async_computation | async-start | bytes 1310720 | tf_op jit(solution)/shard_map/all_to_all | solution.py:538
  17.6 148.2 %all-gather.8.cloned.1.call-start = ((), (), s32[]{:S(2)}) async-start(), calls=%async_computation.11 | async-start | bytes 3276800 | tf_op jit(solution)/shard_map/all_gather | solution.py:540
  29.6 303.8 %all-gather.16.cloned.1.call-start = ((), (), s32[]{:S(2)}) async-start(), calls=%async_computation.20 | async-start | bytes 5242880 | tf_op jit(solution)/shard_map/all_gather | solution.py:557
  75.9 272.5 %all-gather.14.cloned.1.call-start = ((), (), s32[]{:S(2)}) async-start(), calls=%async_computation.19 | async-start | bytes 5242880 | tf_op jit(solution)/shard_map/all_gather | solution.py:557
  77.8 285.5 %all-gather.12.cloned.1.call-start = ((), (), s32[]{:S(2)}) async-start(), calls=%async_computation.13 | async-start | bytes 2621440 | tf_op jit(solution)/shard_map/all_gather | solution.py:559
  78.9 299.5 %all-gather.10.cloned.1.call-start = ((), (), s32[]{:S(2)}) async-start(), calls=%async_computation.12 | async-start | bytes 2621440 | tf_op jit(solution)/shard_map/all_gather | solution.py:559
  82.7 121.0 %copy-start.7 = (f32[2048,128]{1,0:T(8,128)}, f32[2048,128]{1,0:T(8,128)S(1)}, u32[]{:S(2)}) copy-start(f32[2048,128]{1,0:T(8,128)S(1)} %copy.181) | copy-start | bytes 3145732
  85.4 118.3 %copy-start.9 = (f32[2048,128]{1,0:T(8,128)}, f32[2048,128]{1,0:T(8,128)S(1)}, u32[]{:S(2)}) copy-start(f32[2048,128]{1,0:T(8,128)S(1)} %copy.183) | copy-start | bytes 3145732
  181.6 57.3 %all-to-all-start.1 = ((bf16[8,256,256]{1,2,0:T(8,128)(2,1)}), bf16[8,256,256]{1,2,0:T(8,128)(2,1)}, u32[]{:S(2)}, u32[]{:S(2)}) async-start(bf16[8,256,256]{1,2,0:T(8,128)(2,1)} %copy.194), calls=%async_computation.1 | async-start | bytes 2097152 | tf_op jit(solution)/shard_map/all_to_all | solution.py:589
  293.1 173.7 %copy-start.1 = (f32[256,2048]{1,0:T(8,128)}, f32[256,2048]{1,0:T(8,128)S(1)}, u32[]{:S(2)}) copy-start(f32[256,2048]{1,0:T(8,128)S(1)} %get-tuple-element.76) | copy-start | bytes 6291460
  519.0 66.3 %all-to-all-start.3 = ((bf16[256,8,256]{0,2,1:T(8,128)(2,1)}), bf16[256,8,256]{0,2,1:T(8,128)(2,1)}, u32[]{:S(2)}, u32[]{:S(2)}) async-start(bf16[256,8,256]{0,2,1:T(8,128)(2,1)} %bitcast.33), calls=%async_computation.3 | async-start | bytes 2097152 | tf_op jit(solution)/shard_map/all_to_all | solution.py:646
  523.2 288.7 %reduce-scatter.6.cloned.1.call-start = ((), (), s32[]{:S(2)}) async-start(), calls=%async_computation.14 | async-start | bytes 3276800 | tf_op jit(solution)/shard_map/reduce_scatter | solution.py:670
  591.5 229.2 %reduce-scatter.10.cloned.1.call-start = ((), (), s32[]{:S(2)}) async-start(), calls=%async_computation.16 | async-start | bytes 5242880 | tf_op jit(solution)/shard_map/reduce_scatter | solution.py:631
  607.1 213.6 %reduce-scatter.8.cloned.1.call-start = ((), (), s32[]{:S(2)}) async-start(), calls=%async_computation.15 | async-start | bytes 5242880 | tf_op jit(solution)/shard_map/reduce_scatter | solution.py:631
  622.0 227.0 %reduce-scatter.14.cloned.1.call-start = ((), (), s32[]{:S(2)}) async-start(), calls=%async_computation.18 | async-start | bytes 2621440 | tf_op jit(solution)/shard_map/reduce_scatter | solution.py:626
  632.4 262.1 %reduce-scatter.12.cloned.1.call-start = ((), (), s32[]{:S(2)}) async-start(), calls=%async_computation.17 | async-start | bytes 2621440 | tf_op jit(solution)/shard_map/reduce_scatter | solution.py:626
  643.3 44.9 %copy-start.4 = (bf16[256,2048]{1,0:T(8,128)(2,1)S(1)}, bf16[256,2048]{1,0:T(8,128)(2,1)}, u32[]{:S(2)}) copy-start(bf16[256,2048]{1,0:T(8,128)(2,1)} %param.12) | copy-start | bytes 3145732
  643.3 44.9 %copy-start.30 = (f32[256]{0:T(256)S(1)}, f32[256]{0:T(256)}, u32[]{:S(2)}) copy-start(f32[256]{0:T(256)} %copy-done.29) | copy-start | bytes 3076
  765.6 44.8 %copy-start.5 = (f32[256,2048]{1,0:T(8,128)S(1)}, f32[256,2048]{1,0:T(8,128)}, u32[]{:S(2)}) copy-start(f32[256,2048]{1,0:T(8,128)} %plane_scatter.6) | copy-start | bytes 6291460
  765.6 44.8 %copy-start.12 = (f32[256,2048]{1,0:T(8,128)S(1)}, f32[256,2048]{1,0:T(8,128)}, u32[]{:S(2)}) copy-start(f32[256,2048]{1,0:T(8,128)} %get-tuple-element.74) | copy-start | bytes 6291460
  765.6 44.8 %copy-start.33 = (f32[256]{0:T(256)S(1)}, f32[256]{0:T(256)}, u32[]{:S(2)}) copy-start(f32[256]{0:T(256)} %get-tuple-element.109) | copy-start | bytes 3076
  814.3 14.6 %all-to-all-start.4 = ((bf16[8,64,640]{2,1,0:T(8,128)(2,1)}), bf16[8,64,640]{2,1,0:T(8,128)(2,1)S(1)}, u32[]{:S(2)}, u32[]{:S(2)}) async-start(bf16[8,64,640]{2,1,0:T(8,128)(2,1)} %bitcast.35), calls=%async_computation.5 | async-start | bytes 1310720 | tf_op jit(solution)/shard_map/all_to_all | solution.py:691
  828.9 79.0 %all-to-all-start.5 = ((bf16[8,64,2048]{2,1,0:T(8,128)(2,1)}), bf16[8,64,2048]{2,1,0:T(8,128)(2,1)S(1)}, u32[]{:S(2)}, u32[]{:S(2)}) async-start(bf16[8,64,2048]{2,1,0:T(8,128)(2,1)} %reshape.244), calls=%async_computation.8 | async-start | bytes 4194304 | tf_op jit(solution)/shard_map/all_to_all | solution.py:684
  (38 other events, 217.2 us)
Sparse Core Ops, SparseCore 0:
  29.7 54.1 all-gather.7
  85.5 79.5 all-gather.15
  167.2 79.2 all-gather.13
  247.9 44.4 all-gather.11
  293.9 44.6 all-gather.9
  591.6 50.6 reduce-scatter.5
  644.6 77.3 reduce-scatter.9
  724.4 77.3 reduce-scatter.7
  804.7 44.3 reduce-scatter.13
  851.3 43.1 reduce-scatter.11

commit v2 on v1

v2 whole, which is shorter than its diff:
```python
import functools

import jax
import jax.numpy as jnp
from jax import lax
from jax.experimental import pallas as pl
from jax.experimental.pallas import tpu as pltpu
from jax.sharding import PartitionSpec as P

NH = 32
KVH = 8
HD = 64
HALF = HD // 2

EPSILON = 1e-05
RESIDUAL_SCALE = 0.22
ATTENTION_SCALE = 0.015625
ROPE_BASE = 10000000.0
MASKED = -1e30
BLOCK = 256
CHUNKS = 2
PIECES = 4
VMEM_BYTES = 58 * 1024 * 1024
MESH = pl.DeviceIdType.MESH
BF16 = jnp.bfloat16
F32 = jnp.float32


def dot_nn(left, right):
    return jnp.dot(left, right, preferred_element_type=F32)


def dot_nt(left, right):
    return lax.dot_general(left, right, (((1,), (1,)), ((), ())), preferred_element_type=F32)


def dot_tn(left, right):
    return lax.dot_general(left, right, (((0,), (0,)), ((), ())), preferred_element_type=F32)


def flip(index, mask):
    return index + mask * (1 - 2 * ((index // mask) % 2))


def plane_masks(member_count):
    masks = []
    mask = 2
    while mask < member_count:
        masks.append(mask)
        mask *= 2
    return masks


def hop(index, step, masks):
    core = index % 2
    return (1 - core) * flip(index, masks[step]) + core * flip(index, masks[-1 - step])


def walk(index, subset, masks):
    for step in range(len(masks)):
        if (subset >> step) & 1:
            index = hop(index, step, masks)
    return index


def greet(group, member, masks):
    barrier = pltpu.get_barrier_semaphore()
    partners = [hop(member, step, masks) for step in range(len(masks))] + [flip(member, 1)]
    for partner in partners:
        pl.semaphore_signal(barrier, inc=1, device_id=(group, partner), device_id_type=MESH)
    pl.semaphore_wait(barrier, len(partners))


def gather_kernel(
    member_count, in_order, own_ref, all_ref, link_send, link_recv, core_send, core_recv, local_sem
):
    group = lax.axis_index("dp")
    member = lax.axis_index("fsdp")
    masks = plane_masks(member_count)
    steps = len(masks)
    rows = own_ref.shape[0]
    piece = rows // PIECES
    greet(group, member, masks)

    blocks = 1 << steps

    def place(owner, subset, side, part):
        block = walk(owner, subset, masks) if in_order else subset + side * blocks
        return all_ref.at[pl.ds(pl.multiple_of(block * rows + part * piece, piece), piece)]

    def link_copy(step, subset, part):
        number = (1 << step) - 1 + subset
        here = place(member, subset, 0, part)
        there = here if in_order else place(member, subset | (1 << step), 0, part)
        return pltpu.make_async_remote_copy(
            own_ref.at[pl.ds(part * piece, piece)] if subset == 0 else here,
            there,
            link_send.at[number, part],
            link_recv.at[number, part],
            device_id=(group, hop(member, step, masks)),
            device_id_type=MESH,
        )

    def core_copy(subset, part):
        here = place(member, subset, 0, part)
        there = here if in_order else place(member, subset, 1, part)
        return pltpu.make_async_remote_copy(
            own_ref.at[pl.ds(part * piece, piece)] if subset == 0 else here,
            there,
            core_send.at[subset, part],
            core_recv.at[subset, part],
            device_id=(group, flip(member, 1)),
            device_id_type=MESH,
        )

    for part in range(PIECES):
        for step in range(steps):
            link_copy(step, 0, part).start()
    first = pl.multiple_of(member * rows, rows) if in_order else 0
    keep = pltpu.make_async_copy(own_ref, all_ref.at[pl.ds(first, rows)], local_sem)
    keep.start()
    for part in range(PIECES):
        core_copy(0, part).start()
    for step in range(steps):
        for part in range(PIECES):
            for subset in range(1 << step):
                link_copy(step, subset, part).wait_recv()
                arrived = subset | (1 << step)
                for later in range(step + 1, steps):
                    link_copy(later, arrived, part).start()
                core_copy(arrived, part).start()
    for part in range(PIECES):
        for subset in range(1 << steps):
            core_copy(subset, part).wait()
    for part in range(PIECES):
        for step in range(steps):
            for subset in range(1 << step):
                link_copy(step, subset, part).wait_send()
    keep.wait()


def plane_gather(own, member_count, collective_id, in_order):
    rows, width = own.shape
    steps = len(plane_masks(member_count))
    blocks = 1 << steps
    total = member_count * rows
    return pl.pallas_call(
        functools.partial(gather_kernel, member_count, in_order),
        out_shape=jax.ShapeDtypeStruct((total, width), own.dtype),
        in_specs=[pl.BlockSpec(memory_space=pl.ANY)],
        out_specs=pl.BlockSpec(memory_space=pl.ANY),
        scratch_shapes=[
            pltpu.SemaphoreType.DMA((blocks - 1, PIECES)),
            pltpu.SemaphoreType.DMA((blocks - 1, PIECES)),
            pltpu.SemaphoreType.DMA((blocks, PIECES)),
            pltpu.SemaphoreType.DMA((blocks, PIECES)),
            pltpu.SemaphoreType.DMA,
        ],
        compiler_params=pltpu.CompilerParams(collective_id=collective_id, has_side_effects=True),
        cost_estimate=pl.CostEstimate(
            flops=0, bytes_accessed=60 * total * width, transcendentals=0
        ),
        name="plane_gather",
    )(own)


def product_scatter_kernel(member_count, in_order, transposed, count, rows, *refs):
    lefts, rights, sum_ref = refs[:count], refs[count : 2 * count], refs[2 * count]
    held_lefts, held_rights = refs[2 * count + 1 : 3 * count + 1], refs[3 * count + 1 : 4 * count + 1]
    (
        outgoing,
        core_buffer,
        held,
        link_buffer,
        left_sem,
        right_sem,
        link_send,
        link_recv,
        core_send,
        core_recv,
    ) = refs[4 * count + 1 :]
    group = lax.axis_index("dp")
    member = lax.axis_index("fsdp")
    sibling = flip(member, 1)
    masks = plane_masks(member_count)
    steps = len(masks)
    blocks = 1 << steps
    piece = sum_ref.shape[1] // PIECES

    def left_copy(number, side, subset):
        owner = sibling if side else member
        block = walk(owner, subset, masks) if in_order else subset + side * blocks
        return pltpu.make_async_copy(
            lefts[number].at[pl.ds(pl.multiple_of(block * rows, rows), rows)],
            held_lefts[number].at[pl.ds((side * blocks + subset) * rows, rows)],
            left_sem.at[number, side, subset],
        )

    def right_copy(number):
        return pltpu.make_async_copy(rights[number], held_rights[number], right_sem.at[number])

    for number in range(count):
        right_copy(number).start()
        for side in (1, 0):
            for subset in range(blocks):
                left_copy(number, side, subset).start()
    greet(group, member, masks)

    def part(side, subset, where):
        where_rows = pl.ds((side * blocks + subset) * rows, rows)
        total = None
        for number in range(count):
            left = held_lefts[number][where_rows, :]
            if transposed:
                term = dot_nt(left, held_rights[number][where, :])
            else:
                term = dot_nn(left, held_rights[number][:, where])
            total = term if total is None else total + term
        return total

    def columns(index):
        return pl.ds(pl.multiple_of(index * piece, piece), piece)

    def core_copy(index):
        return pltpu.make_async_remote_copy(
            outgoing.at[:, columns(index)],
            core_buffer.at[:, columns(index)],
            core_send.at[index],
            core_recv.at[index],
            device_id=(group, sibling),
            device_id_type=MESH,
        )

    def slot(step, kept):
        return sum(blocks >> (s + 1) for s in range(step)) + (kept >> (step + 1))

    def link_copy(step, subset, index):
        number = slot(step, subset & ~(1 << step))
        return pltpu.make_async_remote_copy(
            held.at[pl.ds(subset * rows, rows), columns(index)],
            link_buffer.at[pl.ds(number * rows, rows), columns(index)],
            link_send.at[number, index],
            link_recv.at[number, index],
            device_id=(group, hop(member, step, masks)),
            device_id_type=MESH,
        )

    order = sorted(range(blocks), key=lambda s: (-(s & 1), -s))

    for number in range(count):
        right_copy(number).wait()
        for side in (1, 0):
            for subset in range(blocks):
                left_copy(number, side, subset).wait()

    def for_sibling(index, carried):
        where = columns(index)
        for subset in range(blocks):
            outgoing[pl.ds(subset * rows, rows), where] = part(1, subset, where).astype(BF16)
        core_copy(index).start()
        return carried

    lax.fori_loop(0, PIECES, for_sibling, 0)

    def for_links(index, carried):
        where = columns(index)
        core_copy(index).wait_recv()
        for subset in order:
            where_rows = pl.ds(subset * rows, rows)
            total = part(0, subset, where) + core_buffer[where_rows, where].astype(F32)
            if subset == 0:
                sum_ref[:, where] = total
            else:
                held[where_rows, where] = total.astype(BF16)
            if subset & 1:
                link_copy(0, subset, index).start()
        return carried

    lax.fori_loop(0, PIECES, for_links, 0)

    for step in range(steps):

        def one_step(index, carried, step=step):
            where = columns(index)
            for kept in sorted(range(0, blocks, 2 << step), reverse=True):
                link_copy(step, kept | (1 << step), index).wait_recv()
                arrived = link_buffer[pl.ds(slot(step, kept) * rows, rows), where].astype(F32)
                if kept == 0:
                    sum_ref[:, where] += arrived
                else:
                    where_rows = pl.ds(kept * rows, rows)
                    held[where_rows, where] = (
                        held[where_rows, where].astype(F32) + arrived
                    ).astype(BF16)
                if (kept >> (step + 1)) & 1:
                    link_copy(step + 1, kept, index).start()
            return carried

        lax.fori_loop(0, PIECES, one_step, 0)

    def finish(index, carried):
        core_copy(index).wait_send()
        for step in range(steps):
            for kept in range(0, blocks, 2 << step):
                link_copy(step, kept | (1 << step), index).wait_send()
        return carried

    lax.fori_loop(0, PIECES, finish, 0)


def product_scatter(lefts, rights, transposed, member_count, collective_id, in_order):
    count = len(lefts)
    total = lefts[0].shape[0]
    width = rights[0].shape[0 if transposed else 1]
    rows = total // member_count
    blocks = 1 << len(plane_masks(member_count))
    depth = sum(left.shape[1] for left in lefts)
    return pl.pallas_call(
        functools.partial(product_scatter_kernel, member_count, in_order, transposed, count, rows),
        out_shape=jax.ShapeDtypeStruct((rows, width), F32),
        in_specs=[pl.BlockSpec(memory_space=pl.ANY)] * (2 * count),
        out_specs=pl.BlockSpec(memory_space=pltpu.VMEM),
        scratch_shapes=[pltpu.VMEM(left.shape, BF16) for left in lefts]
        + [pltpu.VMEM(right.shape, BF16) for right in rights]
        + [
            pltpu.VMEM((blocks * rows, width), BF16),
            pltpu.VMEM((blocks * rows, width), BF16),
            pltpu.VMEM((blocks * rows, width), BF16),
            pltpu.VMEM(((blocks - 1) * rows, width), BF16),
            pltpu.SemaphoreType.DMA((count, 2, blocks)),
            pltpu.SemaphoreType.DMA((count,)),
            pltpu.SemaphoreType.DMA((blocks - 1, PIECES)),
            pltpu.SemaphoreType.DMA((blocks - 1, PIECES)),
            pltpu.SemaphoreType.DMA((PIECES,)),
            pltpu.SemaphoreType.DMA((PIECES,)),
        ],
        compiler_params=pltpu.CompilerParams(
            collective_id=collective_id, has_side_effects=True, vmem_limit_bytes=VMEM_BYTES
        ),
        cost_estimate=pl.CostEstimate(
            flops=2 * total * depth * width, bytes_accessed=60 * total * width, transcendentals=0
        ),
        name="product_scatter",
    )(*lefts, *rights)


def total_kernel(
    member_count, group_count, part_ref, sum_ref, near, held, far, near_send, near_recv, far_send, far_recv
):
    group = lax.axis_index("dp")
    member = lax.axis_index("fsdp")
    barrier = pltpu.get_barrier_semaphore()
    for away in range(1, member_count):
        pl.semaphore_signal(
            barrier,
            inc=1,
            device_id=(group, (member + away) % member_count),
            device_id_type=MESH,
        )
    for away in range(1, group_count):
        pl.semaphore_signal(
            barrier, inc=1, device_id=((group + away) % group_count, member), device_id_type=MESH
        )
    pl.semaphore_wait(barrier, member_count + group_count - 2)

    def near_copy(away):
        target = (member + away) % member_count
        return pltpu.make_async_remote_copy(
            part_ref.at[target],
            near.at[away],
            near_send.at[away],
            near_recv.at[away],
            device_id=(group, target),
            device_id_type=MESH,
        )

    def far_copy(away):
        return pltpu.make_async_remote_copy(
            held,
            far.at[away],
            far_send.at[away],
            far_recv.at[away],
            device_id=((group + away) % group_count, member),
            device_id_type=MESH,
        )

    for away in range(1, member_count):
        near_copy(away).start()
    total = part_ref[member]
    for away in range(1, member_count):
        near_copy(away).wait_recv()
        total = total + near[away]
    held[...] = total
    for away in range(1, group_count):
        far_copy(away).start()
    for away in range(1, group_count):
        far_copy(away).wait_recv()
        total = total + far[away]
    sum_ref[...] = total
    for away in range(1, member_count):
        near_copy(away).wait_send()
    for away in range(1, group_count):
        far_copy(away).wait_send()


def total_over_all(parts, group_count, collective_id):
    member_count, rows, lanes = parts.shape
    return pl.pallas_call(
        functools.partial(total_kernel, member_count, group_count),
        out_shape=jax.ShapeDtypeStruct((rows, lanes), F32),
        in_specs=[pl.BlockSpec(memory_space=pltpu.VMEM)],
        out_specs=pl.BlockSpec(memory_space=pltpu.VMEM),
        scratch_shapes=[
            pltpu.VMEM((member_count, rows, lanes), F32),
            pltpu.VMEM((rows, lanes), F32),
            pltpu.VMEM((group_count, rows, lanes), F32),
            pltpu.SemaphoreType.DMA((member_count,)),
            pltpu.SemaphoreType.DMA((member_count,)),
            pltpu.SemaphoreType.DMA((group_count,)),
            pltpu.SemaphoreType.DMA((group_count,)),
        ],
        compiler_params=pltpu.CompilerParams(collective_id=collective_id, has_side_effects=True),
        name="total_over_all",
    )(parts)


def half_group(shape, heads):
    return (lax.broadcasted_iota(jnp.int32, shape, 1) // HALF) % heads


def full_group(shape):
    return lax.broadcasted_iota(jnp.int32, shape, 1) // HD


def spread_keys(width):
    heads = width // HD
    row = lax.broadcasted_iota(jnp.int32, (2 * HD, width), 0)
    column = lax.broadcasted_iota(jnp.int32, (2 * HD, width), 1)
    source = column // (HALF * heads) * HALF + column % HALF
    return (row == source).astype(F32)


def spread_values(width):
    row = lax.broadcasted_iota(jnp.int32, (2 * HD, width), 0)
    column = lax.broadcasted_iota(jnp.int32, (2 * HD, width), 1)
    return (row == HD + column % HD).astype(F32)


def exact(left, right, dims):
    return lax.dot_general(
        left,
        right,
        (dims, ((), ())),
        precision=lax.Precision.HIGHEST,
        preferred_element_type=F32,
    )


def turn(values, cosine, sine):
    half = cosine.shape[1]
    first = values[:, :half]
    second = values[:, half:]
    return jnp.concatenate([first * cosine - second * sine, second * cosine + first * sine], axis=1)


def forward_kernel(
    heads,
    first_ref,
    projected_ref,
    cosine_ref,
    sine_ref,
    start_ref,
    query_ref,
    key_ref,
    value_ref,
    mixed_ref,
    lse_ref,
    value_columns,
    top,
    total,
    acc,
):
    step = pl.program_id(0)
    width = heads * HD
    start = start_ref[...]
    cosine = cosine_ref[...]
    sine = sine_ref[...]
    query = turn(projected_ref[:, :width], cosine, sine).astype(BF16)
    pair = projected_ref[:, width:]
    keys_here = turn(exact(pair, spread_keys(width), ((1,), (0,))), cosine, sine).astype(BF16)
    own_rows = pl.ds(pl.multiple_of(step * BLOCK, BLOCK), BLOCK)
    query_ref[...] = query
    key_ref[own_rows, :] = keys_here
    value_ref[...] = exact(pair, spread_values(width), ((1,), (0,))).astype(BF16)
    value_columns[:, own_rows] = jnp.transpose(pair)[HD:, :].astype(BF16)
    token = step * BLOCK + lax.broadcasted_iota(jnp.int32, (BLOCK, BLOCK), 1)
    within = lax.broadcasted_iota(jnp.int32, (BLOCK, BLOCK), 0)
    lane_head = half_group((BLOCK, width), heads)
    top[...] = jnp.full_like(top, MASKED)
    total[...] = jnp.zeros_like(total)
    acc[...] = jnp.zeros_like(acc)

    def one_block(block, carried):
        offset = pl.multiple_of(block * BLOCK, BLOCK)
        keys = key_ref[pl.ds(offset, BLOCK), :]
        values = value_columns[:, pl.ds(offset, BLOCK)]
        place = offset + within
        visible = (place >= start) & (place <= token)
        for head in range(heads):
            own_keys = jnp.where(lane_head == head, keys, jnp.zeros_like(keys))
            scores = jnp.where(visible, dot_nt(own_keys, query) * ATTENTION_SCALE, MASKED)
            old = top[head : head + 1, :]
            new = jnp.maximum(old, jnp.max(scores, axis=0, keepdims=True))
            weights = jnp.exp(scores - new)
            fade = jnp.exp(old - new)
            top[head : head + 1, :] = new
            total[head : head + 1, :] = total[head : head + 1, :] * fade + jnp.sum(
                weights, axis=0, keepdims=True
            )
            acc[head * HD : (head + 1) * HD, :] = acc[
                head * HD : (head + 1) * HD, :
            ] * fade + dot_nn(values, weights.astype(BF16))
        return carried

    lax.fori_loop(first_ref[step], step + 1, one_block, 0)
    for head in range(heads):
        acc[head * HD : (head + 1) * HD, :] = (
            acc[head * HD : (head + 1) * HD, :] / total[head : head + 1, :]
        )
    mixed_ref[...] = jnp.transpose(acc[...]).astype(BF16)
    lse_ref[...] = top[...] + jnp.log(total[...])


def attention_forward(first, projected, cosine, sine, start):
    tokens, columns = projected.shape
    width = columns - 2 * HD
    heads = width // HD
    by_block = pl.BlockSpec((BLOCK, width), lambda i, first: (i, 0))
    by_half = pl.BlockSpec((BLOCK, width // 2), lambda i, first: (i, 0))
    whole = pl.BlockSpec((tokens, width), lambda i, first: (0, 0))
    return pl.pallas_call(
        functools.partial(forward_kernel, heads),
        grid_spec=pltpu.PrefetchScalarGridSpec(
            num_scalar_prefetch=1,
            grid=(tokens // BLOCK,),
            in_specs=[
                pl.BlockSpec((BLOCK, columns), lambda i, first: (i, 0)),
                by_half,
                by_half,
                pl.BlockSpec((1, BLOCK), lambda i, first: (0, i)),
            ],
            out_specs=[
                by_block,
                whole,
                by_block,
                by_block,
                pl.BlockSpec((heads, BLOCK), lambda i, first: (0, i)),
            ],
            scratch_shapes=[
                pltpu.VMEM((HD, tokens), BF16),
                pltpu.VMEM((heads, BLOCK), F32),
                pltpu.VMEM((heads, BLOCK), F32),
                pltpu.VMEM((width, BLOCK), F32),
            ],
        ),
        out_shape=[jax.ShapeDtypeStruct((tokens, width), BF16)] * 4
        + [jax.ShapeDtypeStruct((heads, tokens), F32)],
        compiler_params=pltpu.CompilerParams(vmem_limit_bytes=VMEM_BYTES),
        cost_estimate=pl.CostEstimate(
            flops=64 * tokens * BLOCK * width, bytes_accessed=8 * tokens * width, transcendentals=0
        ),
        name="attention_forward",
    )(first, projected, cosine, sine, start)


def backward_kernel(
    heads,
    first_ref,
    query_ref,
    key_ref,
    value_ref,
    mixed_ref,
    grad_ref,
    lse_ref,
    start_ref,
    cosine_ref,
    sine_ref,
    out_ref,
    dquery,
    dkey,
    dvalue,
):
    step = pl.program_id(0)
    query = query_ref[...]
    grad = grad_ref[...]
    start = start_ref[...]
    width = query.shape[1]
    token = step * BLOCK + lax.broadcasted_iota(jnp.int32, (BLOCK, BLOCK), 1)
    within = lax.broadcasted_iota(jnp.int32, (BLOCK, BLOCK), 0)
    half_head = half_group((BLOCK, width), heads)
    full_head = full_group((BLOCK, width))
    zero = jnp.zeros((BLOCK, width), BF16)
    product = grad.astype(F32) * mixed_ref[...].astype(F32)
    chooser = (
        lax.broadcasted_iota(jnp.int32, (8, width), 0)
        == lax.broadcasted_iota(jnp.int32, (8, width), 1) // HD
    ).astype(F32)
    correction = exact(chooser, product, ((1,), (1,)))

    @pl.when(step == 0)
    def _():
        dkey[...] = jnp.zeros_like(dkey)
        dvalue[...] = jnp.zeros_like(dvalue)

    dquery[...] = jnp.zeros_like(dquery)

    def one_block(block, carried):
        offset = pl.multiple_of(block * BLOCK, BLOCK)
        rows = pl.ds(offset, BLOCK)
        keys = key_ref[rows, :]
        values = value_ref[rows, :]
        place = offset + within
        visible = (place >= start) & (place <= token)
        new_query = dquery[...]
        new_key = dkey[rows, :]
        new_value = dvalue[rows, :]
        for head in range(heads):
            own_keys = jnp.where(half_head == head, keys, zero)
            own_values = jnp.where(full_head == head, values, zero)
            scores = dot_nt(own_keys, query) * ATTENTION_SCALE
            probs = jnp.where(visible, jnp.exp(scores - lse_ref[head : head + 1, :]), 0.0)
            pressure = dot_nt(own_values, grad)
            dscores = (probs * (pressure - correction[head : head + 1, :])).astype(BF16)
            new_value = new_value + dot_nn(
                probs.astype(BF16), jnp.where(full_head == head, grad, zero)
            )
            new_key = new_key + dot_nn(dscores, jnp.where(half_head == head, query, zero))
            new_query = new_query + dot_tn(dscores, own_keys)
        dquery[...] = new_query
        dkey[rows, :] = new_key
        dvalue[rows, :] = new_value
        return carried

    lax.fori_loop(first_ref[step], step + 1, one_block, 0)
    own_rows = pl.ds(pl.multiple_of(step * BLOCK, BLOCK), BLOCK)
    out_ref[own_rows, :width] = (
        turn(dquery[...], cosine_ref[own_rows, :], -sine_ref[own_rows, :]) * ATTENTION_SCALE
    ).astype(BF16)

    @pl.when(step == pl.num_programs(0) - 1)
    def _():
        def fold(block, carried):
            rows = pl.ds(pl.multiple_of(block * BLOCK, BLOCK), BLOCK)
            turned = turn(dkey[rows, :], cosine_ref[rows, :], -sine_ref[rows, :]) * ATTENTION_SCALE
            out_ref[rows, width:] = (
                exact(turned, spread_keys(width), ((1,), (1,)))
                + exact(dvalue[rows, :], spread_values(width), ((1,), (1,)))
            ).astype(BF16)
            return carried

        lax.fori_loop(0, pl.num_programs(0), fold, 0)


def attention_backward(first, query, keys, values, mixed, grad, lse, start, cosine, sine):
    tokens, width = query.shape
    heads = width // HD
    columns = width + 2 * HD
    by_block = pl.BlockSpec((BLOCK, width), lambda i, first: (i, 0))
    whole = pl.BlockSpec((tokens, width), lambda i, first: (0, 0))
    whole_half = pl.BlockSpec((tokens, width // 2), lambda i, first: (0, 0))
    return pl.pallas_call(
        functools.partial(backward_kernel, heads),
        grid_spec=pltpu.PrefetchScalarGridSpec(
            num_scalar_prefetch=1,
            grid=(tokens // BLOCK,),
            in_specs=[
                by_block,
                whole,
                whole,
                by_block,
                by_block,
                pl.BlockSpec((heads, BLOCK), lambda i, first: (0, i)),
                pl.BlockSpec((1, BLOCK), lambda i, first: (0, i)),
                whole_half,
                whole_half,
            ],
            out_specs=pl.BlockSpec((tokens, columns), lambda i, first: (0, 0)),
            scratch_shapes=[
                pltpu.VMEM((BLOCK, width), F32),
                pltpu.VMEM((tokens, width), F32),
                pltpu.VMEM((tokens, width), F32),
            ],
        ),
        out_shape=jax.ShapeDtypeStruct((tokens, columns), BF16),
        compiler_params=pltpu.CompilerParams(vmem_limit_bytes=VMEM_BYTES),
        cost_estimate=pl.CostEstimate(
            flops=160 * tokens * BLOCK * width,
            bytes_accessed=24 * tokens * width,
            transcendentals=0,
        ),
        name="attention_backward",
    )(first, query, keys, values, mixed, grad, lse, start, cosine, sine)


def token_starts(lengths_row, group_tokens):
    count = lengths_row.shape[0]
    order = jnp.arange(count, dtype=jnp.int32)
    finish = jnp.sum(jnp.where(order[None, :] <= order[:, None], lengths_row[None, :], 0), axis=1)
    place = jnp.arange(group_tokens, dtype=jnp.int32)
    passed = place[:, None] >= finish[None, :]
    return jnp.max(jnp.where(passed, finish[None, :], 0), axis=1), place


def inverse_norm(values):
    return lax.rsqrt(jnp.mean(values * values, axis=1, keepdims=True) + EPSILON)


def after(value, *earlier):
    return lax.optimization_barrier((value, *earlier))[0]


def sum_over_groups(value):
    return lax.psum_scatter(value, "dp", scatter_dimension=0, tiled=True)


def gather_groups(value):
    return lax.all_gather(value, "dp", axis=0, tiled=True)


def send_to(value, member_count, partner):
    return lax.ppermute(value, "fsdp", [(m, partner(m)) for m in range(member_count)])


def permuted_swap(value):
    member_count = value.shape[0]
    member = lax.axis_index("fsdp")
    return [value] + [
        send_to(
            lax.dynamic_slice_in_dim(value, member ^ away, 1, 0),
            member_count,
            lambda m, away=away: m ^ away,
        )
        for away in range(1, member_count)
    ]


def joined(pieces):
    member = lax.axis_index("fsdp")
    result = pieces[0]
    for away in range(1, len(pieces)):
        result = lax.dynamic_update_slice_in_dim(result, pieces[away], member ^ away, 0)
    return result


def swap_members(value):
    return lax.all_to_all(value, "fsdp", split_axis=0, concat_axis=0, tiled=True)


def body(
    tokens,
    cotangent,
    query_weight,
    key_weight,
    value_weight,
    output_weight,
    gate_weight,
    up_weight,
    down_weight,
    attention_gain,
    feedforward_gain,
    lengths,
):
    members = lax.axis_size("fsdp")
    groups = lax.axis_size("dp")
    rows, model = tokens.shape
    group_tokens = rows * members
    shard = query_weight.shape[0]
    heads = NH // members
    width = heads * HD
    columns = width + 2 * HD
    copies = members // KVH
    out_columns = model // members
    down_rows = down_weight.shape[0]
    chunk_rows = down_rows // CHUNKS
    units = groups * chunk_rows
    gain_one = attention_gain.astype(F32)[:, None]
    gain_two = feedforward_gain.astype(F32)[:, None]

    scaled_query = (query_weight * gain_one).astype(BF16)
    scaled_key = (key_weight * gain_one).astype(BF16)
    scaled_value = (value_weight * gain_one).astype(BF16)
    packed = jnp.concatenate(
        [
            scaled_query.reshape(shard, members, heads, 2, HALF)
            .transpose(1, 0, 3, 2, 4)
            .reshape(members, shard, width),
            jnp.repeat(
                scaled_key.reshape(shard, KVH, HD).transpose(1, 0, 2), copies, axis=0
            ),
            jnp.repeat(
                scaled_value.reshape(shard, KVH, HD).transpose(1, 0, 2), copies, axis=0
            ),
            output_weight.reshape(shard, members, out_columns).transpose(1, 0, 2),
        ],
        axis=2,
    )
    packed = swap_members(packed).reshape(members * shard, columns + out_columns)
    inputs = tokens.astype(F32)
    inverse_one = inverse_norm(inputs)
    normed_one = plane_gather(after((inputs * inverse_one).astype(BF16), packed), members, 0, True)
    packed = after(gather_groups(packed), normed_one)
    upstream = cotangent.astype(F32)
    down_chunks = []
    for chunk in range(CHUNKS):
        part = down_weight[chunk * chunk_rows : (chunk + 1) * chunk_rows]
        down_chunks.append(gather_groups(after(part, normed_one)))
    gate_up = jnp.stack(
        [
            (weight * gain_two)
            .astype(BF16)
            .reshape(shard, groups, members, CHUNKS, chunk_rows)
            .transpose(2, 0, 3, 1, 4)
            for weight in (gate_weight, up_weight)
        ],
        axis=3,
    ).reshape(members, shard, CHUNKS * 2 * units)
    gate_up = permuted_swap(after(gate_up, normed_one))

    start, place = token_starts(lengths[0], group_tokens)
    first = start[::BLOCK] // BLOCK
    frequency = ROPE_BASE ** (-(2.0 * jnp.arange(HALF, dtype=F32)) / HD)
    angles = (place - start).astype(F32)[:, None] * frequency[None, :]
    cosine = jnp.tile(jnp.cos(angles), (1, heads))
    sine = jnp.tile(jnp.sin(angles), (1, heads))
    start = start[None, :]

    projection = packed[:, :columns]
    out_piece = lax.all_to_all(
        packed[:, columns:], "fsdp", split_axis=0, concat_axis=1, tiled=True
    )
    projected = dot_nn(normed_one, projection)
    query, keys, values, mixed, lse = attention_forward(first, projected, cosine, sine, start)
    mixed_then, down_chunks[0], *gate_up = lax.optimization_barrier(
        (mixed, down_chunks[0], *gate_up)
    )
    gate_up = joined(gate_up).reshape(members * shard, CHUNKS * 2 * units)
    gate_up_chunks = [
        gather_groups(gate_up[:, chunk * 2 * units : (chunk + 1) * 2 * units])
        for chunk in range(CHUNKS)
    ]
    branch_one = product_scatter(
        [after(mixed_then, gate_up)], [out_piece], False, members, 2, True
    )
    residual = inputs + RESIDUAL_SCALE * branch_one

    inverse_two = inverse_norm(residual)
    normed_two = plane_gather((residual * inverse_two).astype(BF16), members, 3, False)
    grad_two = plane_gather(
        after((RESIDUAL_SCALE * upstream).astype(BF16), normed_two), members, 1, False
    )
    hiddens = []
    grad_boths = []
    down_grads = []
    gate_up_grads = []
    for chunk in range(CHUNKS):
        both_weight = gate_up_chunks[chunk]
        down_piece = down_chunks[chunk]
        both = dot_nn(normed_two, both_weight)
        gate = both[:, :units]
        up = both[:, units:]
        sigmoid = jax.nn.sigmoid(gate)
        hidden = (gate * sigmoid * up).astype(BF16)
        grad_hidden = dot_nt(grad_two, down_piece)
        grad_both = jnp.concatenate(
            [
                (grad_hidden * up * sigmoid * (1.0 + gate * (1.0 - sigmoid))).astype(BF16),
                (grad_hidden * gate * sigmoid).astype(BF16),
            ],
            axis=1,
        )
        gate_up_grad = dot_tn(normed_two, grad_both).astype(BF16)
        down_grad = dot_tn(hidden, grad_two).astype(BF16)
        gate_up_grads.append(sum_over_groups(gate_up_grad))
        down_grads.append(sum_over_groups(down_grad))
        normed_two, grad_two, hidden, grad_both, _ = lax.optimization_barrier(
            (normed_two, grad_two, hidden, grad_both, gate_up_grad)
        )
        hiddens.append(hidden)
        grad_boths.append(grad_both)
    weighted_two = product_scatter(grad_boths, gate_up_chunks, True, members, 4, False)
    grad_residual = (
        upstream
        + inverse_two * weighted_two
        - residual * inverse_two**3 * jnp.mean(weighted_two * residual, axis=1, keepdims=True)
    )
    gain_term_two = jnp.sum(weighted_two * residual * inverse_two, axis=0)

    grad_one, gate_up_grads[0] = lax.optimization_barrier(
        ((RESIDUAL_SCALE * grad_residual).astype(BF16), gate_up_grads[0])
    )
    grad_one = plane_gather(grad_one, members, 5, True)
    grad_mixed = dot_nt(grad_one, out_piece).astype(BF16)
    out_grad = dot_tn(mixed, grad_one).astype(BF16)
    out_grad = lax.all_to_all(out_grad, "fsdp", split_axis=1, concat_axis=0, tiled=True)
    grad_mixed, gate_up_grads[-1] = lax.optimization_barrier((grad_mixed, gate_up_grads[-1]))
    grad_projected = attention_backward(
        first, query, keys, values, mixed, grad_mixed, lse, start, cosine, sine
    )
    packed_grad = jnp.concatenate(
        [dot_tn(normed_one, grad_projected).astype(BF16), out_grad], axis=1
    )
    grad_projected, packed_grad, down_grads[0] = lax.optimization_barrier(
        (grad_projected, packed_grad, down_grads[0])
    )
    packed_grad = sum_over_groups(packed_grad)
    weighted_one = product_scatter([grad_projected], [projection], True, members, 6, True)
    grad_inputs = (
        grad_residual
        + inverse_one * weighted_one
        - inputs * inverse_one**3 * jnp.mean(weighted_one * inputs, axis=1, keepdims=True)
    )
    gain_term_one = jnp.sum(weighted_one * inputs * inverse_one, axis=0)

    hiddens[-1] = after(hiddens[-1], weighted_one)
    branch_two = product_scatter(hiddens, down_chunks, False, members, 7, False)
    branch_two, down_grads[-1] = lax.optimization_barrier((branch_two, down_grads[-1]))
    output = residual + RESIDUAL_SCALE * branch_two

    gains = jnp.stack(
        [
            gain_term_one.reshape(groups, members, shard),
            gain_term_two.reshape(groups, members, shard),
        ],
        axis=2,
    ).reshape(groups, members, 2 * shard)
    gains = jnp.pad(
        gains.transpose(1, 0, 2), ((0, 0), (0, (-groups) % 8), (0, (-2 * shard) % 128))
    )
    gains = total_over_all(after(gains, branch_two), groups, 8)
    gains = lax.dynamic_slice_in_dim(gains, lax.axis_index("dp"), 1, 0)[0, : 2 * shard]
    gains = gains.reshape(2, shard)

    gate_up_grads = [
        swap_members(after(part.reshape(members, shard, 2 * units), branch_two))
        .reshape(members, shard, 2, groups, chunk_rows)
        for part in gate_up_grads
    ]
    both_grad = [
        jnp.stack([part[:, :, side] for part in gate_up_grads], axis=3)
        .transpose(1, 2, 0, 3, 4)
        .reshape(shard, -1)
        .astype(F32)
        * gain_two
        for side in range(2)
    ]
    packed_grad = swap_members(packed_grad.reshape(members, shard, -1)).astype(F32)
    grad_query = (
        packed_grad[:, :, :width]
        .reshape(members, shard, 2, heads, HALF)
        .transpose(1, 0, 3, 2, 4)
        .reshape(shard, -1)
    )

    def folded(part):
        return (
            part.reshape(KVH, copies, shard, HD).sum(axis=1).transpose(1, 0, 2).reshape(shard, -1)
        )

    return (
        output.astype(BF16),
        grad_inputs.astype(BF16),
        grad_query * gain_one,
        folded(packed_grad[:, :, width : width + HD]) * gain_one,
        folded(packed_grad[:, :, width + HD : columns]) * gain_one,
        packed_grad[:, :, columns:].transpose(1, 0, 2).reshape(shard, -1),
        both_grad[0],
        both_grad[1],
        jnp.concatenate(down_grads, axis=0).astype(F32),
        gains[0] / gain_one[:, 0],
        gains[1] / gain_two[:, 0],
    )


def solution(mesh):
    by_rows = P(("dp", "fsdp"), None)
    by_entries = P(("dp", "fsdp"))
    return jax.shard_map(
        body,
        mesh=mesh,
        in_specs=(by_rows,) * 9 + (by_entries,) * 2 + (P("dp", None),),
        out_specs=(by_rows,) * 9 + (by_entries,) * 2,
        check_vma=False,
    )
```

time: 948 us -> 776 us (0.82)
  matrix products: 206 us -> 131 us
  blocking collectives: 70.9 us -> 16.4 us
  waiting for transfers between devices: 73.8 us -> 32.9 us
  Pallas kernels: 406 us -> 437 us
  local copies, waits for them, and re-layouts: 91.6 us -> 61.9 us
    reduce_scatter x5, waiting for transfers between devices: 60.7 us -> 0.03 us  [sum_over_groups(): return lax.psum_scatter(value, 'dp', scatter_dimension=0, tiled=True)]
    dot_general x6 -> x3, matrix products: 75.7 us -> 32.4 us  [dot_nt(): lax.dot_general(left, right, (((1,), (1,)), ((), ())), preferred_element_...]
    unnamed x1 -> x0, blocking collectives: 41.1 us -> none
    dot_general x6 -> x3, matrix products: 70.5 us -> 39.2 us  [dot_nn(): return jnp.dot(left, right, preferred_element_type=F32)]
    pallas_call x8 -> x9, Pallas kernels: 333 us -> 359 us  [the longest x4 189 us: product_scatter(): pl.pallas_call(functools.partial(product_scatter_kernel, member_count, in...]
    slice x17 -> x6, local copies, waits for them, and re-layouts: 30.2 us -> 8.64 us  [the longest x1 2.77 us: body(): projection = packed[:, :columns]]
    all_to_all x4, waiting for transfers between devices: 12.5 us -> 29.9 us  [the longest x3 15.8 us: swap_members(): lax.all_to_all(value, 'fsdp', split_axis=0, concat_axis=0, tiled=True)]
    all_to_all x1, blocking collectives: 29.8 us -> 16.4 us  [swap_members(): lax.all_to_all(value, 'fsdp', split_axis=0, concat_axis=0, tiled=True)]
  transfers between devices with their start and end apart: 15 -> 22, of which waited for: 4 -> 4; matrix products, arithmetic and copies ran while one was open for 27% -> 28% of each run, Pallas kernels for 34% -> 57%
where the time goes in v2:
time: 776 us; the launch traced here: 769 us
  Pallas kernels  437 us (56%)
  matrix products  131 us (17%)
  local copies, waits for them, and re-layouts  61.9 us (8%)
  other arithmetic  47.8 us (6%)
  waiting for transfers between devices  32.9 us (4%)
  starting transfers between devices  26.5 us (3%)
  blocking collectives  16.4 us (2%)
  between operations  15.4 us (2%)
    pallas_call x4, Pallas kernels, product_scatter(): pl.pallas_call(functools.partial(product_scatter_kernel, member_count, in...  189 us
    pallas_call x4, Pallas kernels, plane_gather(): pl.pallas_call(functools.partial(gather_kernel, member_count, in_order),...  155 us
    dot_general x6, matrix products, dot_tn(): lax.dot_general(left, right, (((0,), (0,)), ((), ())), preferred_element_...  59.6 us
    pallas_call x1, Pallas kernels, attention_backward(): pl.pallas_call(functools.partial(backward_kernel, heads), grid_spec=pltpu...  44.6 us
    dot_general x3, matrix products, dot_nn(): return jnp.dot(left, right, preferred_element_type=F32)  39.2 us
    pallas_call x1, Pallas kernels, attention_forward(): pl.pallas_call(functools.partial(forward_kernel, heads), grid_spec=pltpu....  33.2 us
    dot_general x3, matrix products, dot_nt(): lax.dot_general(left, right, (((1,), (1,)), ((), ())), preferred_element_...  32.4 us
    all_to_all x1, blocking collectives, swap_members(): lax.all_to_all(value, 'fsdp', split_axis=0, concat_axis=0, tiled=True)  16.4 us
  transfers between devices with their start and end apart: 22, of which 4 were waited for; matrix products, arithmetic and copies ran while one was open for 28% of the time, Pallas kernels for 57%

profile of v2, /device:TPU:0, one launch (start us, length us, event | category | flops | bytes accessed | tf_op | source)
XLA Modules:
  0.0 768.8 jit_solution(15028572395709670378)
XLA Ops:
  11.8 16.4 %all_to_all.58 = bf16[8,64,640]{2,1,0:T(8,128)(2,1)} all-to-all(bf16[8,64,640]{2,1,0:T(8,128)(2,1)S(1)} %copy.147), channel_id=1, replica_groups=mesh['dp'=4,'fsdp'=8] {'fsdp'}, dimensions={0} | all-to-all | bytes 1310720 | tf_op jit(solution)/shard_map/all_to_all | solution.py:756
  32.2 38.3 %plane_gather.4 = bf16[2048,2048]{1,0:T(8,128)(2,1)} custom-call(bf16[256,2048]{1,0:T(8,128)(2,1)} %fusion.3.own_ref), custom_call_target="tpu_custom_call" | custom-call | bytes 251658240 | tf_op jit(solution)/shard_map/plane_gather/pallas_call | solution.py:147
  99.7 10.1 %fusion.8.projected_ref = f32[2048,384]{1,0:T(8,128)} fusion(bf16[2048,2048]{1,0:T(8,128)(2,1)} %plane_gather.4, bf16[2048,640]{1,0:T(8,128)(2,1)} %all-gather.6.cloned.1.call-done), kind=kOutput, calls=%fused_computation.98 | convolution fusion | flops 3221225472 | bytes 13107200 | tf_op jit(solution)/shard_map/dot_general | solution.py:30
  110.8 33.2 %attention_forward.1 = (bf16[2048,256]{1,0:T(8,128)(2,1)}, bf16[2048,256]{1,0:T(8,128)(2,1)}, bf16[2048,256]{1,0:T(8,128)(2,1)}, bf16[2048,256]{1,0:T(8,128)(2,1)}, f32[4,2048]{1,0:T(4,128)}) custom-call(s32[8]{0:T(128)} %and_select_fusion.first_ref, f32[2048,384]{1,0:T(8,128)} %fusion.8.projected_ref, f32[2048,128]{1,0:T(8,128)} %copy.148.cosine_ref, ...), custom_call_target="tpu_custom_call" | custom-call | flops 8589934592 | bytes 4194304 | tf_op jit(solution)/shard_map/attention_forward/pallas_call | solution.py:541
  159.5 14.0 %all-to-all-done.1 = bf16[8,256,256]{2,1,0:T(8,128)(2,1)S(1)} async-done(((bf16[8,256,256]{2,1,0:T(8,128)(2,1)}), bf16[8,256,256]{2,1,0:T(8,128)(2,1)S(1)}, u32[]{:S(2)}, u32[]{:S(2)}) %all-to-all-start.1) | async-done | bytes 1048608 | tf_op jit(solution)/shard_map/all_to_all | solution.py:838
  174.7 41.8 %product_scatter.4 = f32[256,2048]{1,0:T(8,128)} custom-call(bf16[2048,256]{1,0:T(8,128)(2,1)} %get-tuple-element.66.refs_0_.mixed_ref, bf16[256,2048]{1,0:T(8,128)(2,1)} %bitcast.105), custom_call_target="tpu_custom_call" | custom-call | flops 2147483648 | bytes 251658240 | tf_op jit(solution)/shard_map/product_scatter/pallas_call | solution.py:318
  219.7 39.2 %plane_gather.5 = bf16[2048,2048]{1,0:T(8,128)(2,1)} custom-call(bf16[256,2048]{1,0:T(8,128)(2,1)} %multiply_convert_fusion.7.own_ref), custom_call_target="tpu_custom_call" | custom-call | bytes 251658240 | tf_op jit(solution)/shard_map/plane_gather/pallas_call | solution.py:147
  258.9 39.1 %plane_gather.6 = bf16[2048,2048]{1,0:T(8,128)(2,1)} custom-call(bf16[256,2048]{1,0:T(8,128)(2,1)} %fusion.own_ref), custom_call_target="tpu_custom_call" | custom-call | bytes 251658240 | tf_op jit(solution)/shard_map/plane_gather/pallas_call | solution.py:147
  298.0 14.6 %fusion.15 = f32[2048,1024]{1,0:T(8,128)} fusion(bf16[2048,2048]{1,0:T(8,128)(2,1)} %plane_gather.5, bf16[2048,1024]{1,0:T(8,128)(2,1)} %all-gather.10.cloned.1.call-done.refs_2_), kind=kOutput, calls=%fused_computation.104 | convolution fusion | flops 8589934592 | bytes 20971520 | tf_op jit(solution)/shard_map/dot_general | solution.py:30
  312.5 11.1 %multiply_convert_fusion.4 = (bf16[2048,512]{1,0:T(8,128)(2,1)}, bf16[2048,512]{1,0:T(8,128)(2,1)}, bf16[2048,512]{1,0:T(8,128)(2,1)}) fusion(f32[2048,1024]{1,0:T(8,128)} %fusion.15, bf16[2048,2048]{1,0:T(8,128)(2,1)S(1)} %copy-done.2, bf16[512,2048]{1,0:T(8,128)(2,1)} %all-gather.8.cloned.1.call-done.refs_2_), kind=kOutput, calls=%fused_computation.7 | convolution fusion | flops 4311744512 | bytes 25165824 | tf_op jit(solution)/shard_map/dot_general | solution.py:34
  323.6 12.7 %convolution_convert_fusion.1 = bf16[2048,1024]{1,0:T(8,128)(2,1)} fusion(bf16[2048,2048]{1,0:T(8,128)(2,1)S(1)} %copy-done.3, bf16[2048,512]{1,0:T(8,128)(2,1)} %get-tuple-element.148, bf16[2048,512]{1,0:T(8,128)(2,1)} %get-tuple-element.147), kind=kOutput, calls=%fused_computation.16 | convolution fusion | flops 8600420352 | bytes 16777216 | tf_op jit(solution)/shard_map/dot_general | solution.py:38
  341.2 14.6 %fusion.16 = f32[2048,1024]{1,0:T(8,128)} fusion(bf16[2048,2048]{1,0:T(8,128)(2,1)} %plane_gather.5, bf16[2048,1024]{1,0:T(8,128)(2,1)} %all-gather.12.cloned.1.call-done.refs_3_), kind=kOutput, calls=%fused_computation.105 | convolution fusion | flops 8589934592 | bytes 20971520 | tf_op jit(solution)/shard_map/dot_general | solution.py:30
  358.1 14.3 %multiply_convert_fusion.1 = (bf16[2048,512]{1,0:T(8,128)(2,1)S(1)}, bf16[2048,512]{1,0:T(8,128)(2,1)S(1)}, bf16[2048,512]{1,0:T(8,128)(2,1)}) fusion(f32[2048,1024]{1,0:T(8,128)} %fusion.16, bf16[2048,2048]{1,0:T(8,128)(2,1)} %plane_gather.6, bf16[512,2048]{1,0:T(8,128)(2,1)} %all-gather.14.cloned.1.call-done.refs_3_), kind=kOutput, calls=%fused_computation.3 | convolution fusion | flops 4311744512 | bytes 25165824 | tf_op jit(solution)/shard_map/dot_general | solution.py:34
  374.4 13.2 %convolution_convert_fusion = bf16[2048,1024]{1,0:T(8,128)(2,1)} fusion(bf16[2048,2048]{1,0:T(8,128)(2,1)} %plane_gather.5, bf16[2048,512]{1,0:T(8,128)(2,1)S(1)} %get-tuple-element.146, bf16[2048,512]{1,0:T(8,128)(2,1)S(1)} %get-tuple-element.145), kind=kOutput, calls=%fused_computation.15 | convolution fusion | flops 8600420352 | bytes 16777216 | tf_op jit(solution)/shard_map/dot_general | solution.py:38
  387.6 9.9 %convolution_convert_fusion.3 = bf16[512,2048]{1,0:T(8,128)(2,1)} fusion(bf16[2048,512]{1,0:T(8,128)(2,1)} %get-tuple-element.69.refs_0_, bf16[2048,2048]{1,0:T(8,128)(2,1)} %plane_gather.6), kind=kOutput, calls=%fused_computation.18 | convolution fusion | flops 4296015872 | bytes 12582912 | tf_op jit(solution)/shard_map/dot_general | solution.py:38
  402.4 55.0 %product_scatter.5 = f32[256,2048]{1,0:T(8,128)} custom-call(bf16[2048,1024]{1,0:T(8,128)(2,1)} %pad_maximum_fusion.refs_0_, bf16[2048,1024]{1,0:T(8,128)(2,1)} %pad_maximum_fusion.1.refs_1_, bf16[2048,1024]{1,0:T(8,128)(2,1)} %all-gather.10.cloned.1.call-done.refs_2_, bf16[2048,1024]{1,0:T(8,128)(2,1)} %all-gather.12.cloned.1.call-done.refs_3_), custom_call_target="tpu_custom_call" | custom-call | flops 17179869184 | bytes 251658240 | tf_op jit(solution)/shard_map/product_scatter/pallas_call | solution.py:318
  459.7 9.1 %convolution_convert_fusion.2 = bf16[512,2048]{1,0:T(8,128)(2,1)} fusion(bf16[2048,512]{1,0:T(8,128)(2,1)S(1)} %copy-done.29, bf16[2048,2048]{1,0:T(8,128)(2,1)} %plane_gather.6), kind=kOutput, calls=%fused_computation.17 | convolution fusion | flops 4296015872 | bytes 12582912 | tf_op jit(solution)/shard_map/dot_general | solution.py:38
  473.9 38.7 %plane_gather.7 = bf16[2048,2048]{1,0:T(8,128)(2,1)} custom-call(bf16[256,2048]{1,0:T(8,128)(2,1)} %get-tuple-element.79.own_ref), custom_call_target="tpu_custom_call" | custom-call | bytes 251658240 | tf_op jit(solution)/shard_map/plane_gather/pallas_call | solution.py:147
  530.7 44.6 %attention_backward.1.refs_0_ = bf16[2048,384]{1,0:T(8,128)(2,1)} custom-call(s32[8]{0:T(128)} %and_select_fusion.first_ref, bf16[2048,256]{1,0:T(8,128)(2,1)} %get-tuple-element.74.query_ref, bf16[2048,256]{1,0:T(8,128)(2,1)} %get-tuple-element.75.key_ref, bf16[2048,256]{1,0:T(8,128)(2,1)} %get-tuple-element.76.value_ref, ...), custom_call_target="tpu_custom_call" | custom-call | flops 21474836480 | bytes 12582912 | tf_op jit(solution)/shard_map/attention_backward/pallas_call | solution.py:671
  575.3 8.5 %convolution_convert_fusion.4 = bf16[2048,384]{0,1:T(8,128)(2,1)} fusion(bf16[2048,2048]{1,0:T(8,128)(2,1)} %plane_gather.4, bf16[2048,384]{1,0:T(8,128)(2,1)} %attention_backward.1.refs_0_), kind=kOutput, calls=%fused_computation.19 | convolution fusion | flops 3222011904 | bytes 11534336 | tf_op jit(solution)/shard_map/dot_general | solution.py:38
  589.9 44.5 %product_scatter.6 = f32[256,2048]{1,0:T(8,128)} custom-call(bf16[2048,384]{1,0:T(8,128)(2,1)} %attention_backward.1.refs_0_, bf16[2048,384]{1,0:T(8,128)(2,1)} %slice.66.refs_1_), custom_call_target="tpu_custom_call" | custom-call | flops 3221225472 | bytes 251658240 | tf_op jit(solution)/shard_map/product_scatter/pallas_call | solution.py:318
  634.5 47.2 %product_scatter.7 = f32[256,2048]{1,0:T(8,128)} custom-call(bf16[2048,512]{1,0:T(8,128)(2,1)} %get-tuple-element.69.refs_0_, bf16[2048,512]{1,0:T(8,128)(2,1)} %get-tuple-element.83.refs_1_, bf16[512,2048]{1,0:T(8,128)(2,1)} %all-gather.8.cloned.1.call-done.refs_2_, bf16[512,2048]{1,0:T(8,128)(2,1)} %all-gather.14.cloned.1.call-done.refs_3_), custom_call_target="tpu_custom_call" | custom-call | flops 8589934592 | bytes 251658240 | tf_op jit(solution)/shard_map/product_scatter/pallas_call | solution.py:318
  689.0 15.0 %total_over_all.1 = f32[8,128]{1,0:T(8,128)} custom-call(f32[8,8,128]{2,1,0:T(8,128)} %pad.4.part_ref), custom_call_target="tpu_custom_call" | custom-call | tf_op jit(solution)/shard_map/total_over_all/pallas_call | solution.py:408
  719.1 8.9 %all-to-all-done.5 = bf16[8,64,1024]{2,1,0:T(8,128)(2,1)} async-done(((bf16[8,64,1024]{2,1,0:T(8,128)(2,1)}), bf16[8,64,1024]{2,1,0:T(8,128)(2,1)}, u32[]{:S(2)}, u32[]{:S(2)}) %all-to-all-start.5) | async-done | bytes 1048608 | tf_op jit(solution)/shard_map/all_to_all | solution.py:756
  (210 shorter events, 159.3 us)
Async XLA Ops:
  7.2 92.5 %all-gather.6.cloned.1.call-start = ((), (), s32[]{:S(2)}) async-start(), calls=%async_computation.11 | async-start | bytes 3276800 | tf_op jit(solution)/shard_map/all_gather | solution.py:727
  28.2 115.9 %all-gather.8.cloned.1.call-start = ((), (), s32[]{:S(2)}) async-start(), calls=%async_computation.12 | async-start | bytes 2621440 | tf_op jit(solution)/shard_map/all_gather | solution.py:727
  70.6 227.3 %all-gather.10.cloned.1.call-start = ((), (), s32[]{:S(2)}) async-start(), calls=%async_computation.13 | async-start | bytes 5242880 | tf_op jit(solution)/shard_map/all_gather | solution.py:727
  94.3 15.4 %collective-permute-start.6 = (bf16[1,64,2048]{2,1,0:T(8,128)(2,1)}, bf16[1,64,2048]{2,1,0:T(8,128)(2,1)S(1)}, u32[]{:S(2)}, u32[]{:S(2)}) collective-permute-start(bf16[1,64,2048]{2,1,0:T(8,128)(2,1)} %get-tuple-element.153), channel_id=1, source_target_pairs={{0,7},{1,6},{2,5},{3,4},{4,3},{5,2},{6,1},{7,0},{8,15},{9,14},{10,... | collective-permute-start | bytes 786440 | tf_op jit(solution)/shard_map/ppermute | solution.py:731
  95.8 15.0 %collective-permute-start.5 = (bf16[1,64,2048]{2,1,0:T(8,128)(2,1)}, bf16[1,64,2048]{2,1,0:T(8,128)(2,1)}, u32[]{:S(2)}, u32[]{:S(2)}) collective-permute-start(bf16[1,64,2048]{2,1,0:T(8,128)(2,1)} %get-tuple-element.154), channel_id=1, source_target_pairs={{0,6},{1,7},{2,4},{3,5},{4,2},{5,3},{6,0},{7,1},{8,14},{9,15},{10,... | collective-permute-start | bytes 786440 | tf_op jit(solution)/shard_map/ppermute | solution.py:731
  97.2 46.8 %collective-permute-start.4 = (bf16[1,64,2048]{2,1,0:T(8,128)(2,1)}, bf16[1,64,2048]{2,1,0:T(8,128)(2,1)}, u32[]{:S(2)}, u32[]{:S(2)}) collective-permute-start(bf16[1,64,2048]{2,1,0:T(8,128)(2,1)} %get-tuple-element.155), channel_id=1, source_target_pairs={{0,5},{1,4},{2,7},{3,6},{4,1},{5,0},{6,3},{7,2},{8,13},{9,12},{10,... | collective-permute-start | bytes 786440 | tf_op jit(solution)/shard_map/ppermute | solution.py:731
  97.9 46.1 %collective-permute-start.3 = (bf16[1,64,2048]{2,1,0:T(8,128)(2,1)}, bf16[1,64,2048]{2,1,0:T(8,128)(2,1)}, u32[]{:S(2)}, u32[]{:S(2)}) collective-permute-start(bf16[1,64,2048]{2,1,0:T(8,128)(2,1)} %get-tuple-element.156), channel_id=1, source_target_pairs={{0,4},{1,5},{2,6},{3,7},{4,0},{5,1},{6,2},{7,3},{8,12},{9,13},{10,... | collective-permute-start | bytes 786440 | tf_op jit(solution)/shard_map/ppermute | solution.py:731
  98.7 45.3 %collective-permute-start.2 = (bf16[1,64,2048]{2,1,0:T(8,128)(2,1)}, bf16[1,64,2048]{2,1,0:T(8,128)(2,1)}, u32[]{:S(2)}, u32[]{:S(2)}) collective-permute-start(bf16[1,64,2048]{2,1,0:T(8,128)(2,1)} %get-tuple-element.157), channel_id=1, source_target_pairs={{0,3},{1,2},{2,1},{3,0},{4,7},{5,6},{6,5},{7,4},{8,11},{9,10},{10,... | collective-permute-start | bytes 786440 | tf_op jit(solution)/shard_map/ppermute | solution.py:731
  109.7 34.3 %collective-permute-start.1 = (bf16[1,64,2048]{2,1,0:T(8,128)(2,1)S(1)}, bf16[1,64,2048]{2,1,0:T(8,128)(2,1)}, u32[]{:S(2)}, u32[]{:S(2)}) collective-permute-start(bf16[1,64,2048]{2,1,0:T(8,128)(2,1)S(1)} %copy-done.16), channel_id=1, source_target_pairs={{0,2},{1,3},{2,0},{3,1},{4,6},{5,7},{6,4},{7,5},{8,10},{9,11},{10,... | collective-permute-start | bytes 786440 | tf_op jit(solution)/shard_map/ppermute | solution.py:731
  110.8 33.3 %collective-permute-start = (bf16[1,64,2048]{2,1,0:T(8,128)(2,1)S(1)}, bf16[1,64,2048]{2,1,0:T(8,128)(2,1)}, u32[]{:S(2)}, u32[]{:S(2)}) collective-permute-start(bf16[1,64,2048]{2,1,0:T(8,128)(2,1)S(1)} %copy-done.15), channel_id=1, source_target_pairs={{0,1},{1,0},{2,3},{3,2},{4,5},{5,4},{6,7},{7,6},{8,9},{9,8},{10,11... | collective-permute-start | bytes 786440 | tf_op jit(solution)/shard_map/ppermute | solution.py:731
  151.5 189.7 %all-gather.12.cloned.1.call-start = ((), (), s32[]{:S(2)}) async-start(), calls=%async_computation.14 | async-start | bytes 5242880 | tf_op jit(solution)/shard_map/all_gather | solution.py:727
  154.5 19.1 %all-to-all-start.1 = ((bf16[8,256,256]{2,1,0:T(8,128)(2,1)}), bf16[8,256,256]{2,1,0:T(8,128)(2,1)S(1)}, u32[]{:S(2)}, u32[]{:S(2)}) async-start(bf16[8,256,256]{2,1,0:T(8,128)(2,1)} %bitcast.95), calls=%async_computation.1 | async-start | bytes 2097152 | tf_op jit(solution)/shard_map/all_to_all | solution.py:838
  158.2 199.8 %all-gather.14.cloned.1.call-start = ((), (), s32[]{:S(2)}) async-start(), calls=%async_computation.15 | async-start | bytes 2621440 | tf_op jit(solution)/shard_map/all_gather | solution.py:727
  159.5 314.4 %reduce-scatter.6.cloned.1.call-start = ((), (), s32[]{:S(2)}) async-start(), calls=%async_computation.16 | async-start | bytes 5242880 | tf_op jit(solution)/shard_map/reduce_scatter | solution.py:723
  336.4 190.7 %reduce-scatter.8.cloned.1.call-start = ((), (), s32[]{:S(2)}) async-start(), calls=%async_computation.17 | async-start | bytes 5242880 | tf_op jit(solution)/shard_map/reduce_scatter | solution.py:723
  387.6 199.5 %reduce-scatter.10.cloned.1.call-start = ((), (), s32[]{:S(2)}) async-start(), calls=%async_computation.18 | async-start | bytes 2621440 | tf_op jit(solution)/shard_map/reduce_scatter | solution.py:723
  397.6 284.1 %reduce-scatter.12.cloned.1.call-start = ((), (), s32[]{:S(2)}) async-start(), calls=%async_computation.19 | async-start | bytes 2621440 | tf_op jit(solution)/shard_map/reduce_scatter | solution.py:723
  527.1 56.8 %all-to-all-start.2 = ((bf16[256,8,256]{0,2,1:T(8,128)(2,1)}), bf16[256,8,256]{0,2,1:T(8,128)(2,1)S(1)}, u32[]{:S(2)}, u32[]{:S(2)}) async-start(bf16[256,8,256]{0,2,1:T(8,128)(2,1)} %bitcast.21), calls=%async_computation.4 | async-start | bytes 2097152 | tf_op jit(solution)/shard_map/all_to_all | solution.py:904
  530.6 209.6 %reduce-scatter.14.cloned.1.call-start = ((), (), s32[]{:S(2)}) async-start(), calls=%async_computation.20 | async-start | bytes 3276800 | tf_op jit(solution)/shard_map/reduce_scatter | solution.py:723
  681.8 26.3 %all-to-all-start.4 = ((bf16[8,64,1024]{2,1,0:T(8,128)(2,1)}), bf16[8,64,1024]{2,1,0:T(8,128)(2,1)}, u32[]{:S(2)}, u32[]{:S(2)}) async-start(bf16[8,64,1024]{2,1,0:T(8,128)(2,1)} %bitcast.103), calls=%async_computation.9 | async-start | bytes 2097152 | tf_op jit(solution)/shard_map/all_to_all | solution.py:756
  686.2 18.5 %copy-start.25 = (bf16[64]{0:T(256)(128)(2,1)S(1)}, bf16[64]{0:T(256)(128)(2,1)}, u32[]{:S(2)}) copy-start(bf16[64]{0:T(256)(128)(2,1)} %param.21) | copy-start | bytes 388
  686.2 18.5 %copy-start.27 = (bf16[64]{0:T(256)(128)(2,1)S(1)}, bf16[64]{0:T(256)(128)(2,1)}, u32[]{:S(2)}) copy-start(bf16[64]{0:T(256)(128)(2,1)} %param.22) | copy-start | bytes 388
  708.1 19.9 %all-to-all-start.5 = ((bf16[8,64,1024]{2,1,0:T(8,128)(2,1)}), bf16[8,64,1024]{2,1,0:T(8,128)(2,1)}, u32[]{:S(2)}, u32[]{:S(2)}) async-start(bf16[8,64,1024]{2,1,0:T(8,128)(2,1)} %bitcast.104), calls=%async_computation.10 | async-start | bytes 2097152 | tf_op jit(solution)/shard_map/all_to_all | solution.py:756
  742.6 14.6 %all-to-all-start.3 = ((bf16[8,64,640]{2,1,0:T(8,128)(2,1)}), bf16[8,64,640]{2,1,0:T(8,128)(2,1)S(1)}, u32[]{:S(2)}, u32[]{:S(2)}) async-start(bf16[8,64,640]{2,1,0:T(8,128)(2,1)} %bitcast.23), calls=%async_computation.8 | async-start | bytes 1310720 | tf_op jit(solution)/shard_map/all_to_all | solution.py:756
  (28 other events, 179.1 us)
Sparse Core Ops, SparseCore 0:
  28.3 54.1 all-gather.5
  84.6 44.6 all-gather.7
  151.6 79.1 all-gather.9
  232.3 79.2 all-gather.11
  313.6 44.4 all-gather.13
  360.2 75.4 reduce-scatter.5
  438.1 77.2 reduce-scatter.7
  517.7 44.3 reduce-scatter.9
  564.5 42.9 reduce-scatter.11
  609.7 51.6 reduce-scatter.13

commit v3 on v2

--- a/solution.py
+++ b/solution.py
@@ -71,9 +71,11 @@
     pl.semaphore_wait(barrier, len(partners))
 
 
-def gather_kernel(
-    member_count, in_order, own_ref, all_ref, link_send, link_recv, core_send, core_recv, local_sem
-):
+def gather_kernel(member_count, in_order, count, own_ref, *refs):
+    operands = refs[: count + 2] if count else ()
+    refs = refs[len(operands) :]
+    all_ref, results, refs = refs[0], refs[1 : 4 if count else 1], refs[4 if count else 1 :]
+    link_send, link_recv, core_send, core_recv, local_sem = refs[:5]
     group = lax.axis_index("dp")
     member = lax.axis_index("fsdp")
     masks = plane_masks(member_count)
@@ -121,6 +123,74 @@
     keep.start()
     for part in range(PIECES):
         core_copy(0, part).start()
+    tiles = []
+    if count:
+        helds = refs[5 : 7 + count]
+        down_grad, out_sibling, out_own = refs[7 + count : 10 + count]
+        load_sem, store_sem = refs[10 + count :]
+        hiddens, gradient, down = helds[:count], helds[count], helds[count + 1]
+        units = hiddens[0].shape[1]
+        loads = [
+            pltpu.make_async_copy(source, target, load_sem.at[number])
+            for number, (source, target) in enumerate(zip(operands, helds))
+        ]
+        stores = [
+            pltpu.make_async_copy(source, target, store_sem.at[number])
+            for number, (source, target) in enumerate(
+                zip((down_grad, out_sibling, out_own), results)
+            )
+        ]
+        for load in loads:
+            load.start()
+        half = out_own.shape[0]
+        height = min(256, half)
+        width = down.shape[1] // 4
+
+        def out_tile(target, base, row):
+            def one_part(index, carried):
+                columns = pl.ds(pl.multiple_of(index * width, width), width)
+                total = None
+                for number in range(count):
+                    term = dot_nn(
+                        hiddens[number][base + row : base + row + height, :],
+                        down[number * units : (number + 1) * units, columns],
+                    )
+                    total = term if total is None else total + term
+                target[row : row + height, columns] = total.astype(BF16)
+                return carried
+
+            lax.fori_loop(0, 4, one_part, 0)
+
+        tile = min(256, units)
+
+        def grad_tile(number, column):
+            def one_part(index, carried):
+                columns = pl.ds(pl.multiple_of(index * width, width), width)
+                first = number * units + column
+                down_grad[first : first + tile, columns] = dot_tn(
+                    hiddens[number][:, column : column + tile], gradient[:, columns]
+                ).astype(BF16)
+                return carried
+
+            lax.fori_loop(0, 4, one_part, 0)
+
+        for load in loads[:count] + loads[count + 1 :]:
+            tiles.append(load.wait)
+        for target, base, store in (
+            (out_sibling, half, stores[1]),
+            (out_own, 0, stores[2]),
+        ):
+            for row in range(0, half, height):
+                tiles.append(functools.partial(out_tile, target, base, row))
+            tiles.append(store.start)
+        tiles.append(loads[count].wait)
+        for number in range(count):
+            for column in range(0, units, tile):
+                tiles.append(functools.partial(grad_tile, number, column))
+        tiles.append(stores[0].start)
+    share = -(-len(tiles) // (steps * PIECES))
+
+    turn = 0
     for step in range(steps):
         for part in range(PIECES):
             for subset in range(1 << step):
@@ -129,6 +199,9 @@
                 for later in range(step + 1, steps):
                     link_copy(later, arrived, part).start()
                 core_copy(arrived, part).start()
+            for run in tiles[turn * share : (turn + 1) * share]:
+                run()
+            turn += 1
     for part in range(PIECES):
         for subset in range(1 << steps):
             core_copy(subset, part).wait()
@@ -137,31 +210,118 @@
             for subset in range(1 << step):
                 link_copy(step, subset, part).wait_send()
     keep.wait()
-
-
-def plane_gather(own, member_count, collective_id, in_order):
+    if count:
+        for store in stores:
+            store.wait()
+
+
+def plane_gather(own, member_count, collective_id, in_order, extras=None):
     rows, width = own.shape
     steps = len(plane_masks(member_count))
     blocks = 1 << steps
     total = member_count * rows
-    return pl.pallas_call(
-        functools.partial(gather_kernel, member_count, in_order),
-        out_shape=jax.ShapeDtypeStruct((total, width), own.dtype),
-        in_specs=[pl.BlockSpec(memory_space=pl.ANY)],
-        out_specs=pl.BlockSpec(memory_space=pl.ANY),
-        scratch_shapes=[
-            pltpu.SemaphoreType.DMA((blocks - 1, PIECES)),
-            pltpu.SemaphoreType.DMA((blocks - 1, PIECES)),
-            pltpu.SemaphoreType.DMA((blocks, PIECES)),
-            pltpu.SemaphoreType.DMA((blocks, PIECES)),
-            pltpu.SemaphoreType.DMA,
-        ],
-        compiler_params=pltpu.CompilerParams(collective_id=collective_id, has_side_effects=True),
+    any_space = pl.BlockSpec(memory_space=pl.ANY)
+    scratch = [
+        pltpu.SemaphoreType.DMA((blocks - 1, PIECES)),
+        pltpu.SemaphoreType.DMA((blocks - 1, PIECES)),
+        pltpu.SemaphoreType.DMA((blocks, PIECES)),
+        pltpu.SemaphoreType.DMA((blocks, PIECES)),
+        pltpu.SemaphoreType.DMA,
+    ]
+    operands = [own]
+    out_shape = [jax.ShapeDtypeStruct((total, width), own.dtype)]
+    count = 0
+    if extras:
+        hiddens, gradient, down = extras
+        count = len(hiddens)
+        operands += [*hiddens, gradient, down]
+        scratch += [pltpu.VMEM(value.shape, BF16) for value in operands[1:]]
+        out_shape += [
+            jax.ShapeDtypeStruct((down.shape[0], gradient.shape[1]), BF16),
+            jax.ShapeDtypeStruct((total // 2, down.shape[1]), BF16),
+            jax.ShapeDtypeStruct((total // 2, down.shape[1]), BF16),
+        ]
+        scratch += [pltpu.VMEM(value.shape, BF16) for value in out_shape[1:]]
+        scratch += [pltpu.SemaphoreType.DMA((count + 2,)), pltpu.SemaphoreType.DMA((3,))]
+    result = pl.pallas_call(
+        functools.partial(gather_kernel, member_count, in_order, count),
+        out_shape=out_shape,
+        in_specs=[any_space] * len(operands),
+        out_specs=[any_space] * len(out_shape),
+        scratch_shapes=scratch,
+        compiler_params=pltpu.CompilerParams(
+            collective_id=collective_id, has_side_effects=True, vmem_limit_bytes=VMEM_BYTES
+        ),
         cost_estimate=pl.CostEstimate(
             flops=0, bytes_accessed=60 * total * width, transcendentals=0
         ),
         name="plane_gather",
-    )(own)
+    )(*operands)
+    return result if extras else result[0]
+
+
+def swap_kernel(member_count, count, *refs):
+    sources, targets = refs[:count], refs[count : 2 * count]
+    send_sem, recv_sem, local_sem = refs[2 * count :]
+    group = lax.axis_index("dp")
+    member = lax.axis_index("fsdp")
+    barrier = pltpu.get_barrier_semaphore()
+    for away in range(1, member_count):
+        pl.semaphore_signal(
+            barrier,
+            inc=1,
+            device_id=(group, (member + away) % member_count),
+            device_id_type=MESH,
+        )
+    pl.semaphore_wait(barrier, member_count - 1)
+
+    def copy(number, away):
+        target = (member + away) % member_count
+        return pltpu.make_async_remote_copy(
+            sources[number].at[target],
+            targets[number].at[member],
+            send_sem.at[number, away],
+            recv_sem.at[number, away],
+            device_id=(group, target),
+            device_id_type=MESH,
+        )
+
+    def keep(number):
+        return pltpu.make_async_copy(
+            sources[number].at[member], targets[number].at[member], local_sem.at[number]
+        )
+
+    for number in range(count):
+        for away in range(1, member_count):
+            copy(number, away).start()
+        keep(number).start()
+    for number in range(count):
+        for away in range(1, member_count):
+            copy(number, away).wait()
+        keep(number).wait()
+
+
+def plane_swap(values, member_count, collective_id):
+    count = len(values)
+    any_space = pl.BlockSpec(memory_space=pl.ANY)
+    return pl.pallas_call(
+        functools.partial(swap_kernel, member_count, count),
+        out_shape=[jax.ShapeDtypeStruct(value.shape, value.dtype) for value in values],
+        in_specs=[any_space] * count,
+        out_specs=[any_space] * count,
+        scratch_shapes=[
+            pltpu.SemaphoreType.DMA((count, member_count)),
+            pltpu.SemaphoreType.DMA((count, member_count)),
+            pltpu.SemaphoreType.DMA((count,)),
+        ],
+        compiler_params=pltpu.CompilerParams(collective_id=collective_id, has_side_effects=True),
+        cost_estimate=pl.CostEstimate(
+            flops=0,
+            bytes_accessed=60 * sum(value.size for value in values),
+            transcendentals=0,
+        ),
+        name="plane_swap",
+    )(*values)
 
 
 def product_scatter_kernel(member_count, in_order, transposed, count, rows, *refs):
@@ -315,12 +475,8 @@
     rows = total // member_count
     blocks = 1 << len(plane_masks(member_count))
     depth = sum(left.shape[1] for left in lefts)
-    return pl.pallas_call(
-        functools.partial(product_scatter_kernel, member_count, in_order, transposed, count, rows),
-        out_shape=jax.ShapeDtypeStruct((rows, width), F32),
-        in_specs=[pl.BlockSpec(memory_space=pl.ANY)] * (2 * count),
-        out_specs=pl.BlockSpec(memory_space=pltpu.VMEM),
-        scratch_shapes=[pltpu.VMEM(left.shape, BF16) for left in lefts]
+    scratch = (
+        [pltpu.VMEM(left.shape, BF16) for left in lefts]
         + [pltpu.VMEM(right.shape, BF16) for right in rights]
         + [
             pltpu.VMEM((blocks * rows, width), BF16),
@@ -333,7 +489,16 @@
             pltpu.SemaphoreType.DMA((blocks - 1, PIECES)),
             pltpu.SemaphoreType.DMA((PIECES,)),
             pltpu.SemaphoreType.DMA((PIECES,)),
-        ],
+        ]
+    )
+    any_space = pl.BlockSpec(memory_space=pl.ANY)
+    in_vmem = pl.BlockSpec(memory_space=pltpu.VMEM)
+    return pl.pallas_call(
+        functools.partial(product_scatter_kernel, member_count, in_order, transposed, count, rows),
+        out_shape=jax.ShapeDtypeStruct((rows, width), F32),
+        in_specs=[any_space] * (2 * count),
+        out_specs=in_vmem,
+        scratch_shapes=scratch,
         compiler_params=pltpu.CompilerParams(
             collective_id=collective_id, has_side_effects=True, vmem_limit_bytes=VMEM_BYTES
         ),
@@ -344,7 +509,7 @@
     )(*lefts, *rights)
 
 
-def total_kernel(
+def total_steps(
     member_count, group_count, part_ref, sum_ref, near, held, far, near_send, near_recv, far_send, far_recv
 ):
     group = lax.axis_index("dp")
@@ -384,29 +549,39 @@
             device_id_type=MESH,
         )
 
-    for away in range(1, member_count):
-        near_copy(away).start()
-    total = part_ref[member]
-    for away in range(1, member_count):
-        near_copy(away).wait_recv()
-        total = total + near[away]
-    held[...] = total
-    for away in range(1, group_count):
-        far_copy(away).start()
-    for away in range(1, group_count):
-        far_copy(away).wait_recv()
-        total = total + far[away]
-    sum_ref[...] = total
-    for away in range(1, member_count):
-        near_copy(away).wait_send()
-    for away in range(1, group_count):
-        far_copy(away).wait_send()
+    def near_step():
+        for away in range(1, member_count):
+            near_copy(away).start()
+
+    def far_step():
+        total = part_ref[member]
+        for away in range(1, member_count):
+            near_copy(away).wait_recv()
+            total = total + near[away]
+        held[...] = total
+        for away in range(1, group_count):
+            far_copy(away).start()
+
+    def end_step():
+        total = held[...]
+        for away in range(1, group_count):
+            far_copy(away).wait_recv()
+            total = total + far[away]
+        sum_ref[...] = total
+        for away in range(1, member_count):
+            near_copy(away).wait_send()
+        for away in range(1, group_count):
+            far_copy(away).wait_send()
+
+    near_step()
+    far_step()
+    end_step()
 
 
 def total_over_all(parts, group_count, collective_id):
     member_count, rows, lanes = parts.shape
     return pl.pallas_call(
-        functools.partial(total_kernel, member_count, group_count),
+        functools.partial(total_steps, member_count, group_count),
         out_shape=jax.ShapeDtypeStruct((rows, lanes), F32),
         in_specs=[pl.BlockSpec(memory_space=pltpu.VMEM)],
         out_specs=pl.BlockSpec(memory_space=pltpu.VMEM),
@@ -420,8 +595,206 @@
             pltpu.SemaphoreType.DMA((group_count,)),
         ],
         compiler_params=pltpu.CompilerParams(collective_id=collective_id, has_side_effects=True),
+        cost_estimate=pl.CostEstimate(flops=0, bytes_accessed=40000000, transcendentals=0),
         name="total_over_all",
     )(parts)
+
+
+def local_call(kernel, name, out_shape, *operands):
+    in_vmem = pl.BlockSpec(memory_space=pltpu.VMEM)
+    size = sum(value.size * value.dtype.itemsize for value in operands[1:])
+    size += sum(value.size * value.dtype.itemsize for value in out_shape)
+    return pl.pallas_call(
+        kernel,
+        grid_spec=pltpu.PrefetchScalarGridSpec(
+            num_scalar_prefetch=1,
+            in_specs=[in_vmem] * (len(operands) - 1),
+            out_specs=[in_vmem] * len(out_shape),
+            grid=(),
+        ),
+        out_shape=out_shape,
+        compiler_params=pltpu.CompilerParams(vmem_limit_bytes=VMEM_BYTES),
+        cost_estimate=pl.CostEstimate(flops=0, bytes_accessed=size, transcendentals=0),
+        name=name,
+    )(*operands)
+
+
+def rows_apart(member, value, member_count):
+    rows = value.shape[0] // member_count
+
+    def kernel(member_ref, value_ref, *out_refs):
+        for away, out_ref in enumerate(out_refs):
+            other = member_ref[0] ^ away
+            out_ref[...] = value_ref[pl.ds(pl.multiple_of(other * rows, rows), rows), :]
+
+    shape = jax.ShapeDtypeStruct((rows, value.shape[1]), value.dtype)
+    return local_call(kernel, "rows_apart", [shape] * member_count, member, value)
+
+
+def rows_together(member, blocks, chunks):
+    rows, width = blocks[0].shape
+    part = width // chunks
+    count = len(blocks)
+
+    def kernel(member_ref, *refs):
+        for away in range(count):
+            where = pl.ds(pl.multiple_of((member_ref[0] ^ away) * rows, rows), rows)
+            for chunk in range(chunks):
+                refs[count + chunk][where, :] = refs[away][:, chunk * part : (chunk + 1) * part]
+
+    shape = jax.ShapeDtypeStruct((count * rows, part), blocks[0].dtype)
+    return local_call(kernel, "rows_together", [shape] * chunks, member, *blocks)
+
+
+def columns_together(member, blocks):
+    rows, width = blocks[0].shape
+    count = len(blocks)
+
+    def kernel(member_ref, *refs):
+        for away in range(count):
+            where = pl.ds(pl.multiple_of((member_ref[0] ^ away) * width, width), width)
+            refs[count][:, where] = refs[away][...]
+
+    shape = jax.ShapeDtypeStruct((rows, count * width), blocks[0].dtype)
+    return local_call(kernel, "columns_together", [shape], member, *blocks)[0]
+
+
+def exchanged(blocks):
+    return [blocks[0]] + [
+        lax.ppermute(blocks[away], "fsdp", [(m, m ^ away) for m in range(len(blocks))])
+        for away in range(1, len(blocks))
+    ]
+
+
+def added(left, right):
+    return left.astype(F32) + right.astype(F32)
+
+
+def send_to(value, member_count, partner):
+    return lax.ppermute(value, "fsdp", [(m, partner(m)) for m in range(member_count)])
+
+
+def hopped(step, member_count):
+    masks = plane_masks(member_count)
+    return lambda m: (m ^ masks[step]) if m % 2 == 0 else (m ^ masks[-1 - step])
+
+
+def unit_strips(member_count, group_count, chunks, per):
+    share = group_count // chunks
+    for chunk in range(chunks):
+        for side in range(2):
+            for place in range(share):
+                group = chunk * share + place
+                yield chunk, side, (side * share + place) * per, group * member_count * per
+
+
+def units_apart(member, gate, up, gain, member_count, group_count, chunks):
+    shard, width = gate.shape
+    per = width // (member_count * group_count)
+    columns = 2 * group_count * per
+    strips = list(unit_strips(member_count, group_count, chunks, per))
+    shape = jax.ShapeDtypeStruct((shard, columns), BF16)
+    if per % 128:
+        scaled = [(value * gain).astype(BF16) for value in (gate, up)]
+
+        def block(away):
+            other = member[0] ^ away
+            return jnp.concatenate(
+                [
+                    lax.dynamic_slice_in_dim(scaled[side], base + other * per, per, 1)
+                    for chunk, side, column, base in strips
+                ],
+                axis=1,
+            )
+
+        return [block(away) for away in range(member_count)]
+
+    def kernel(member_ref, gate_ref, up_ref, gain_ref, *out_refs):
+        for away, out_ref in enumerate(out_refs):
+            other = member_ref[0] ^ away
+            for chunk, side, column, base in strips:
+                where = pl.ds(pl.multiple_of(base + other * per, per), per)
+                source = (gate_ref, up_ref)[side][:, where].astype(F32)
+                column += chunk * (columns // chunks)
+                out_ref[:, column : column + per] = (source * gain_ref[...]).astype(BF16)
+
+    return local_call(kernel, "units_apart", [shape] * member_count, member, gate, up, gain)
+
+
+def units_together(member, chunk_blocks, gain, member_count, group_count):
+    chunks = len(chunk_blocks)
+    shard, columns = chunk_blocks[0][0].shape
+    per = columns * chunks // (2 * group_count)
+    width = per * member_count * group_count
+    strips = list(unit_strips(member_count, group_count, chunks, per))
+    blocks = [block for group in chunk_blocks for block in group]
+    if per % 128:
+        results = []
+        for side in range(2):
+            result = jnp.zeros((shard, width), F32)
+            for away in range(member_count):
+                other = member[0] ^ away
+                for chunk, this, column, base in strips:
+                    if this == side:
+                        piece = chunk_blocks[chunk][away][:, column : column + per]
+                        result = lax.dynamic_update_slice_in_dim(
+                            result, piece.astype(F32) * gain, base + other * per, 1
+                        )
+            results.append(result)
+        return results
+
+    def kernel(member_ref, gain_ref, *refs):
+        outs = refs[len(blocks) :]
+        for away in range(member_count):
+            other = member_ref[0] ^ away
+            for chunk, side, column, base in strips:
+                where = pl.ds(pl.multiple_of(base + other * per, per), per)
+                piece = refs[chunk * member_count + away][:, column : column + per]
+                outs[side][:, where] = piece.astype(F32) * gain_ref[...]
+
+    shape = jax.ShapeDtypeStruct((shard, width), F32)
+    return local_call(kernel, "units_together", [shape] * 2, member, gain, *blocks)
+
+
+def heads_together(member, blocks, gain, heads):
+    count = len(blocks)
+    shard, columns = blocks[0].shape
+    width = heads * HD
+    out_width = columns - width - 2 * HD
+    copies = count // KVH
+
+    def kernel(member_ref, gain_ref, *refs):
+        ins, (query_out, key_out, value_out, out_out) = refs[:count], refs[count:]
+        row = lax.broadcasted_iota(jnp.int32, (width, width), 0)
+        column = lax.broadcasted_iota(jnp.int32, (width, width), 1)
+        source = column % HD // HALF * (HALF * heads) + column // HD * HALF + column % HALF
+        order = (row == source).astype(BF16)
+        pair_row = lax.broadcasted_iota(jnp.int32, (2 * HD, KVH * HD), 0)
+        pair_column = lax.broadcasted_iota(jnp.int32, (2 * HD, KVH * HD), 1)
+        gain_here = gain_ref[...]
+        keys = jnp.zeros((shard, KVH * HD), F32)
+        values = jnp.zeros((shard, KVH * HD), F32)
+        for away in range(count):
+            other = member_ref[0] ^ away
+            block = ins[away]
+            where = pl.ds(pl.multiple_of(other * width, width), width)
+            query_out[:, where] = dot_nn(block[:, :width], order) * gain_here
+            pair = block[:, width : width + 2 * HD]
+            first = other // copies * HD
+            keys = keys + dot_nn(pair, (pair_column == pair_row + first).astype(BF16) * (pair_row < HD).astype(BF16))
+            values = values + dot_nn(
+                pair, (pair_column == pair_row - HD + first).astype(BF16) * (pair_row >= HD).astype(BF16)
+            )
+            out_where = pl.ds(pl.multiple_of(other * out_width, out_width), out_width)
+            out_out[:, out_where] = block[:, width + 2 * HD :].astype(F32)
+        key_out[...] = keys * gain_here
+        value_out[...] = values * gain_here
+
+    shapes = [
+        jax.ShapeDtypeStruct((shard, size), F32)
+        for size in (count * width, KVH * HD, KVH * HD, count * out_width)
+    ]
+    return local_call(kernel, "heads_together", shapes, member, gain, *blocks)
 
 
 def half_group(shape, heads):
@@ -456,6 +829,16 @@
     )
 
 
+def tables(table, width):
+    half = width // 2
+    row = lax.broadcasted_iota(jnp.int32, (2 * HALF, half), 0)
+    column = lax.broadcasted_iota(jnp.int32, (2 * HALF, half), 1) % HALF
+    return (
+        exact(table, (row == column).astype(F32), ((1,), (0,))),
+        exact(table, (row == column + HALF).astype(F32), ((1,), (0,))),
+    )
+
+
 def turn(values, cosine, sine):
     half = cosine.shape[1]
     first = values[:, :half]
@@ -467,8 +850,7 @@
     heads,
     first_ref,
     projected_ref,
-    cosine_ref,
-    sine_ref,
+    table_ref,
     start_ref,
     query_ref,
     key_ref,
@@ -483,8 +865,7 @@
     step = pl.program_id(0)
     width = heads * HD
     start = start_ref[...]
-    cosine = cosine_ref[...]
-    sine = sine_ref[...]
+    cosine, sine = tables(table_ref[...], width)
     query = turn(projected_ref[:, :width], cosine, sine).astype(BF16)
     pair = projected_ref[:, width:]
     keys_here = turn(exact(pair, spread_keys(width), ((1,), (0,))), cosine, sine).astype(BF16)
@@ -531,12 +912,11 @@
     lse_ref[...] = top[...] + jnp.log(total[...])
 
 
-def attention_forward(first, projected, cosine, sine, start):
+def attention_forward(first, projected, table, start):
     tokens, columns = projected.shape
     width = columns - 2 * HD
     heads = width // HD
     by_block = pl.BlockSpec((BLOCK, width), lambda i, first: (i, 0))
-    by_half = pl.BlockSpec((BLOCK, width // 2), lambda i, first: (i, 0))
     whole = pl.BlockSpec((tokens, width), lambda i, first: (0, 0))
     return pl.pallas_call(
         functools.partial(forward_kernel, heads),
@@ -545,8 +925,7 @@
             grid=(tokens // BLOCK,),
             in_specs=[
                 pl.BlockSpec((BLOCK, columns), lambda i, first: (i, 0)),
-                by_half,
-                by_half,
+                pl.BlockSpec((BLOCK, 2 * HALF), lambda i, first: (i, 0)),
                 pl.BlockSpec((1, BLOCK), lambda i, first: (0, i)),
             ],
             out_specs=[
@@ -570,7 +949,7 @@
             flops=64 * tokens * BLOCK * width, bytes_accessed=8 * tokens * width, transcendentals=0
         ),
         name="attention_forward",
-    )(first, projected, cosine, sine, start)
+    )(first, projected, table, start)
 
 
 def backward_kernel(
@@ -583,8 +962,7 @@
     grad_ref,
     lse_ref,
     start_ref,
-    cosine_ref,
-    sine_ref,
+    table_ref,
     out_ref,
     dquery,
     dkey,
@@ -643,15 +1021,15 @@
 
     lax.fori_loop(first_ref[step], step + 1, one_block, 0)
     own_rows = pl.ds(pl.multiple_of(step * BLOCK, BLOCK), BLOCK)
-    out_ref[own_rows, :width] = (
-        turn(dquery[...], cosine_ref[own_rows, :], -sine_ref[own_rows, :]) * ATTENTION_SCALE
-    ).astype(BF16)
+    cosine, sine = tables(table_ref[own_rows, :], width)
+    out_ref[own_rows, :width] = (turn(dquery[...], cosine, -sine) * ATTENTION_SCALE).astype(BF16)
 
     @pl.when(step == pl.num_programs(0) - 1)
     def _():
         def fold(block, carried):
             rows = pl.ds(pl.multiple_of(block * BLOCK, BLOCK), BLOCK)
-            turned = turn(dkey[rows, :], cosine_ref[rows, :], -sine_ref[rows, :]) * ATTENTION_SCALE
+            cosine, sine = tables(table_ref[rows, :], width)
+            turned = turn(dkey[rows, :], cosine, -sine) * ATTENTION_SCALE
             out_ref[rows, width:] = (
                 exact(turned, spread_keys(width), ((1,), (1,)))
                 + exact(dvalue[rows, :], spread_values(width), ((1,), (1,)))
@@ -661,13 +1039,12 @@
         lax.fori_loop(0, pl.num_programs(0), fold, 0)
 
 
-def attention_backward(first, query, keys, values, mixed, grad, lse, start, cosine, sine):
+def attention_backward(first, query, keys, values, mixed, grad, lse, start, table):
     tokens, width = query.shape
     heads = width // HD
     columns = width + 2 * HD
     by_block = pl.BlockSpec((BLOCK, width), lambda i, first: (i, 0))
     whole = pl.BlockSpec((tokens, width), lambda i, first: (0, 0))
-    whole_half = pl.BlockSpec((tokens, width // 2), lambda i, first: (0, 0))
     return pl.pallas_call(
         functools.partial(backward_kernel, heads),
         grid_spec=pltpu.PrefetchScalarGridSpec(
@@ -681,8 +1058,7 @@
                 by_block,
                 pl.BlockSpec((heads, BLOCK), lambda i, first: (0, i)),
                 pl.BlockSpec((1, BLOCK), lambda i, first: (0, i)),
-                whole_half,
-                whole_half,
+                pl.BlockSpec((tokens, 2 * HALF), lambda i, first: (0, 0)),
             ],
             out_specs=pl.BlockSpec((tokens, columns), lambda i, first: (0, 0)),
             scratch_shapes=[
@@ -699,7 +1075,7 @@
             transcendentals=0,
         ),
         name="attention_backward",
-    )(first, query, keys, values, mixed, grad, lse, start, cosine, sine)
+    )(first, query, keys, values, mixed, grad, lse, start, table)
 
 
 def token_starts(lengths_row, group_tokens):
@@ -725,35 +1101,6 @@
 
 def gather_groups(value):
     return lax.all_gather(value, "dp", axis=0, tiled=True)
-
-
-def send_to(value, member_count, partner):
-    return lax.ppermute(value, "fsdp", [(m, partner(m)) for m in range(member_count)])
-
-
-def permuted_swap(value):
-    member_count = value.shape[0]
-    member = lax.axis_index("fsdp")
-    return [value] + [
-        send_to(
-            lax.dynamic_slice_in_dim(value, member ^ away, 1, 0),
-            member_count,
-            lambda m, away=away: m ^ away,
-        )
-        for away in range(1, member_count)
-    ]
-
-
-def joined(pieces):
-    member = lax.axis_index("fsdp")
-    result = pieces[0]
-    for away in range(1, len(pieces)):
-        result = lax.dynamic_update_slice_in_dim(result, pieces[away], member ^ away, 0)
-    return result
-
-
-def swap_members(value):
-    return lax.all_to_all(value, "fsdp", split_axis=0, concat_axis=0, tiled=True)
 
 
 def body(
@@ -781,15 +1128,15 @@
     copies = members // KVH
     out_columns = model // members
     down_rows = down_weight.shape[0]
-    chunk_rows = down_rows // CHUNKS
-    units = groups * chunk_rows
+    units = groups * down_rows // CHUNKS
     gain_one = attention_gain.astype(F32)[:, None]
     gain_two = feedforward_gain.astype(F32)[:, None]
+    member = lax.axis_index("fsdp").astype(jnp.int32)[None]
 
     scaled_query = (query_weight * gain_one).astype(BF16)
     scaled_key = (key_weight * gain_one).astype(BF16)
     scaled_value = (value_weight * gain_one).astype(BF16)
-    packed = jnp.concatenate(
+    packed_in = jnp.concatenate(
         [
             scaled_query.reshape(shard, members, heads, 2, HALF)
             .transpose(1, 0, 3, 2, 4)
@@ -800,71 +1147,69 @@
             jnp.repeat(
                 scaled_value.reshape(shard, KVH, HD).transpose(1, 0, 2), copies, axis=0
             ),
-            output_weight.reshape(shard, members, out_columns).transpose(1, 0, 2),
         ],
         axis=2,
     )
-    packed = swap_members(packed).reshape(members * shard, columns + out_columns)
+    packed_in, packed_out = plane_swap(
+        [packed_in, output_weight.reshape(shard, members, out_columns).transpose(1, 0, 2)],
+        members,
+        1,
+    )
+    packed_in = packed_in.reshape(members * shard, columns)
+    packed_out = packed_out.reshape(members * shard, out_columns)
     inputs = tokens.astype(F32)
     inverse_one = inverse_norm(inputs)
-    normed_one = plane_gather(after((inputs * inverse_one).astype(BF16), packed), members, 0, True)
-    packed = after(gather_groups(packed), normed_one)
+    normed_one = plane_gather(after((inputs * inverse_one).astype(BF16), packed_in), members, 0, True)
+    projection = gather_groups(packed_in)
+    out_columns_piece = gather_groups(packed_out)
     upstream = cotangent.astype(F32)
-    down_chunks = []
-    for chunk in range(CHUNKS):
-        part = down_weight[chunk * chunk_rows : (chunk + 1) * chunk_rows]
-        down_chunks.append(gather_groups(after(part, normed_one)))
-    gate_up = jnp.stack(
-        [
-            (weight * gain_two)
-            .astype(BF16)
-            .reshape(shard, groups, members, CHUNKS, chunk_rows)
-            .transpose(2, 0, 3, 1, 4)
-            for weight in (gate_weight, up_weight)
-        ],
-        axis=3,
-    ).reshape(members, shard, CHUNKS * 2 * units)
-    gate_up = permuted_swap(after(gate_up, normed_one))
+    down_all = gather_groups(after(down_weight, normed_one))
+    gate_up = exchanged(
+        units_apart(
+            member,
+            after(gate_weight, normed_one),
+            up_weight,
+            gain_two,
+            members,
+            groups,
+            CHUNKS,
+        )
+    )
 
     start, place = token_starts(lengths[0], group_tokens)
     first = start[::BLOCK] // BLOCK
     frequency = ROPE_BASE ** (-(2.0 * jnp.arange(HALF, dtype=F32)) / HD)
     angles = (place - start).astype(F32)[:, None] * frequency[None, :]
-    cosine = jnp.tile(jnp.cos(angles), (1, heads))
-    sine = jnp.tile(jnp.sin(angles), (1, heads))
+    table = jnp.concatenate([jnp.cos(angles), jnp.sin(angles)], axis=1)
     start = start[None, :]
 
-    projection = packed[:, :columns]
-    out_piece = lax.all_to_all(
-        packed[:, columns:], "fsdp", split_axis=0, concat_axis=1, tiled=True
-    )
     projected = dot_nn(normed_one, projection)
-    query, keys, values, mixed, lse = attention_forward(first, projected, cosine, sine, start)
-    mixed_then, down_chunks[0], *gate_up = lax.optimization_barrier(
-        (mixed, down_chunks[0], *gate_up)
-    )
-    gate_up = joined(gate_up).reshape(members * shard, CHUNKS * 2 * units)
+    out_blocks = exchanged(
+        rows_apart(member, after(out_columns_piece, projected), members)
+    )
+    query, keys, values, mixed, lse = attention_forward(first, projected, table, start)
+    mixed_then, out_blocks, gate_up = lax.optimization_barrier((mixed, out_blocks, gate_up))
     gate_up_chunks = [
-        gather_groups(gate_up[:, chunk * 2 * units : (chunk + 1) * 2 * units])
-        for chunk in range(CHUNKS)
+        gather_groups(part) for part in rows_together(member, gate_up, CHUNKS)
     ]
-    branch_one = product_scatter(
-        [after(mixed_then, gate_up)], [out_piece], False, members, 2, True
-    )
+    out_piece = columns_together(member, out_blocks)
+    branch_one = product_scatter([mixed_then], [out_piece], False, members, 2, True)
     residual = inputs + RESIDUAL_SCALE * branch_one
 
     inverse_two = inverse_norm(residual)
-    normed_two = plane_gather((residual * inverse_two).astype(BF16), members, 3, False)
+    normed_two, down_all = lax.optimization_barrier(
+        ((residual * inverse_two).astype(BF16), down_all)
+    )
+    normed_two = plane_gather(normed_two, members, 3, False)
     grad_two = plane_gather(
-        after((RESIDUAL_SCALE * upstream).astype(BF16), normed_two), members, 1, False
+        after((RESIDUAL_SCALE * upstream).astype(BF16), normed_two), members, 9, False
     )
     hiddens = []
     grad_boths = []
-    down_grads = []
     gate_up_grads = []
     for chunk in range(CHUNKS):
         both_weight = gate_up_chunks[chunk]
-        down_piece = down_chunks[chunk]
+        down_piece = down_all[chunk * units : (chunk + 1) * units]
         both = dot_nn(normed_two, both_weight)
         gate = both[:, :units]
         up = both[:, units:]
@@ -879,9 +1224,7 @@
             axis=1,
         )
         gate_up_grad = dot_tn(normed_two, grad_both).astype(BF16)
-        down_grad = dot_tn(hidden, grad_two).astype(BF16)
         gate_up_grads.append(sum_over_groups(gate_up_grad))
-        down_grads.append(sum_over_groups(down_grad))
         normed_two, grad_two, hidden, grad_both, _ = lax.optimization_barrier(
             (normed_two, grad_two, hidden, grad_both, gate_up_grad)
         )
@@ -898,20 +1241,45 @@
     grad_one, gate_up_grads[0] = lax.optimization_barrier(
         ((RESIDUAL_SCALE * grad_residual).astype(BF16), gate_up_grads[0])
     )
-    grad_one = plane_gather(grad_one, members, 5, True)
+    grad_one, down_grad, out_sibling, out_own = plane_gather(
+        grad_one, members, 5, True, (hiddens, grad_two, down_all)
+    )
+    down_grad = sum_over_groups(down_grad)
+    half_rows = group_tokens // 2
+    out_sibling = send_to(out_sibling, members, lambda m: m ^ 1)
     grad_mixed = dot_nt(grad_one, out_piece).astype(BF16)
     out_grad = dot_tn(mixed, grad_one).astype(BF16)
     out_grad = lax.all_to_all(out_grad, "fsdp", split_axis=1, concat_axis=0, tiled=True)
-    grad_mixed, gate_up_grads[-1] = lax.optimization_barrier((grad_mixed, gate_up_grads[-1]))
+    grad_mixed, gate_up_grads[-1], out_own, out_sibling = lax.optimization_barrier(
+        (grad_mixed, gate_up_grads[-1], out_own, out_sibling)
+    )
+    steps = len(plane_masks(members))
+    half_rows //= 2
+    out_sent = send_to(
+        added(out_own[half_rows:], out_sibling[half_rows:]).astype(BF16),
+        members,
+        hopped(steps - 1, members),
+    )
+    out_kept = added(out_own[:half_rows], out_sibling[:half_rows]).astype(BF16)
+    gate_up_grads = [exchanged(rows_apart(member, part, members)) for part in gate_up_grads]
     grad_projected = attention_backward(
-        first, query, keys, values, mixed, grad_mixed, lse, start, cosine, sine
+        first, query, keys, values, mixed, grad_mixed, lse, start, table
     )
     packed_grad = jnp.concatenate(
         [dot_tn(normed_one, grad_projected).astype(BF16), out_grad], axis=1
     )
-    grad_projected, packed_grad, down_grads[0] = lax.optimization_barrier(
-        (grad_projected, packed_grad, down_grads[0])
-    )
+    grad_projected, packed_grad, gate_up_grads, out_sent, out_kept, down_grad = (
+        lax.optimization_barrier(
+            (grad_projected, packed_grad, gate_up_grads, out_sent, out_kept, down_grad)
+        )
+    )
+    for step in reversed(range(steps - 1)):
+        half_rows //= 2
+        out_next = added(out_kept[half_rows:], out_sent[half_rows:]).astype(BF16)
+        out_kept = added(out_kept[:half_rows], out_sent[:half_rows])
+        if step:
+            out_kept = out_kept.astype(BF16)
+        out_sent = send_to(out_next, members, hopped(step, members))
     packed_grad = sum_over_groups(packed_grad)
     weighted_one = product_scatter([grad_projected], [projection], True, members, 6, True)
     grad_inputs = (
@@ -920,11 +1288,6 @@
         - inputs * inverse_one**3 * jnp.mean(weighted_one * inputs, axis=1, keepdims=True)
     )
     gain_term_one = jnp.sum(weighted_one * inputs * inverse_one, axis=0)
-
-    hiddens[-1] = after(hiddens[-1], weighted_one)
-    branch_two = product_scatter(hiddens, down_chunks, False, members, 7, False)
-    branch_two, down_grads[-1] = lax.optimization_barrier((branch_two, down_grads[-1]))
-    output = residual + RESIDUAL_SCALE * branch_two
 
     gains = jnp.stack(
         [
@@ -936,46 +1299,28 @@
     gains = jnp.pad(
         gains.transpose(1, 0, 2), ((0, 0), (0, (-groups) % 8), (0, (-2 * shard) % 128))
     )
-    gains = total_over_all(after(gains, branch_two), groups, 8)
+    gains = total_over_all(gains, groups, 8)
+    out_sent, out_kept, _ = lax.optimization_barrier((out_sent, out_kept, gains))
+    output = residual + RESIDUAL_SCALE * added(out_kept, out_sent)
+
     gains = lax.dynamic_slice_in_dim(gains, lax.axis_index("dp"), 1, 0)[0, : 2 * shard]
     gains = gains.reshape(2, shard)
-
-    gate_up_grads = [
-        swap_members(after(part.reshape(members, shard, 2 * units), branch_two))
-        .reshape(members, shard, 2, groups, chunk_rows)
-        for part in gate_up_grads
-    ]
-    both_grad = [
-        jnp.stack([part[:, :, side] for part in gate_up_grads], axis=3)
-        .transpose(1, 2, 0, 3, 4)
-        .reshape(shard, -1)
-        .astype(F32)
-        * gain_two
-        for side in range(2)
-    ]
-    packed_grad = swap_members(packed_grad.reshape(members, shard, -1)).astype(F32)
-    grad_query = (
-        packed_grad[:, :, :width]
-        .reshape(members, shard, 2, heads, HALF)
-        .transpose(1, 0, 3, 2, 4)
-        .reshape(shard, -1)
-    )
-
-    def folded(part):
-        return (
-            part.reshape(KVH, copies, shard, HD).sum(axis=1).transpose(1, 0, 2).reshape(shard, -1)
-        )
-
+    gate_grad, up_grad = units_together(
+        member, after(gate_up_grads, gains), gain_two, members, groups
+    )
+    query_grad, key_grad, value_grad, out_grad = heads_together(
+        member, exchanged(rows_apart(member, packed_grad, members)), gain_one, heads
+    )
     return (
         output.astype(BF16),
         grad_inputs.astype(BF16),
-        grad_query * gain_one,
-        folded(packed_grad[:, :, width : width + HD]) * gain_one,
-        folded(packed_grad[:, :, width + HD : columns]) * gain_one,
-        packed_grad[:, :, columns:].transpose(1, 0, 2).reshape(shard, -1),
-        both_grad[0],
-        both_grad[1],
-        jnp.concatenate(down_grads, axis=0).astype(F32),
+        query_grad,
+        key_grad,
+        value_grad,
+        out_grad,
+        gate_grad,
+        up_grad,
+        down_grad.astype(F32),
         gains[0] / gain_one[:, 0],
         gains[1] / gain_two[:, 0],
     )

time: 776 us -> 711 us (0.916)
  local copies, waits for them, and re-layouts: 61.9 us -> 13.8 us
  matrix products: 131 us -> 106 us
  blocking collectives: 16.4 us -> 0 us
  starting transfers between devices: 26.5 us -> 38.4 us
    pallas_call x4 -> x3, Pallas kernels: 189 us -> 143 us  [product_scatter(): pl.pallas_call(functools.partial(product_scatter_kernel, member_count, in...]
    pallas_call x5 -> x15, Pallas kernels: 170 us -> 214 us  [the longest x4 164 us: plane_gather(): pl.pallas_call(functools.partial(gather_kernel, member_count, in_order, c...]
    ppermute x0 -> x35, starting transfers between devices: none -> 31 us  [exchanged(): lax.ppermute(blocks[away], 'fsdp', [(m, m ^ away) for m in range(len(bloc...]
    all_to_all x4 -> x0, waiting for transfers between devices: 29.9 us -> none  [the longest x3 15.8 us: swap_members(): lax.all_to_all(value, 'fsdp', split_axis=0, concat_axis=0, tiled=True)]
    dot_general x6 -> x4, matrix products: 59.6 us -> 39.2 us  [dot_tn(): lax.dot_general(left, right, (((0,), (0,)), ((), ())), preferred_element_...]
    all_gather x5, waiting for transfers between devices: 2.29 us -> 22 us  [gather_groups(): return lax.all_gather(value, 'dp', axis=0, tiled=True)]
    all_to_all x1 -> x0, blocking collectives: 16.4 us -> none  [swap_members(): lax.all_to_all(value, 'fsdp', split_axis=0, concat_axis=0, tiled=True)]
    all_to_all x4 -> x0, starting transfers between devices: 16.2 us -> none  [the longest x3 12.4 us: swap_members(): lax.all_to_all(value, 'fsdp', split_axis=0, concat_axis=0, tiled=True)]
  transfers between devices with their start and end apart: 22 -> 48, of which waited for: 4 -> 6; matrix products, arithmetic and copies ran while one was open for 28% -> 23% of each run, Pallas kernels for 57% -> 60%
where the time goes in v3:
time: 711 us; the launch traced here: 701 us
  Pallas kernels  440 us (62%)
  matrix products  106 us (15%)
  other arithmetic  53.8 us (8%)
  starting transfers between devices  38.4 us (5%)
  waiting for transfers between devices  35.5 us (5%)
  between operations  14.8 us (2%)
  local copies, waits for them, and re-layouts  13.8 us (2%)
    pallas_call x4, Pallas kernels, plane_gather(): pl.pallas_call(functools.partial(gather_kernel, member_count, in_order, c...  164 us
    pallas_call x3, Pallas kernels, product_scatter(): pl.pallas_call(functools.partial(product_scatter_kernel, member_count, in...  143 us
    pallas_call x1, Pallas kernels, attention_backward(): pl.pallas_call(functools.partial(backward_kernel, heads), grid_spec=pltpu...  48.1 us
    dot_general x4, matrix products, dot_tn(): lax.dot_general(left, right, (((0,), (0,)), ((), ())), preferred_element_...  39.2 us
    dot_general x3, matrix products, dot_nn(): return jnp.dot(left, right, preferred_element_type=F32)  37.3 us
    pallas_call x1, Pallas kernels, attention_forward(): pl.pallas_call(functools.partial(forward_kernel, heads), grid_spec=pltpu....  34.9 us
    ppermute x35, starting transfers between devices, exchanged(): lax.ppermute(blocks[away], 'fsdp', [(m, m ^ away) for m in range(len(bloc...  31 us
    dot_general x3, matrix products, dot_nt(): lax.dot_general(left, right, (((1,), (1,)), ((), ())), preferred_element_...  29 us
  transfers between devices with their start and end apart: 48, of which 6 were waited for; matrix products, arithmetic and copies ran while one was open for 23% of the time, Pallas kernels for 60%

profile of v3, /device:TPU:0, one launch (start us, length us, event | category | flops | bytes accessed | tf_op | source)
XLA Modules:
  0.0 701.5 jit_solution(13712684450931491352)
XLA Ops:
  13.9 12.8 %plane_swap.1 = (bf16[8,64,384]{2,1,0:T(8,128)(2,1)}, bf16[8,64,256]{2,1,0:T(8,128)(2,1)}) custom-call(bf16[8,64,384]{2,1,0:T(8,128)(2,1)} %pad_maximum_fusion.4.refs_0_, bf16[8,64,256]{2,1,0:T(8,128)(2,1)} %bitcast.59), custom_call_target="tpu_custom_call" | custom-call | bytes 19660800 | tf_op jit(solution)/shard_map/plane_swap/pallas_call | solution.py:307
  29.6 39.7 %plane_gather.4 = bf16[2048,2048]{1,0:T(8,128)(2,1)} custom-call(bf16[256,2048]{1,0:T(8,128)(2,1)} %fusion.3.own_ref), custom_call_target="tpu_custom_call" | custom-call | bytes 251658240 | tf_op jit(solution)/shard_map/plane_gather/pallas_call | solution.py:246
  85.2 10.1 %fusion.13.projected_ref = f32[2048,384]{1,0:T(8,128)} fusion(bf16[2048,2048]{1,0:T(8,128)(2,1)} %plane_gather.4, bf16[2048,384]{1,0:T(8,128)(2,1)} %all-gather.6.cloned.1.call-done.refs_1_), kind=kOutput, calls=%fused_computation.79 | convolution fusion | flops 3221225472 | bytes 13107200 | tf_op jit(solution)/shard_map/dot_general | solution.py:30
  105.9 34.9 %attention_forward.1 = (bf16[2048,256]{1,0:T(8,128)(2,1)}, bf16[2048,256]{1,0:T(8,128)(2,1)}, bf16[2048,256]{1,0:T(8,128)(2,1)}, bf16[2048,256]{1,0:T(8,128)(2,1)}, f32[4,2048]{1,0:T(4,128)}) custom-call(s32[8]{0:T(128)} %and_select_fusion.first_ref, f32[2048,384]{1,0:T(8,128)} %fusion.13.projected_ref, f32[2048,64]{1,0:T(8,128)} %pad_maximum_fusion.3.table_ref, ...), custom_call_target="tpu_custom_call" | custom-call | flops 8589934592 | bytes 4194304 | tf_op jit(solution)/shard_map/attention_forward/pallas_call | solution.py:921
  148.2 43.2 %product_scatter.3 = f32[256,2048]{1,0:T(8,128)} custom-call(bf16[2048,256]{1,0:T(8,128)(2,1)} %get-tuple-element.168.refs_0_.mixed_ref, bf16[256,2048]{1,0:T(8,128)(2,1)} %columns_together.1.refs_1_), custom_call_target="tpu_custom_call" | custom-call | flops 2147483648 | bytes 251658240 | tf_op jit(solution)/shard_map/product_scatter/pallas_call | solution.py:496
  194.7 38.9 %plane_gather.5 = bf16[2048,2048]{1,0:T(8,128)(2,1)} custom-call(bf16[256,2048]{1,0:T(8,128)(2,1)} %multiply_convert_fusion.7.own_ref), custom_call_target="tpu_custom_call" | custom-call | bytes 251658240 | tf_op jit(solution)/shard_map/plane_gather/pallas_call | solution.py:246
  233.5 39.1 %plane_gather.6.refs_2_ = bf16[2048,2048]{1,0:T(8,128)(2,1)} custom-call(bf16[256,2048]{1,0:T(8,128)(2,1)} %fusion.own_ref), custom_call_target="tpu_custom_call" | custom-call | bytes 251658240 | tf_op jit(solution)/shard_map/plane_gather/pallas_call | solution.py:246
  272.6 14.5 %fusion.14 = f32[2048,1024]{1,0:T(8,128)} fusion(bf16[2048,2048]{1,0:T(8,128)(2,1)} %plane_gather.5, bf16[2048,1024]{1,0:T(8,128)(2,1)} %all-gather.12.cloned.1.call-done.refs_2_), kind=kOutput, calls=%fused_computation.80 | convolution fusion | flops 8589934592 | bytes 20971520 | tf_op jit(solution)/shard_map/dot_general | solution.py:30
  287.2 10.8 %multiply_convert_fusion.4 = (bf16[2048,512]{1,0:T(8,128)(2,1)S(1)}, bf16[2048,512]{1,0:T(8,128)(2,1)}, bf16[2048,512]{1,0:T(8,128)(2,1)}) fusion(f32[2048,1024]{1,0:T(8,128)} %fusion.14, bf16[2048,2048]{1,0:T(8,128)(2,1)S(1)} %copy-done, bf16[1024,2048]{1,0:T(8,128)(2,1)} %all-gather.10.cloned.1.call-done.refs_3_), kind=kOutput, calls=%fused_computation.9 | convolution fusion | flops 4311744512 | bytes 25165824 | tf_op jit(solution)/shard_map/dot_general | solution.py:34
  299.3 11.2 %convolution_convert_fusion.1 = bf16[2048,1024]{1,0:T(8,128)(2,1)} fusion(bf16[2048,2048]{1,0:T(8,128)(2,1)S(1)} %copy-done.5, bf16[2048,512]{1,0:T(8,128)(2,1)} %get-tuple-element.292, bf16[2048,512]{1,0:T(8,128)(2,1)S(1)} %get-tuple-element.291), kind=kOutput, calls=%fused_computation.18 | convolution fusion | flops 8600420352 | bytes 16777216 | tf_op jit(solution)/shard_map/dot_general | solution.py:38
  315.5 22.0 %all-gather.14.cloned.1.call-done.refs_3_ = bf16[2048,1024]{1,0:T(8,128)(2,1)} async-done(((bf16[512,1024]{1,0:T(8,128)(2,1)}), bf16[2048,1024]{1,0:T(8,128)(2,1)}) %all-gather.14.cloned.1.call-update) | async-done | bytes 4194320 | tf_op jit(solution)/shard_map/all_gather | solution.py:1103
  337.5 12.6 %fusion.15 = f32[2048,1024]{1,0:T(8,128)S(1)} fusion(bf16[2048,2048]{1,0:T(8,128)(2,1)} %plane_gather.5, bf16[2048,1024]{1,0:T(8,128)(2,1)} %all-gather.14.cloned.1.call-done.refs_3_), kind=kOutput, calls=%fused_computation.81 | convolution fusion | flops 8589934592 | bytes 20971520 | tf_op jit(solution)/shard_map/dot_general | solution.py:30
  350.1 11.1 %multiply_convert_fusion.1 = (bf16[2048,512]{1,0:T(8,128)(2,1)S(1)}, bf16[2048,512]{1,0:T(8,128)(2,1)S(1)}, bf16[2048,512]{1,0:T(8,128)(2,1)}) fusion(f32[2048,1024]{1,0:T(8,128)S(1)} %fusion.15, bf16[2048,2048]{1,0:T(8,128)(2,1)} %plane_gather.6.refs_2_, bf16[1024,2048]{1,0:T(8,128)(2,1)S(1)} %copy-done.8), kind=kOutput, calls=%fused_computation.5 | convolution fusion | flops 4311744512 | bytes 25165824 | tf_op jit(solution)/shard_map/dot_general | solution.py:34
  363.2 12.7 %convolution_convert_fusion = bf16[2048,1024]{1,0:T(8,128)(2,1)} fusion(bf16[2048,2048]{1,0:T(8,128)(2,1)} %plane_gather.5, bf16[2048,512]{1,0:T(8,128)(2,1)S(1)} %get-tuple-element.290, bf16[2048,512]{1,0:T(8,128)(2,1)S(1)} %get-tuple-element.289), kind=kOutput, calls=%fused_computation.17 | convolution fusion | flops 8600420352 | bytes 16777216 | tf_op jit(solution)/shard_map/dot_general | solution.py:38
  376.0 4.8 pad_maximum_fusion.1.refs_1_
  380.8 55.3 %product_scatter.4 = f32[256,2048]{1,0:T(8,128)} custom-call(bf16[2048,1024]{1,0:T(8,128)(2,1)} %pad_maximum_fusion.refs_0_, bf16[2048,1024]{1,0:T(8,128)(2,1)} %pad_maximum_fusion.1.refs_1_, bf16[2048,1024]{1,0:T(8,128)(2,1)} %all-gather.12.cloned.1.call-done.refs_2_, bf16[2048,1024]{1,0:T(8,128)(2,1)} %all-gather.14.cloned.1.call-done.refs_3_), custom_call_target="tpu_custom_call" | custom-call | flops 17179869184 | bytes 251658240 | tf_op jit(solution)/shard_map/product_scatter/pallas_call | solution.py:496
  441.1 46.7 %plane_gather.7 = (bf16[2048,2048]{1,0:T(8,128)(2,1)}, bf16[1024,2048]{1,0:T(8,128)(2,1)}, bf16[1024,2048]{1,0:T(8,128)(2,1)}, bf16[1024,2048]{1,0:T(8,128)(2,1)}) custom-call(bf16[256,2048]{1,0:T(8,128)(2,1)} %get-tuple-element.198.own_ref, bf16[2048,512]{1,0:T(8,128)(2,1)} %get-tuple-element.199.refs_0_, bf16[2048,512]{1,0:T(8,128)(2,1)} %get-tuple-element.200.refs_1_, ...), custom_call_target="tpu_custom_call" | custom-call | bytes 251658240 | tf_op jit(solution)/shard_map/plane_gather/pallas_call | solution.py:246
  493.1 5.8 convolution_convert_fusion.3
  503.8 7.1 %convolution_convert_fusion.4.grad_ref = bf16[2048,256]{1,0:T(8,128)(2,1)} fusion(bf16[2048,2048]{1,0:T(8,128)(2,1)} %get-tuple-element.202, bf16[256,2048]{1,0:T(8,128)(2,1)} %columns_together.1.refs_1_), kind=kOutput, calls=%fused_computation.24 | convolution fusion | flops 2148007936 | bytes 10485760 | tf_op jit(solution)/shard_map/dot_general | solution.py:34
  512.6 5.7 add_convert_fusion
  521.3 48.1 %attention_backward.1.refs_0_ = bf16[2048,384]{1,0:T(8,128)(2,1)} custom-call(s32[8]{0:T(128)} %and_select_fusion.first_ref, bf16[2048,256]{1,0:T(8,128)(2,1)} %get-tuple-element.177.query_ref, bf16[2048,256]{1,0:T(8,128)(2,1)} %get-tuple-element.178.key_ref, bf16[2048,256]{1,0:T(8,128)(2,1)} %get-tuple-element.179.value_ref, ...), custom_call_target="tpu_custom_call" | custom-call | flops 21474836480 | bytes 12582912 | tf_op jit(solution)/shard_map/attention_backward/pallas_call | solution.py:1048
  574.4 9.5 %convolution_convert_fusion.2 = bf16[2048,384]{1,0:T(8,128)(2,1)} fusion(bf16[2048,2048]{1,0:T(8,128)(2,1)} %plane_gather.4, bf16[2048,384]{1,0:T(8,128)(2,1)} %attention_backward.1.refs_0_), kind=kOutput, calls=%fused_computation.19 | convolution fusion | flops 3222011904 | bytes 11534336 | tf_op jit(solution)/shard_map/dot_general | solution.py:38
  599.5 44.2 %product_scatter.5 = f32[256,2048]{1,0:T(8,128)} custom-call(bf16[2048,384]{1,0:T(8,128)(2,1)} %attention_backward.1.refs_0_, bf16[2048,384]{1,0:T(8,128)(2,1)} %all-gather.6.cloned.1.call-done.refs_1_), custom_call_target="tpu_custom_call" | custom-call | flops 3221225472 | bytes 251658240 | tf_op jit(solution)/shard_map/product_scatter/pallas_call | solution.py:496
  647.8 11.8 %total_over_all.1 = f32[8,128]{1,0:T(8,128)} custom-call(f32[8,8,128]{2,1,0:T(8,128)} %pad.4.part_ref), custom_call_target="tpu_custom_call" | custom-call | bytes 40000000 | tf_op jit(solution)/shard_map/total_over_all/pallas_call | solution.py:583
  (280 shorter events, 134.0 us)
Async XLA Ops:
  7.2 78.0 %all-gather.6.cloned.1.call-start = ((), (), s32[]{:S(2)}) async-start(), calls=%async_computation.5 | async-start | bytes 1966080 | tf_op jit(solution)/shard_map/all_gather | solution.py:1103
  26.7 68.6 %all-gather.8.cloned.1.call-start = ((), (), s32[]{:S(2)}) async-start(), calls=%async_computation.6 | async-start | bytes 1310720 | tf_op jit(solution)/shard_map/all_gather | solution.py:1103
  27.4 167.2 %all-gather.10.cloned.1.call-start = ((), (), s32[]{:S(2)}) async-start(), calls=%async_computation.7 | async-start | bytes 5242880 | tf_op jit(solution)/shard_map/all_gather | solution.py:1103
  69.4 203.2 %all-gather.12.cloned.1.call-start = ((), (), s32[]{:S(2)}) async-start(), calls=%async_computation.8 | async-start | bytes 5242880 | tf_op jit(solution)/shard_map/all_gather | solution.py:1103
  74.5 23.1 %collective-permute-start.9 = (bf16[64,2048]{1,0:T(8,128)(2,1)}, bf16[64,2048]{1,0:T(8,128)(2,1)}, u32[]{:S(2)}, u32[]{:S(2)}) collective-permute-start(bf16[64,2048]{1,0:T(8,128)(2,1)} %get-tuple-element.163), channel_id=1, source_target_pairs={{0,3},{1,2},{2,1},{3,0},{4,7},{5,6},{6,5},{7,4},{8,11},{9,10},{10,... | collective-permute-start | bytes 786440 | tf_op jit(solution)/shard_map/ppermute | solution.py:664
  76.0 25.1 %collective-permute-start.11 = (bf16[64,2048]{1,0:T(8,128)(2,1)}, bf16[64,2048]{1,0:T(8,128)(2,1)}, u32[]{:S(2)}, u32[]{:S(2)}) collective-permute-start(bf16[64,2048]{1,0:T(8,128)(2,1)} %get-tuple-element.165), channel_id=1, source_target_pairs={{0,5},{1,4},{2,7},{3,6},{4,1},{5,0},{6,3},{7,2},{8,13},{9,12},{10,... | collective-permute-start | bytes 786440 | tf_op jit(solution)/shard_map/ppermute | solution.py:664
  101.1 39.8 %collective-permute-start.2 = (bf16[256,256]{1,0:T(8,128)(2,1)}, bf16[256,256]{1,0:T(8,128)(2,1)S(1)}, u32[]{:S(2)}, u32[]{:S(2)}) collective-permute-start(bf16[256,256]{1,0:T(8,128)(2,1)} %get-tuple-element.154), channel_id=1, source_target_pairs={{0,3},{1,2},{2,1},{3,0},{4,7},{5,6},{6,5},{7,4},{8,11},{9,10},{10,... | collective-permute-start | bytes 393224 | tf_op jit(solution)/shard_map/ppermute | solution.py:664
  101.5 39.4 %collective-permute-start.3 = (bf16[256,256]{1,0:T(8,128)(2,1)}, bf16[256,256]{1,0:T(8,128)(2,1)S(1)}, u32[]{:S(2)}, u32[]{:S(2)}) collective-permute-start(bf16[256,256]{1,0:T(8,128)(2,1)} %get-tuple-element.155), channel_id=1, source_target_pairs={{0,4},{1,5},{2,6},{3,7},{4,0},{5,1},{6,2},{7,3},{8,12},{9,13},{10,... | collective-permute-start | bytes 393224 | tf_op jit(solution)/shard_map/ppermute | solution.py:664
  102.9 38.0 %collective-permute-start.4 = (bf16[256,256]{1,0:T(8,128)(2,1)}, bf16[256,256]{1,0:T(8,128)(2,1)S(1)}, u32[]{:S(2)}, u32[]{:S(2)}) collective-permute-start(bf16[256,256]{1,0:T(8,128)(2,1)} %get-tuple-element.156), channel_id=1, source_target_pairs={{0,5},{1,4},{2,7},{3,6},{4,1},{5,0},{6,3},{7,2},{8,13},{9,12},{10,... | collective-permute-start | bytes 393224 | tf_op jit(solution)/shard_map/ppermute | solution.py:664
  103.2 37.7 %collective-permute-start.5 = (bf16[256,256]{1,0:T(8,128)(2,1)}, bf16[256,256]{1,0:T(8,128)(2,1)S(1)}, u32[]{:S(2)}, u32[]{:S(2)}) collective-permute-start(bf16[256,256]{1,0:T(8,128)(2,1)} %get-tuple-element.157), channel_id=1, source_target_pairs={{0,6},{1,7},{2,4},{3,5},{4,2},{5,3},{6,0},{7,1},{8,14},{9,15},{10,... | collective-permute-start | bytes 393224 | tf_op jit(solution)/shard_map/ppermute | solution.py:664
  104.6 36.4 %collective-permute-start.6 = (bf16[256,256]{1,0:T(8,128)(2,1)}, bf16[256,256]{1,0:T(8,128)(2,1)S(1)}, u32[]{:S(2)}, u32[]{:S(2)}) collective-permute-start(bf16[256,256]{1,0:T(8,128)(2,1)} %get-tuple-element.158), channel_id=1, source_target_pairs={{0,7},{1,6},{2,5},{3,4},{4,3},{5,2},{6,1},{7,0},{8,15},{9,14},{10,... | collective-permute-start | bytes 393224 | tf_op jit(solution)/shard_map/ppermute | solution.py:664
  144.1 193.4 %all-gather.14.cloned.1.call-start = ((), (), s32[]{:S(2)}) async-start(), calls=%async_computation.9 | async-start | bytes 5242880 | tf_op jit(solution)/shard_map/all_gather | solution.py:1103
  193.5 247.7 %reduce-scatter.5.cloned.1.call-start = ((), (), s32[]{:S(2)}) async-start(), calls=%async_computation.10 | async-start | bytes 5242880 | tf_op jit(solution)/shard_map/reduce_scatter | solution.py:1099
  310.5 202.1 %reduce-scatter.7.cloned.1.call-start = ((), (), s32[]{:S(2)}) async-start(), calls=%async_computation.11 | async-start | bytes 5242880 | tf_op jit(solution)/shard_map/reduce_scatter | solution.py:1099
  376.0 222.0 %reduce-scatter.9.cloned.1.call-start = ((), (), s32[]{:S(2)}) async-start(), calls=%async_computation.12 | async-start | bytes 5242880 | tf_op jit(solution)/shard_map/reduce_scatter | solution.py:1099
  490.6 27.6 %collective-permute-start.15 = (bf16[64,1024]{1,0:T(8,128)(2,1)}, bf16[64,1024]{1,0:T(8,128)(2,1)S(1)}, u32[]{:S(2)}, u32[]{:S(2)}) collective-permute-start(bf16[64,1024]{1,0:T(8,128)(2,1)} %get-tuple-element.209), channel_id=1, source_target_pairs={{0,1},{1,0},{2,3},{3,2},{4,5},{5,4},{6,7},{7,6},{8,9},{9,8},{10,11... | collective-permute-start | bytes 393224 | tf_op jit(solution)/shard_map/ppermute | solution.py:664
  490.9 29.0 %collective-permute-start.16 = (bf16[64,1024]{1,0:T(8,128)(2,1)}, bf16[64,1024]{1,0:T(8,128)(2,1)S(1)}, u32[]{:S(2)}, u32[]{:S(2)}) collective-permute-start(bf16[64,1024]{1,0:T(8,128)(2,1)} %get-tuple-element.210), channel_id=1, source_target_pairs={{0,2},{1,3},{2,0},{3,1},{4,6},{5,7},{6,4},{7,5},{8,10},{9,11},{10,... | collective-permute-start | bytes 393224 | tf_op jit(solution)/shard_map/ppermute | solution.py:664
  491.5 80.1 %collective-permute-start.17 = (bf16[64,1024]{1,0:T(8,128)(2,1)}, bf16[64,1024]{1,0:T(8,128)(2,1)S(1)}, u32[]{:S(2)}, u32[]{:S(2)}) collective-permute-start(bf16[64,1024]{1,0:T(8,128)(2,1)} %get-tuple-element.211), channel_id=1, source_target_pairs={{0,3},{1,2},{2,1},{3,0},{4,7},{5,6},{6,5},{7,4},{8,11},{9,10},{10,... | collective-permute-start | bytes 393224 | tf_op jit(solution)/shard_map/ppermute | solution.py:664
  492.5 80.0 %collective-permute-start.18 = (bf16[64,1024]{1,0:T(8,128)(2,1)}, bf16[64,1024]{1,0:T(8,128)(2,1)}, u32[]{:S(2)}, u32[]{:S(2)}) collective-permute-start(bf16[64,1024]{1,0:T(8,128)(2,1)} %get-tuple-element.212), channel_id=1, source_target_pairs={{0,4},{1,5},{2,6},{3,7},{4,0},{5,1},{6,2},{7,3},{8,12},{9,13},{10,... | collective-permute-start | bytes 393224 | tf_op jit(solution)/shard_map/ppermute | solution.py:664
  500.0 89.0 %all-to-all-start = ((bf16[256,8,256]{2,0,1:T(8,128)(2,1)}), bf16[256,8,256]{2,0,1:T(8,128)(2,1)S(1)}, u32[]{:S(2)}, u32[]{:S(2)}) async-start(bf16[256,8,256]{2,0,1:T(8,128)(2,1)} %bitcast.56), calls=%async_computation.2 | async-start | bytes 2097152 | tf_op jit(solution)/shard_map/all_to_all | solution.py:1252
  503.6 164.1 %reduce-scatter.11.cloned.1.call-start = ((), (), s32[]{:S(2)}) async-start(), calls=%async_computation.13 | async-start | bytes 3276800 | tf_op jit(solution)/shard_map/reduce_scatter | solution.py:1099
  510.9 61.6 %collective-permute-start.19 = (bf16[64,1024]{1,0:T(8,128)(2,1)}, bf16[64,1024]{1,0:T(8,128)(2,1)}, u32[]{:S(2)}, u32[]{:S(2)}) collective-permute-start(bf16[64,1024]{1,0:T(8,128)(2,1)} %get-tuple-element.213), channel_id=1, source_target_pairs={{0,5},{1,4},{2,7},{3,6},{4,1},{5,0},{6,3},{7,2},{8,13},{9,12},{10,... | collective-permute-start | bytes 393224 | tf_op jit(solution)/shard_map/ppermute | solution.py:664
  518.3 55.6 %collective-permute-start.20 = (bf16[64,1024]{1,0:T(8,128)(2,1)S(1)}, bf16[64,1024]{1,0:T(8,128)(2,1)S(1)}, u32[]{:S(2)}, u32[]{:S(2)}) collective-permute-start(bf16[64,1024]{1,0:T(8,128)(2,1)S(1)} %copy-done.52), channel_id=1, source_target_pairs={{0,6},{1,7},{2,4},{3,5},{4,2},{5,3},{6,0},{7,1},{8,14},{9,15},{10,... | collective-permute-start | bytes 393224 | tf_op jit(solution)/shard_map/ppermute | solution.py:664
  519.9 78.1 %collective-permute-start.29 = (bf16[512,2048]{1,0:T(8,128)(2,1)}, bf16[512,2048]{1,0:T(8,128)(2,1)}, u32[]{:S(2)}, u32[]{:S(2)}) collective-permute-start(bf16[512,2048]{1,0:T(8,128)(2,1)} %get-tuple-element.294), channel_id=1, source_target_pairs={{0,4},{1,3},{2,6},{3,1},{4,0},{5,7},{6,2},{7,5},{8,12},{9,11},{10,... | collective-permute-start | bytes 6291464 | tf_op jit(solution)/shard_map/ppermute | solution.py:674
  (83 other events, 1381.1 us)
Sparse Core Ops, SparseCore 0:
  26.8 38.2 all-gather.5
  66.7 26.7 all-gather.7
  95.1 80.2 all-gather.9
  177.4 79.2 all-gather.11
  258.1 79.2 all-gather.13
  339.6 75.2 reduce-scatter.4
  417.3 77.2 reduce-scatter.6
  496.9 77.2 reduce-scatter.8
  598.1 53.8 reduce-scatter.10

commit v4 on v3

--- a/solution.py
+++ b/solution.py
@@ -20,6 +20,7 @@
 BLOCK = 256
 CHUNKS = 2
 PIECES = 4
+SCATTER_PIECES = 8
 VMEM_BYTES = 58 * 1024 * 1024
 MESH = pl.DeviceIdType.MESH
 BF16 = jnp.bfloat16
@@ -126,8 +127,8 @@
     tiles = []
     if count:
         helds = refs[5 : 7 + count]
-        down_grad, out_sibling, out_own = refs[7 + count : 10 + count]
-        load_sem, store_sem = refs[10 + count :]
+        down_grad, out_sibling, out_own, turned = refs[7 + count : 11 + count]
+        load_sem, store_sem = refs[11 + count :]
         hiddens, gradient, down = helds[:count], helds[count], helds[count + 1]
         units = hiddens[0].shape[1]
         loads = [
@@ -143,36 +144,25 @@
         for load in loads:
             load.start()
         half = out_own.shape[0]
-        height = min(256, half)
-        width = down.shape[1] // 4
-
-        def out_tile(target, base, row):
-            def one_part(index, carried):
-                columns = pl.ds(pl.multiple_of(index * width, width), width)
-                total = None
-                for number in range(count):
-                    term = dot_nn(
-                        hiddens[number][base + row : base + row + height, :],
-                        down[number * units : (number + 1) * units, columns],
-                    )
-                    total = term if total is None else total + term
-                target[row : row + height, columns] = total.astype(BF16)
-                return carried
-
-            lax.fori_loop(0, 4, one_part, 0)
-
-        tile = min(256, units)
+        width = 256
+
+        def out_tile(target, base, column):
+            total = None
+            for number in range(count):
+                term = dot_nn(
+                    hiddens[number][base : base + half, :],
+                    down[number * units : (number + 1) * units, column : column + width],
+                )
+                total = term if total is None else total + term
+            target[:, column : column + width] = total.astype(BF16)
+
+        def turn_tile(number):
+            turned[...] = jnp.transpose(hiddens[number][...])
 
         def grad_tile(number, column):
-            def one_part(index, carried):
-                columns = pl.ds(pl.multiple_of(index * width, width), width)
-                first = number * units + column
-                down_grad[first : first + tile, columns] = dot_tn(
-                    hiddens[number][:, column : column + tile], gradient[:, columns]
-                ).astype(BF16)
-                return carried
-
-            lax.fori_loop(0, 4, one_part, 0)
+            down_grad[number * units : (number + 1) * units, column : column + width] = dot_nn(
+                turned[...], gradient[:, column : column + width]
+            ).astype(BF16)
 
         for load in loads[:count] + loads[count + 1 :]:
             tiles.append(load.wait)
@@ -180,15 +170,17 @@
             (out_sibling, half, stores[1]),
             (out_own, 0, stores[2]),
         ):
-            for row in range(0, half, height):
-                tiles.append(functools.partial(out_tile, target, base, row))
+            for column in range(0, down.shape[1], width):
+                tiles.append(functools.partial(out_tile, target, base, column))
             tiles.append(store.start)
         tiles.append(loads[count].wait)
         for number in range(count):
-            for column in range(0, units, tile):
+            tiles.append(functools.partial(turn_tile, number))
+            for column in range(0, down.shape[1], width):
                 tiles.append(functools.partial(grad_tile, number, column))
         tiles.append(stores[0].start)
-    share = -(-len(tiles) // (steps * PIECES))
+    shares = [1 << step for step in range(steps) for part in range(PIECES)]
+    ends = [-(-len(tiles) * sum(shares[: n + 1]) // sum(shares)) for n in range(len(shares))]
 
     turn = 0
     for step in range(steps):
@@ -199,7 +191,7 @@
                 for later in range(step + 1, steps):
                     link_copy(later, arrived, part).start()
                 core_copy(arrived, part).start()
-            for run in tiles[turn * share : (turn + 1) * share]:
+            for run in tiles[ends[turn - 1] if turn else 0 : ends[turn]]:
                 run()
             turn += 1
     for part in range(PIECES):
@@ -242,6 +234,7 @@
             jax.ShapeDtypeStruct((total // 2, down.shape[1]), BF16),
         ]
         scratch += [pltpu.VMEM(value.shape, BF16) for value in out_shape[1:]]
+        scratch.append(pltpu.VMEM(hiddens[0].shape[::-1], BF16))
         scratch += [pltpu.SemaphoreType.DMA((count + 2,)), pltpu.SemaphoreType.DMA((3,))]
     result = pl.pallas_call(
         functools.partial(gather_kernel, member_count, in_order, count),
@@ -253,7 +246,7 @@
             collective_id=collective_id, has_side_effects=True, vmem_limit_bytes=VMEM_BYTES
         ),
         cost_estimate=pl.CostEstimate(
-            flops=0, bytes_accessed=60 * total * width, transcendentals=0
+            flops=0, bytes_accessed=(1 if extras else 60) * total * width, transcendentals=0
         ),
         name="plane_gather",
     )(*operands)
@@ -324,7 +317,11 @@
     )(*values)
 
 
-def product_scatter_kernel(member_count, in_order, transposed, count, rows, *refs):
+def product_scatter_kernel(member_count, in_order, transposed, count, rows, with_grad, *refs):
+    if with_grad:
+        other_ref, grad_ref = refs[0], refs[2 * count + 2]
+        held_other, held_grad, other_sem, grad_sem = refs[-4:]
+        refs = refs[1 : 2 * count + 2] + refs[2 * count + 3 : -4]
     lefts, rights, sum_ref = refs[:count], refs[count : 2 * count], refs[2 * count]
     held_lefts, held_rights = refs[2 * count + 1 : 3 * count + 1], refs[3 * count + 1 : 4 * count + 1]
     (
@@ -345,7 +342,8 @@
     masks = plane_masks(member_count)
     steps = len(masks)
     blocks = 1 << steps
-    piece = sum_ref.shape[1] // PIECES
+    pieces = SCATTER_PIECES
+    piece = sum_ref.shape[1] // pieces
 
     def left_copy(number, side, subset):
         owner = sibling if side else member
@@ -357,13 +355,19 @@
         )
 
     def right_copy(number):
-        return pltpu.make_async_copy(rights[number], held_rights[number], right_sem.at[number])
+        source = rights[number]
+        if transposed and source.shape[1] != held_rights[number].shape[1]:
+            source = source.at[:, pl.ds(0, held_rights[number].shape[1])]
+        return pltpu.make_async_copy(source, held_rights[number], right_sem.at[number])
 
     for number in range(count):
         right_copy(number).start()
         for side in (1, 0):
             for subset in range(blocks):
                 left_copy(number, side, subset).start()
+    if with_grad:
+        other_copy = pltpu.make_async_copy(other_ref, held_other, other_sem)
+        other_copy.start()
     greet(group, member, masks)
 
     def part(side, subset, where):
@@ -413,16 +417,13 @@
             for subset in range(blocks):
                 left_copy(number, side, subset).wait()
 
-    def for_sibling(index, carried):
+    def for_sibling(index):
         where = columns(index)
         for subset in range(blocks):
             outgoing[pl.ds(subset * rows, rows), where] = part(1, subset, where).astype(BF16)
         core_copy(index).start()
-        return carried
-
-    lax.fori_loop(0, PIECES, for_sibling, 0)
-
-    def for_links(index, carried):
+
+    def for_links(index):
         where = columns(index)
         core_copy(index).wait_recv()
         for subset in order:
@@ -434,14 +435,33 @@
                 held[where_rows, where] = total.astype(BF16)
             if subset & 1:
                 link_copy(0, subset, index).start()
+
+    def for_both(index, carried):
+        for_sibling(index)
+        for_links(index - 1)
         return carried
 
-    lax.fori_loop(0, PIECES, for_links, 0)
+    for_sibling(0)
+    lax.fori_loop(1, pieces, for_both, 0)
+    for_links(pieces - 1)
+    if with_grad:
+        other_copy.wait()
+        units = held_grad.shape[1] // pieces
+        late = 3 if steps > 1 else 0
+
+    def grad_tile(index):
+        where = pl.ds(pl.multiple_of(index * units, units), units)
+        turned = dot_tn(held_lefts[-1][:, where], held_other[...])
+        held_grad[:, where] = jnp.transpose(turned.astype(BF16))
 
     for step in range(steps):
 
         def one_step(index, carried, step=step):
             where = columns(index)
+            if with_grad and step == 0:
+                pl.when(index >= late)(lambda: grad_tile(index - late))
+            if with_grad and step == 1:
+                pl.when(index < late)(lambda: grad_tile(pieces - late + index))
             for kept in sorted(range(0, blocks, 2 << step), reverse=True):
                 link_copy(step, kept | (1 << step), index).wait_recv()
                 arrived = link_buffer[pl.ds(slot(step, kept) * rows, rows), where].astype(F32)
@@ -456,7 +476,10 @@
                     link_copy(step + 1, kept, index).start()
             return carried
 
-        lax.fori_loop(0, PIECES, one_step, 0)
+        lax.fori_loop(0, pieces, one_step, 0)
+        if with_grad and step == min(1, steps - 1):
+            grad_copy = pltpu.make_async_copy(held_grad, grad_ref, grad_sem)
+            grad_copy.start()
 
     def finish(index, carried):
         core_copy(index).wait_send()
@@ -465,10 +488,14 @@
                 link_copy(step, kept | (1 << step), index).wait_send()
         return carried
 
-    lax.fori_loop(0, PIECES, finish, 0)
-
-
-def product_scatter(lefts, rights, transposed, member_count, collective_id, in_order):
+    lax.fori_loop(0, pieces, finish, 0)
+    if with_grad:
+        grad_copy.wait()
+
+
+def product_scatter(
+    lefts, rights, transposed, member_count, collective_id, in_order, other=None, weight=60
+):
     count = len(lefts)
     total = lefts[0].shape[0]
     width = rights[0].shape[0 if transposed else 1]
@@ -477,7 +504,10 @@
     depth = sum(left.shape[1] for left in lefts)
     scratch = (
         [pltpu.VMEM(left.shape, BF16) for left in lefts]
-        + [pltpu.VMEM(right.shape, BF16) for right in rights]
+        + [
+            pltpu.VMEM((right.shape[0], left.shape[1]) if transposed else right.shape, BF16)
+            for left, right in zip(lefts, rights)
+        ]
         + [
             pltpu.VMEM((blocks * rows, width), BF16),
             pltpu.VMEM((blocks * rows, width), BF16),
@@ -485,35 +515,57 @@
             pltpu.VMEM(((blocks - 1) * rows, width), BF16),
             pltpu.SemaphoreType.DMA((count, 2, blocks)),
             pltpu.SemaphoreType.DMA((count,)),
-            pltpu.SemaphoreType.DMA((blocks - 1, PIECES)),
-            pltpu.SemaphoreType.DMA((blocks - 1, PIECES)),
-            pltpu.SemaphoreType.DMA((PIECES,)),
-            pltpu.SemaphoreType.DMA((PIECES,)),
+            pltpu.SemaphoreType.DMA((blocks - 1, SCATTER_PIECES)),
+            pltpu.SemaphoreType.DMA((blocks - 1, SCATTER_PIECES)),
+            pltpu.SemaphoreType.DMA((SCATTER_PIECES,)),
+            pltpu.SemaphoreType.DMA((SCATTER_PIECES,)),
         ]
     )
     any_space = pl.BlockSpec(memory_space=pl.ANY)
     in_vmem = pl.BlockSpec(memory_space=pltpu.VMEM)
-    return pl.pallas_call(
-        functools.partial(product_scatter_kernel, member_count, in_order, transposed, count, rows),
-        out_shape=jax.ShapeDtypeStruct((rows, width), F32),
-        in_specs=[any_space] * (2 * count),
-        out_specs=in_vmem,
+    operands = [*lefts, *rights]
+    out_shape = [jax.ShapeDtypeStruct((rows, width), F32)]
+    if other is not None:
+        operands = [other] + operands
+        grad_shape = (other.shape[1], lefts[-1].shape[1])
+        out_shape.append(jax.ShapeDtypeStruct(grad_shape, BF16))
+        scratch += [
+            pltpu.VMEM(other.shape, BF16),
+            pltpu.VMEM(grad_shape, BF16),
+            pltpu.SemaphoreType.DMA,
+            pltpu.SemaphoreType.DMA,
+        ]
+    result = pl.pallas_call(
+        functools.partial(
+            product_scatter_kernel,
+            member_count,
+            in_order,
+            transposed,
+            count,
+            rows,
+            other is not None,
+        ),
+        out_shape=out_shape,
+        in_specs=[any_space] * len(operands),
+        out_specs=[in_vmem] + [any_space] * (len(out_shape) - 1),
         scratch_shapes=scratch,
         compiler_params=pltpu.CompilerParams(
             collective_id=collective_id, has_side_effects=True, vmem_limit_bytes=VMEM_BYTES
         ),
         cost_estimate=pl.CostEstimate(
-            flops=2 * total * depth * width, bytes_accessed=60 * total * width, transcendentals=0
+            flops=0, bytes_accessed=weight * total * width, transcendentals=0
         ),
         name="product_scatter",
-    )(*lefts, *rights)
-
-
-def total_steps(
-    member_count, group_count, part_ref, sum_ref, near, held, far, near_send, near_recv, far_send, far_recv
-):
+    )(*operands)
+    return result[0] if other is None else result
+
+
+def finale_kernel(member_count, group_count, packed_ref, part_ref, arrived, sum_ref, *refs):
+    near, held, far = refs[:3]
+    packed_send, packed_recv, own_sem, near_send, near_recv, far_send, far_recv = refs[3:]
     group = lax.axis_index("dp")
     member = lax.axis_index("fsdp")
+    shard = arrived.shape[1]
     barrier = pltpu.get_barrier_semaphore()
     for away in range(1, member_count):
         pl.semaphore_signal(
@@ -527,6 +579,20 @@
             barrier, inc=1, device_id=((group + away) % group_count, member), device_id_type=MESH
         )
     pl.semaphore_wait(barrier, member_count + group_count - 2)
+
+    def rows_of(target):
+        return packed_ref.at[pl.ds(pl.multiple_of(target * shard, shard), shard)]
+
+    def packed_copy(away):
+        target = (member + away) % member_count
+        return pltpu.make_async_remote_copy(
+            rows_of(target),
+            arrived.at[away],
+            packed_send.at[away],
+            packed_recv.at[away],
+            device_id=(group, target),
+            device_id_type=MESH,
+        )
 
     def near_copy(away):
         target = (member + away) % member_count
@@ -549,55 +615,65 @@
             device_id_type=MESH,
         )
 
-    def near_step():
-        for away in range(1, member_count):
-            near_copy(away).start()
-
-    def far_step():
-        total = part_ref[member]
-        for away in range(1, member_count):
-            near_copy(away).wait_recv()
-            total = total + near[away]
-        held[...] = total
-        for away in range(1, group_count):
-            far_copy(away).start()
-
-    def end_step():
-        total = held[...]
-        for away in range(1, group_count):
-            far_copy(away).wait_recv()
-            total = total + far[away]
-        sum_ref[...] = total
-        for away in range(1, member_count):
-            near_copy(away).wait_send()
-        for away in range(1, group_count):
-            far_copy(away).wait_send()
-
-    near_step()
-    far_step()
-    end_step()
-
-
-def total_over_all(parts, group_count, collective_id):
-    member_count, rows, lanes = parts.shape
+    own_copy = pltpu.make_async_copy(rows_of(member), arrived.at[0], own_sem)
+    for away in range(1, member_count):
+        near_copy(away).start()
+    for away in range(1, member_count):
+        packed_copy(away).start()
+    own_copy.start()
+    total = part_ref[member]
+    for away in range(1, member_count):
+        near_copy(away).wait_recv()
+        total = total + near[away]
+    held[...] = total
+    for away in range(1, group_count):
+        far_copy(away).start()
+
+    for away in range(1, member_count):
+        packed_copy(away).wait_recv()
+    own_copy.wait()
+    for away in range(1, group_count):
+        far_copy(away).wait_recv()
+        total = total + far[away]
+    sum_ref[...] = total
+    for away in range(1, member_count):
+        near_copy(away).wait_send()
+        packed_copy(away).wait_send()
+    for away in range(1, group_count):
+        far_copy(away).wait_send()
+
+
+def finale(packed, parts, group_count, collective_id):
+    member_count, lines, lanes = parts.shape
+    shard = packed.shape[0] // member_count
+    in_vmem = pl.BlockSpec(memory_space=pltpu.VMEM)
+    any_space = pl.BlockSpec(memory_space=pl.ANY)
+    members_dma = pltpu.SemaphoreType.DMA((member_count,))
+    groups_dma = pltpu.SemaphoreType.DMA((group_count,))
     return pl.pallas_call(
-        functools.partial(total_steps, member_count, group_count),
-        out_shape=jax.ShapeDtypeStruct((rows, lanes), F32),
-        in_specs=[pl.BlockSpec(memory_space=pltpu.VMEM)],
-        out_specs=pl.BlockSpec(memory_space=pltpu.VMEM),
+        functools.partial(finale_kernel, member_count, group_count),
+        out_shape=[
+            jax.ShapeDtypeStruct((member_count, shard, packed.shape[1]), BF16),
+            jax.ShapeDtypeStruct((lines, lanes), F32),
+        ],
+        in_specs=[any_space, in_vmem],
+        out_specs=[any_space, in_vmem],
         scratch_shapes=[
-            pltpu.VMEM((member_count, rows, lanes), F32),
-            pltpu.VMEM((rows, lanes), F32),
-            pltpu.VMEM((group_count, rows, lanes), F32),
-            pltpu.SemaphoreType.DMA((member_count,)),
-            pltpu.SemaphoreType.DMA((member_count,)),
-            pltpu.SemaphoreType.DMA((group_count,)),
-            pltpu.SemaphoreType.DMA((group_count,)),
+            pltpu.VMEM((member_count, lines, lanes), F32),
+            pltpu.VMEM((lines, lanes), F32),
+            pltpu.VMEM((group_count, lines, lanes), F32),
+            members_dma,
+            members_dma,
+            pltpu.SemaphoreType.DMA,
+            members_dma,
+            members_dma,
+            groups_dma,
+            groups_dma,
         ],
         compiler_params=pltpu.CompilerParams(collective_id=collective_id, has_side_effects=True),
         cost_estimate=pl.CostEstimate(flops=0, bytes_accessed=40000000, transcendentals=0),
-        name="total_over_all",
-    )(parts)
+        name="finale",
+    )(packed, parts)
 
 
 def local_call(kernel, name, out_shape, *operands):
@@ -619,15 +695,15 @@
     )(*operands)
 
 
-def rows_apart(member, value, member_count):
+def rows_apart(member, value, member_count, column=0):
     rows = value.shape[0] // member_count
 
     def kernel(member_ref, value_ref, *out_refs):
         for away, out_ref in enumerate(out_refs):
             other = member_ref[0] ^ away
-            out_ref[...] = value_ref[pl.ds(pl.multiple_of(other * rows, rows), rows), :]
-
-    shape = jax.ShapeDtypeStruct((rows, value.shape[1]), value.dtype)
+            out_ref[...] = value_ref[pl.ds(pl.multiple_of(other * rows, rows), rows), column:]
+
+    shape = jax.ShapeDtypeStruct((rows, value.shape[1] - column), value.dtype)
     return local_call(kernel, "rows_apart", [shape] * member_count, member, value)
 
 
@@ -756,15 +832,13 @@
     return local_call(kernel, "units_together", [shape] * 2, member, gain, *blocks)
 
 
-def heads_together(member, blocks, gain, heads):
-    count = len(blocks)
-    shard, columns = blocks[0].shape
+def heads_together(member, arrived, gain, heads):
+    count, shard, columns = arrived.shape
     width = heads * HD
     out_width = columns - width - 2 * HD
     copies = count // KVH
 
-    def kernel(member_ref, gain_ref, *refs):
-        ins, (query_out, key_out, value_out, out_out) = refs[:count], refs[count:]
+    def kernel(member_ref, arrived_ref, gain_ref, query_out, key_out, value_out, out_out):
         row = lax.broadcasted_iota(jnp.int32, (width, width), 0)
         column = lax.broadcasted_iota(jnp.int32, (width, width), 1)
         source = column % HD // HALF * (HALF * heads) + column // HD * HALF + column % HALF
@@ -775,18 +849,17 @@
         keys = jnp.zeros((shard, KVH * HD), F32)
         values = jnp.zeros((shard, KVH * HD), F32)
         for away in range(count):
-            other = member_ref[0] ^ away
-            block = ins[away]
+            other = (member_ref[0] + count - away) % count
             where = pl.ds(pl.multiple_of(other * width, width), width)
-            query_out[:, where] = dot_nn(block[:, :width], order) * gain_here
-            pair = block[:, width : width + 2 * HD]
+            query_out[:, where] = dot_nn(arrived_ref[away, :, :width], order) * gain_here
+            pair = arrived_ref[away, :, width : width + 2 * HD]
             first = other // copies * HD
-            keys = keys + dot_nn(pair, (pair_column == pair_row + first).astype(BF16) * (pair_row < HD).astype(BF16))
-            values = values + dot_nn(
-                pair, (pair_column == pair_row - HD + first).astype(BF16) * (pair_row >= HD).astype(BF16)
-            )
+            to_keys = (pair_column == pair_row + first) & (pair_row < HD)
+            to_values = (pair_column == pair_row - HD + first) & (pair_row >= HD)
+            keys = keys + dot_nn(pair, to_keys.astype(BF16))
+            values = values + dot_nn(pair, to_values.astype(BF16))
             out_where = pl.ds(pl.multiple_of(other * out_width, out_width), out_width)
-            out_out[:, out_where] = block[:, width + 2 * HD :].astype(F32)
+            out_out[:, out_where] = arrived_ref[away, :, width + 2 * HD :].astype(F32)
         key_out[...] = keys * gain_here
         value_out[...] = values * gain_here
 
@@ -794,7 +867,59 @@
         jax.ShapeDtypeStruct((shard, size), F32)
         for size in (count * width, KVH * HD, KVH * HD, count * out_width)
     ]
-    return local_call(kernel, "heads_together", shapes, member, gain, *blocks)
+    return local_call(kernel, "heads_together", shapes, member, arrived, gain)
+
+
+def units_kernel(normed_ref, gradient_ref, both_ref, down_ref, hidden_ref, grad_ref):
+    units = down_ref.shape[0]
+    normed = normed_ref[...]
+    gradient = gradient_ref[...]
+    part = min(256, units)
+    for first in range(0, units, part):
+        where = slice(first, first + part)
+        past = slice(units + first, units + first + part)
+        gate = dot_nn(normed, both_ref[:, where])
+        up = dot_nn(normed, both_ref[:, past])
+        upstream = dot_nt(gradient, down_ref[where, :])
+        sigmoid = jax.nn.sigmoid(gate)
+        active = gate * sigmoid
+        hidden_ref[:, where] = (active * up).astype(BF16)
+        grad_ref[:, where] = (
+            upstream * up * sigmoid * (1.0 + gate * (1.0 - sigmoid))
+        ).astype(BF16)
+        grad_ref[:, past] = (upstream * active).astype(BF16)
+
+
+def hidden_units(normed, gradient, both, down, chunk):
+    tokens, model = normed.shape
+    units = both.shape[1] // 2
+    tile = 512
+    by_tile = pl.BlockSpec((tile, model), lambda i: (i, 0))
+    return pl.pallas_call(
+        units_kernel,
+        grid=(tokens // tile,),
+        in_specs=[
+            by_tile,
+            by_tile,
+            pl.BlockSpec(both.shape, lambda i: (0, 0)),
+            pl.BlockSpec((units, model), lambda i: (chunk, 0)),
+        ],
+        out_specs=[
+            pl.BlockSpec((tile, units), lambda i: (i, 0)),
+            pl.BlockSpec((tile, 2 * units), lambda i: (i, 0)),
+        ],
+        out_shape=[
+            jax.ShapeDtypeStruct((tokens, units), BF16),
+            jax.ShapeDtypeStruct((tokens, 2 * units), BF16),
+        ],
+        compiler_params=pltpu.CompilerParams(vmem_limit_bytes=VMEM_BYTES),
+        cost_estimate=pl.CostEstimate(
+            flops=6 * tokens * model * units,
+            bytes_accessed=4 * tokens * model + 6 * units * model,
+            transcendentals=tokens * units,
+        ),
+        name="hidden_units",
+    )(normed, gradient, both, down)
 
 
 def half_group(shape, heads):
@@ -849,11 +974,13 @@
 def forward_kernel(
     heads,
     first_ref,
-    projected_ref,
+    normed_ref,
+    weight_ref,
     table_ref,
     start_ref,
     query_ref,
     key_ref,
+    key_columns_ref,
     value_ref,
     mixed_ref,
     lse_ref,
@@ -866,12 +993,16 @@
     width = heads * HD
     start = start_ref[...]
     cosine, sine = tables(table_ref[...], width)
-    query = turn(projected_ref[:, :width], cosine, sine).astype(BF16)
-    pair = projected_ref[:, width:]
+    projected = dot_nn(normed_ref[...], weight_ref[:, : width + 2 * HD])
+    query = turn(projected[:, :width], cosine, sine).astype(BF16)
+    pair = projected[:, width:]
     keys_here = turn(exact(pair, spread_keys(width), ((1,), (0,))), cosine, sine).astype(BF16)
     own_rows = pl.ds(pl.multiple_of(step * BLOCK, BLOCK), BLOCK)
     query_ref[...] = query
     key_ref[own_rows, :] = keys_here
+    turned_keys = jnp.transpose(keys_here.astype(F32)).astype(BF16)
+    key_columns_ref[:HALF, :] = turned_keys[:HALF, :]
+    key_columns_ref[HALF:, :] = turned_keys[width // 2 : width // 2 + HALF, :]
     value_ref[...] = exact(pair, spread_values(width), ((1,), (0,))).astype(BF16)
     value_columns[:, own_rows] = jnp.transpose(pair)[HD:, :].astype(BF16)
     token = step * BLOCK + lax.broadcasted_iota(jnp.int32, (BLOCK, BLOCK), 1)
@@ -912,10 +1043,9 @@
     lse_ref[...] = top[...] + jnp.log(total[...])
 
 
-def attention_forward(first, projected, table, start):
-    tokens, columns = projected.shape
-    width = columns - 2 * HD
-    heads = width // HD
+def attention_forward(first, normed, weight, table, start, heads):
+    tokens, model = normed.shape
+    width = heads * HD
     by_block = pl.BlockSpec((BLOCK, width), lambda i, first: (i, 0))
     whole = pl.BlockSpec((tokens, width), lambda i, first: (0, 0))
     return pl.pallas_call(
@@ -924,13 +1054,15 @@
             num_scalar_prefetch=1,
             grid=(tokens // BLOCK,),
             in_specs=[
-                pl.BlockSpec((BLOCK, columns), lambda i, first: (i, 0)),
+                pl.BlockSpec((BLOCK, model), lambda i, first: (i, 0)),
+                pl.BlockSpec(weight.shape, lambda i, first: (0, 0)),
                 pl.BlockSpec((BLOCK, 2 * HALF), lambda i, first: (i, 0)),
                 pl.BlockSpec((1, BLOCK), lambda i, first: (0, i)),
             ],
             out_specs=[
                 by_block,
                 whole,
+                pl.BlockSpec((HD, BLOCK), lambda i, first: (0, i)),
                 by_block,
                 by_block,
                 pl.BlockSpec((heads, BLOCK), lambda i, first: (0, i)),
@@ -942,14 +1074,16 @@
                 pltpu.VMEM((width, BLOCK), F32),
             ],
         ),
-        out_shape=[jax.ShapeDtypeStruct((tokens, width), BF16)] * 4
+        out_shape=[jax.ShapeDtypeStruct((tokens, width), BF16)] * 2
+        + [jax.ShapeDtypeStruct((HD, tokens), BF16)]
+        + [jax.ShapeDtypeStruct((tokens, width), BF16)] * 2
         + [jax.ShapeDtypeStruct((heads, tokens), F32)],
         compiler_params=pltpu.CompilerParams(vmem_limit_bytes=VMEM_BYTES),
         cost_estimate=pl.CostEstimate(
             flops=64 * tokens * BLOCK * width, bytes_accessed=8 * tokens * width, transcendentals=0
         ),
         name="attention_forward",
-    )(first, projected, table, start)
+    )(first, normed, weight, table, start)
 
 
 def backward_kernel(
@@ -957,20 +1091,25 @@
     first_ref,
     query_ref,
     key_ref,
+    key_columns_ref,
     value_ref,
     mixed_ref,
     grad_ref,
+    weight_ref,
     lse_ref,
     start_ref,
     table_ref,
     out_ref,
+    weight_grad_ref,
     dquery,
     dkey,
     dvalue,
+    weight_grad,
 ):
     step = pl.program_id(0)
     query = query_ref[...]
-    grad = grad_ref[...]
+    grad_one = grad_ref[...]
+    grad = dot_nt(grad_one, weight_ref[...]).astype(BF16)
     start = start_ref[...]
     width = query.shape[1]
     token = step * BLOCK + lax.broadcasted_iota(jnp.int32, (BLOCK, BLOCK), 1)
@@ -989,7 +1128,9 @@
     def _():
         dkey[...] = jnp.zeros_like(dkey)
         dvalue[...] = jnp.zeros_like(dvalue)
-
+        weight_grad[...] = jnp.zeros_like(weight_grad)
+
+    weight_grad[...] += dot_tn(mixed_ref[...], grad_one)
     dquery[...] = jnp.zeros_like(dquery)
 
     def one_block(block, carried):
@@ -997,9 +1138,9 @@
         rows = pl.ds(offset, BLOCK)
         keys = key_ref[rows, :]
         values = value_ref[rows, :]
+        key_columns = key_columns_ref[:, rows]
         place = offset + within
         visible = (place >= start) & (place <= token)
-        new_query = dquery[...]
         new_key = dkey[rows, :]
         new_value = dvalue[rows, :]
         for head in range(heads):
@@ -1013,8 +1154,11 @@
                 probs.astype(BF16), jnp.where(full_head == head, grad, zero)
             )
             new_key = new_key + dot_nn(dscores, jnp.where(half_head == head, query, zero))
-            new_query = new_query + dot_tn(dscores, own_keys)
-        dquery[...] = new_query
+            term = dot_nn(key_columns, dscores)
+            low = slice(head * HALF, (head + 1) * HALF)
+            high = slice(width // 2 + head * HALF, width // 2 + (head + 1) * HALF)
+            dquery[low, :] += term[:HALF]
+            dquery[high, :] += term[HALF:]
         dkey[rows, :] = new_key
         dvalue[rows, :] = new_value
         return carried
@@ -1022,7 +1166,9 @@
     lax.fori_loop(first_ref[step], step + 1, one_block, 0)
     own_rows = pl.ds(pl.multiple_of(step * BLOCK, BLOCK), BLOCK)
     cosine, sine = tables(table_ref[own_rows, :], width)
-    out_ref[own_rows, :width] = (turn(dquery[...], cosine, -sine) * ATTENTION_SCALE).astype(BF16)
+    out_ref[own_rows, :width] = (
+        turn(jnp.transpose(dquery[...]), cosine, -sine) * ATTENTION_SCALE
+    ).astype(BF16)
 
     @pl.when(step == pl.num_programs(0) - 1)
     def _():
@@ -1031,16 +1177,20 @@
             cosine, sine = tables(table_ref[rows, :], width)
             turned = turn(dkey[rows, :], cosine, -sine) * ATTENTION_SCALE
             out_ref[rows, width:] = (
-                exact(turned, spread_keys(width), ((1,), (1,)))
-                + exact(dvalue[rows, :], spread_values(width), ((1,), (1,)))
+                dot_nt(turned.astype(BF16), spread_keys(width).astype(BF16))
+                + dot_nt(dvalue[rows, :].astype(BF16), spread_values(width).astype(BF16))
             ).astype(BF16)
             return carried
 
         lax.fori_loop(0, pl.num_programs(0), fold, 0)
-
-
-def attention_backward(first, query, keys, values, mixed, grad, lse, start, table):
+        weight_grad_ref[...] = weight_grad[...].astype(BF16)
+
+
+def attention_backward(
+    first, query, keys, key_columns, values, mixed, grad, weight, lse, start, table
+):
     tokens, width = query.shape
+    model = grad.shape[1]
     heads = width // HD
     columns = width + 2 * HD
     by_block = pl.BlockSpec((BLOCK, width), lambda i, first: (i, 0))
@@ -1053,29 +1203,36 @@
             in_specs=[
                 by_block,
                 whole,
+                pl.BlockSpec((HD, tokens), lambda i, first: (0, 0)),
                 whole,
                 by_block,
-                by_block,
+                pl.BlockSpec((BLOCK, model), lambda i, first: (i, 0)),
+                pl.BlockSpec((width, model), lambda i, first: (0, 0)),
                 pl.BlockSpec((heads, BLOCK), lambda i, first: (0, i)),
                 pl.BlockSpec((1, BLOCK), lambda i, first: (0, i)),
                 pl.BlockSpec((tokens, 2 * HALF), lambda i, first: (0, 0)),
             ],
-            out_specs=pl.BlockSpec((tokens, columns), lambda i, first: (0, 0)),
+            out_specs=[
+                pl.BlockSpec((tokens, columns), lambda i, first: (0, 0)),
+                pl.BlockSpec((width, model), lambda i, first: (0, 0)),
+            ],
             scratch_shapes=[
-                pltpu.VMEM((BLOCK, width), F32),
+                pltpu.VMEM((width, BLOCK), F32),
                 pltpu.VMEM((tokens, width), F32),
                 pltpu.VMEM((tokens, width), F32),
+                pltpu.VMEM((width, model), F32),
             ],
         ),
-        out_shape=jax.ShapeDtypeStruct((tokens, columns), BF16),
+        out_shape=[
+            jax.ShapeDtypeStruct((tokens, columns), BF16),
+            jax.ShapeDtypeStruct((width, model), BF16),
+        ],
         compiler_params=pltpu.CompilerParams(vmem_limit_bytes=VMEM_BYTES),
         cost_estimate=pl.CostEstimate(
-            flops=160 * tokens * BLOCK * width,
-            bytes_accessed=24 * tokens * width,
-            transcendentals=0,
+            flops=0, bytes_accessed=tokens * width, transcendentals=0
         ),
         name="attention_backward",
-    )(first, query, keys, values, mixed, grad, lse, start, table)
+    )(first, query, keys, key_columns, values, mixed, grad, weight, lse, start, table)
 
 
 def token_starts(lengths_row, group_tokens):
@@ -1147,23 +1304,22 @@
             jnp.repeat(
                 scaled_value.reshape(shard, KVH, HD).transpose(1, 0, 2), copies, axis=0
             ),
+            output_weight.reshape(shard, members, out_columns).transpose(1, 0, 2),
         ],
         axis=2,
     )
-    packed_in, packed_out = plane_swap(
-        [packed_in, output_weight.reshape(shard, members, out_columns).transpose(1, 0, 2)],
-        members,
-        1,
-    )
-    packed_in = packed_in.reshape(members * shard, columns)
-    packed_out = packed_out.reshape(members * shard, out_columns)
+    [packed_in] = plane_swap([packed_in], members, 1)
+    packed_in = packed_in.reshape(members * shard, columns + out_columns)
     inputs = tokens.astype(F32)
     inverse_one = inverse_norm(inputs)
-    normed_one = plane_gather(after((inputs * inverse_one).astype(BF16), packed_in), members, 0, True)
-    projection = gather_groups(packed_in)
-    out_columns_piece = gather_groups(packed_out)
+    early = model // 4
+    down_early = gather_groups(down_weight[:, :early])
+    normed_one = plane_gather(
+        after((inputs * inverse_one).astype(BF16), packed_in, down_early), members, 0, True
+    )
+    packed = gather_groups(packed_in)
     upstream = cotangent.astype(F32)
-    down_all = gather_groups(after(down_weight, normed_one))
+    down_rest = gather_groups(after(down_weight[:, early:], normed_one))
     gate_up = exchanged(
         units_apart(
             member,
@@ -1183,11 +1339,10 @@
     table = jnp.concatenate([jnp.cos(angles), jnp.sin(angles)], axis=1)
     start = start[None, :]
 
-    projected = dot_nn(normed_one, projection)
-    out_blocks = exchanged(
-        rows_apart(member, after(out_columns_piece, projected), members)
-    )
-    query, keys, values, mixed, lse = attention_forward(first, projected, table, start)
+    out_blocks = exchanged(rows_apart(member, packed, members, columns))
+    query, keys, key_columns, values, mixed, lse = attention_forward(
+        first, normed_one, packed, table, start, heads
+    )
     mixed_then, out_blocks, gate_up = lax.optimization_barrier((mixed, out_blocks, gate_up))
     gate_up_chunks = [
         gather_groups(part) for part in rows_together(member, gate_up, CHUNKS)
@@ -1197,40 +1352,36 @@
     residual = inputs + RESIDUAL_SCALE * branch_one
 
     inverse_two = inverse_norm(residual)
-    normed_two, down_all = lax.optimization_barrier(
-        ((residual * inverse_two).astype(BF16), down_all)
+    normed_two, down_rest = lax.optimization_barrier(
+        ((residual * inverse_two).astype(BF16), down_rest)
     )
     normed_two = plane_gather(normed_two, members, 3, False)
     grad_two = plane_gather(
         after((RESIDUAL_SCALE * upstream).astype(BF16), normed_two), members, 9, False
     )
+    down_all = jnp.concatenate([down_early, after(down_rest, grad_two)], axis=1)
+    fused = group_tokens <= 2048
     hiddens = []
     grad_boths = []
     gate_up_grads = []
     for chunk in range(CHUNKS):
         both_weight = gate_up_chunks[chunk]
-        down_piece = down_all[chunk * units : (chunk + 1) * units]
-        both = dot_nn(normed_two, both_weight)
-        gate = both[:, :units]
-        up = both[:, units:]
-        sigmoid = jax.nn.sigmoid(gate)
-        hidden = (gate * sigmoid * up).astype(BF16)
-        grad_hidden = dot_nt(grad_two, down_piece)
-        grad_both = jnp.concatenate(
-            [
-                (grad_hidden * up * sigmoid * (1.0 + gate * (1.0 - sigmoid))).astype(BF16),
-                (grad_hidden * gate * sigmoid).astype(BF16),
-            ],
-            axis=1,
-        )
-        gate_up_grad = dot_tn(normed_two, grad_both).astype(BF16)
-        gate_up_grads.append(sum_over_groups(gate_up_grad))
-        normed_two, grad_two, hidden, grad_both, _ = lax.optimization_barrier(
-            (normed_two, grad_two, hidden, grad_both, gate_up_grad)
-        )
+        hidden, grad_both = hidden_units(normed_two, grad_two, both_weight, down_all, chunk)
         hiddens.append(hidden)
         grad_boths.append(grad_both)
-    weighted_two = product_scatter(grad_boths, gate_up_chunks, True, members, 4, False)
+        if chunk < CHUNKS - 1 or not fused:
+            gate_up_grad = dot_tn(normed_two, grad_both).astype(BF16)
+            gate_up_grads.append(sum_over_groups(gate_up_grad))
+            normed_two, grad_two, hiddens, grad_boths, _ = lax.optimization_barrier(
+                (normed_two, grad_two, hiddens, grad_boths, gate_up_grad)
+            )
+    if fused:
+        weighted_two, gate_up_grad = product_scatter(
+            grad_boths, gate_up_chunks, True, members, 4, False, normed_two
+        )
+        gate_up_grads.append(sum_over_groups(gate_up_grad))
+    else:
+        weighted_two = product_scatter(grad_boths, gate_up_chunks, True, members, 4, False)
     grad_residual = (
         upstream
         + inverse_two * weighted_two
@@ -1247,11 +1398,9 @@
     down_grad = sum_over_groups(down_grad)
     half_rows = group_tokens // 2
     out_sibling = send_to(out_sibling, members, lambda m: m ^ 1)
-    grad_mixed = dot_nt(grad_one, out_piece).astype(BF16)
-    out_grad = dot_tn(mixed, grad_one).astype(BF16)
-    out_grad = lax.all_to_all(out_grad, "fsdp", split_axis=1, concat_axis=0, tiled=True)
-    grad_mixed, gate_up_grads[-1], out_own, out_sibling = lax.optimization_barrier(
-        (grad_mixed, gate_up_grads[-1], out_own, out_sibling)
+    gate_up_grads[0] = exchanged(rows_apart(member, gate_up_grads[0], members))
+    grad_one, out_own, out_sibling = lax.optimization_barrier(
+        (grad_one, out_own, out_sibling)
     )
     steps = len(plane_masks(members))
     half_rows //= 2
@@ -1261,17 +1410,19 @@
         hopped(steps - 1, members),
     )
     out_kept = added(out_own[:half_rows], out_sibling[:half_rows]).astype(BF16)
-    gate_up_grads = [exchanged(rows_apart(member, part, members)) for part in gate_up_grads]
-    grad_projected = attention_backward(
-        first, query, keys, values, mixed, grad_mixed, lse, start, table
-    )
+    grad_projected, out_grad = attention_backward(
+        first, query, keys, key_columns, values, mixed, grad_one, out_piece, lse, start, table
+    )
+    out_grad = lax.all_to_all(out_grad, "fsdp", split_axis=1, concat_axis=0, tiled=True)
     packed_grad = jnp.concatenate(
         [dot_tn(normed_one, grad_projected).astype(BF16), out_grad], axis=1
     )
-    grad_projected, packed_grad, gate_up_grads, out_sent, out_kept, down_grad = (
-        lax.optimization_barrier(
-            (grad_projected, packed_grad, gate_up_grads, out_sent, out_kept, down_grad)
-        )
+    gate_up_grads[1:] = [
+        exchanged(rows_apart(member, part, members))
+        for part in after(gate_up_grads[1:], grad_projected)
+    ]
+    grad_projected, packed_grad, gate_up_grads[0], out_sent, out_kept = lax.optimization_barrier(
+        (grad_projected, packed_grad, gate_up_grads[0], out_sent, out_kept)
     )
     for step in reversed(range(steps - 1)):
         half_rows //= 2
@@ -1281,7 +1432,8 @@
             out_kept = out_kept.astype(BF16)
         out_sent = send_to(out_next, members, hopped(step, members))
     packed_grad = sum_over_groups(packed_grad)
-    weighted_one = product_scatter([grad_projected], [projection], True, members, 6, True)
+    weighted_one = product_scatter([grad_projected], [packed], True, members, 6, True, weight=1)
+    weighted_one, down_grad = lax.optimization_barrier((weighted_one, down_grad))
     grad_inputs = (
         grad_residual
         + inverse_one * weighted_one
@@ -1299,20 +1451,17 @@
     gains = jnp.pad(
         gains.transpose(1, 0, 2), ((0, 0), (0, (-groups) % 8), (0, (-2 * shard) % 128))
     )
-    gains = total_over_all(gains, groups, 8)
-    out_sent, out_kept, _ = lax.optimization_barrier((out_sent, out_kept, gains))
-    output = residual + RESIDUAL_SCALE * added(out_kept, out_sent)
-
+    output = (residual + RESIDUAL_SCALE * added(out_kept, out_sent)).astype(BF16)
+
+    gate_grad, up_grad = units_together(
+        member, after(gate_up_grads, weighted_one), gain_two, members, groups
+    )
+    arrived, gains = finale(packed_grad, gains, groups, 8)
+    query_grad, key_grad, value_grad, out_grad = heads_together(member, arrived, gain_one, heads)
     gains = lax.dynamic_slice_in_dim(gains, lax.axis_index("dp"), 1, 0)[0, : 2 * shard]
     gains = gains.reshape(2, shard)
-    gate_grad, up_grad = units_together(
-        member, after(gate_up_grads, gains), gain_two, members, groups
-    )
-    query_grad, key_grad, value_grad, out_grad = heads_together(
-        member, exchanged(rows_apart(member, packed_grad, members)), gain_one, heads
-    )
     return (
-        output.astype(BF16),
+        output,
         grad_inputs.astype(BF16),
         query_grad,
         key_grad,

time: 711 us -> 676 us (0.951)
  matrix products: 106 us -> 23.5 us
  Pallas kernels: 440 us -> 493 us
  other arithmetic: 53.8 us -> 41 us
    dot_general x6 -> x0, matrix products: 66.3 us -> none  [the longest x3 37.3 us: dot_nn(): return jnp.dot(left, right, preferred_element_type=F32)]
    pallas_call x1 -> x3, Pallas kernels: 11.8 us -> 56.2 us  [the longest x2 38.9 us: hidden_units(): pl.pallas_call(units_kernel, grid=(tokens // tile,), in_specs=[by_tile, b...]
    dot_general x4 -> x2, matrix products: 39.2 us -> 23.5 us  [dot_tn(): lax.dot_general(left, right, (((0,), (0,)), ((), ())), preferred_element_...]
    all_gather x5, waiting for transfers between devices: 22 us -> 12.4 us  [gather_groups(): return lax.all_gather(value, 'dp', axis=0, tiled=True)]
    concatenate x2 -> x0, other arithmetic: 9.58 us -> none  [body(): jnp.concatenate([(grad_hidden * up * sigmoid * (1.0 + gate * (1.0 - sigmo...]
    ppermute x35 -> x28, waiting for transfers between devices: 10.8 us -> 20.1 us  [exchanged(): lax.ppermute(blocks[away], 'fsdp', [(m, m ^ away) for m in range(len(bloc...]
    ppermute x35 -> x28, starting transfers between devices: 31 us -> 26.6 us  [exchanged(): lax.ppermute(blocks[away], 'fsdp', [(m, m ^ away) for m in range(len(bloc...]
    pallas_call x9 -> x8, Pallas kernels: 24.9 us -> 22.8 us  [local_call(): pl.pallas_call(kernel, grid_spec=pltpu.PrefetchScalarGridSpec(num_scalar_...]
  transfers between devices with their start and end apart: 48 -> 41, of which waited for: 6 -> 8; matrix products, arithmetic and copies ran while one was open for 23% -> 11% of each run, Pallas kernels for 60% -> 71%
where the time goes in v4:
time: 676 us; the launch traced here: 665 us
  Pallas kernels  493 us (73%)
  waiting for transfers between devices  42.1 us (6%)
  other arithmetic  41 us (6%)
  starting transfers between devices  33.9 us (5%)
  matrix products  23.5 us (3%)
  local copies, waits for them, and re-layouts  16.2 us (2%)
  between operations  14.9 us (2%)
    pallas_call x4, Pallas kernels, plane_gather(): pl.pallas_call(functools.partial(gather_kernel, member_count, in_order, c...  163 us
    pallas_call x3, Pallas kernels, product_scatter(): pl.pallas_call(functools.partial(product_scatter_kernel, member_count, in...  148 us
    pallas_call x1, Pallas kernels, attention_backward(): pl.pallas_call(functools.partial(backward_kernel, heads), grid_spec=pltpu...  52.1 us
    pallas_call x1, Pallas kernels, attention_forward(): pl.pallas_call(functools.partial(forward_kernel, heads), grid_spec=pltpu....  39.2 us
    pallas_call x2, Pallas kernels, hidden_units(): pl.pallas_call(units_kernel, grid=(tokens // tile,), in_specs=[by_tile, b...  38.9 us
    ppermute x28, starting transfers between devices, exchanged(): lax.ppermute(blocks[away], 'fsdp', [(m, m ^ away) for m in range(len(bloc...  26.6 us
    dot_general x2, matrix products, dot_tn(): lax.dot_general(left, right, (((0,), (0,)), ((), ())), preferred_element_...  23.5 us
    pallas_call x8, Pallas kernels, local_call(): pl.pallas_call(kernel, grid_spec=pltpu.PrefetchScalarGridSpec(num_scalar_...  22.8 us
  transfers between devices with their start and end apart: 41, of which 8 were waited for; matrix products, arithmetic and copies ran while one was open for 11% of the time, Pallas kernels for 71%

profile of v4, /device:TPU:0, one launch (start us, length us, event | category | flops | bytes accessed | tf_op | source)
XLA Modules:
  0.0 664.9 jit_solution(685601554610455959)
XLA Ops:
  13.6 11.9 %plane_swap.1 = bf16[8,64,640]{2,1,0:T(8,128)(2,1)} custom-call(bf16[8,64,640]{2,1,0:T(8,128)(2,1)} %pad_maximum_fusion.2.refs_0_), custom_call_target="tpu_custom_call" | custom-call | bytes 19660800 | tf_op jit(solution)/shard_map/plane_swap/pallas_call | solution.py:300
  29.2 11.6 %all-gather.6.cloned.1.call-done = bf16[1024,512]{1,0:T(8,128)(2,1)} async-done(((bf16[256,512]{1,0:T(8,128)(2,1)}), bf16[1024,512]{1,0:T(8,128)(2,1)}) %all-gather.6.cloned.1.call-update) | async-done | bytes 1048592 | tf_op jit(solution)/shard_map/all_gather | solution.py:1260
  40.8 39.3 %plane_gather.4.normed_ref = bf16[2048,2048]{1,0:T(8,128)(2,1)} custom-call(bf16[256,2048]{1,0:T(8,128)(2,1)} %fusion.3.own_ref), custom_call_target="tpu_custom_call" | custom-call | bytes 251658240 | tf_op jit(solution)/shard_map/plane_gather/pallas_call | solution.py:239
  101.7 10.3 %collective-permute-done.11.refs_5_ = bf16[64,2048]{1,0:T(8,128)(2,1)S(1)} collective-permute-done((bf16[64,2048]{1,0:T(8,128)(2,1)}, bf16[64,2048]{1,0:T(8,128)(2,1)S(1)}, u32[]{:S(2)}, u32[]{:S(2)}) %collective-permute-start.11) | collective-permute-done | bytes 262176 | tf_op jit(solution)/shard_map/ppermute | solution.py:740
  117.6 39.2 %attention_forward.1 = (bf16[2048,256]{1,0:T(8,128)(2,1)}, bf16[2048,256]{1,0:T(8,128)(2,1)}, bf16[64,2048]{1,0:T(8,128)(2,1)}, bf16[2048,256]{1,0:T(8,128)(2,1)...) custom-call(s32[8]{0:T(128)} %and_select_fusion.first_ref, bf16[2048,2048]{1,0:T(8,128)(2,1)} %plane_gather.4.normed_ref, ...), custom_call_target="tpu_custom_call" | custom-call | flops 8589934592 | bytes 4194304 | tf_op jit(solution)/shard_map/attention_forward/pallas_call | solution.py:1051
  166.3 42.7 %product_scatter.3 = f32[256,2048]{1,0:T(8,128)} custom-call(bf16[2048,256]{1,0:T(8,128)(2,1)} %get-tuple-element.154.refs_0_.mixed_ref, bf16[256,2048]{1,0:T(8,128)(2,1)} %columns_together.1.refs_1_.weight_ref), custom_call_target="tpu_custom_call" | custom-call | bytes 251658240 | tf_op jit(solution)/shard_map/product_scatter/pallas_call | solution.py:538
  212.2 38.6 %plane_gather.5.normed_ref.refs_0_ = bf16[2048,2048]{1,0:T(8,128)(2,1)} custom-call(bf16[256,2048]{1,0:T(8,128)(2,1)} %multiply_convert_fusion.1.own_ref), custom_call_target="tpu_custom_call" | custom-call | bytes 251658240 | tf_op jit(solution)/shard_map/plane_gather/pallas_call | solution.py:239
  250.8 39.1 %plane_gather.6.gradient_ref.refs_2_ = bf16[2048,2048]{1,0:T(8,128)(2,1)} custom-call(bf16[256,2048]{1,0:T(8,128)(2,1)} %fusion.own_ref), custom_call_target="tpu_custom_call" | custom-call | bytes 251658240 | tf_op jit(solution)/shard_map/plane_gather/pallas_call | solution.py:239
  290.0 3.9 constant_dynamic-update-slice_fusion.down_ref.refs_3_
  293.8 19.5 %hidden_units.2 = (bf16[2048,512]{1,0:T(8,128)(2,1)}, bf16[2048,1024]{1,0:T(8,128)(2,1)}) custom-call(bf16[2048,2048]{1,0:T(8,128)(2,1)} %plane_gather.5.normed_ref.refs_0_, bf16[2048,2048]{1,0:T(8,128)(2,1)} %plane_gather.6.gradient_ref.refs_2_, bf16[2048,1024]{1,0:T(8,128)(2,1)} %all-gather.12.cloned.1.call-done.both_ref.refs_3_, ...), custom_call_target="tpu_custom_call" | custom-call | flops 12884901888 | bytes 23068672 | tf_op jit(solution)/shard_map/hidden_units/pallas_call | solution.py:898
  313.3 14.0 %convolution_convert_fusion = bf16[2048,1024]{1,0:T(8,128)(2,1)} fusion(bf16[2048,2048]{1,0:T(8,128)(2,1)} %plane_gather.5.normed_ref.refs_0_, bf16[2048,1024]{1,0:T(8,128)(2,1)} %get-tuple-element.184.refs_1_), kind=kOutput, calls=%fused_computation.7 | convolution fusion | flops 8592031744 | bytes 16777216 | tf_op jit(solution)/shard_map/dot_general | solution.py:39
  327.8 19.4 %hidden_units.3 = (bf16[2048,512]{1,0:T(8,128)(2,1)}, bf16[2048,1024]{1,0:T(8,128)(2,1)}) custom-call(bf16[2048,2048]{1,0:T(8,128)(2,1)} %plane_gather.5.normed_ref.refs_0_, bf16[2048,2048]{1,0:T(8,128)(2,1)} %plane_gather.6.gradient_ref.refs_2_, bf16[2048,1024]{1,0:T(8,128)(2,1)} %all-gather.14.cloned.1.call-done.both_ref.refs_4_, ...), custom_call_target="tpu_custom_call" | custom-call | flops 12884901888 | bytes 23068672 | tf_op jit(solution)/shard_map/hidden_units/pallas_call | solution.py:898
  347.2 53.5 %product_scatter.4 = (f32[256,2048]{1,0:T(8,128)}, bf16[2048,1024]{1,0:T(8,128)(2,1)}) custom-call(bf16[2048,2048]{1,0:T(8,128)(2,1)} %plane_gather.5.normed_ref.refs_0_, bf16[2048,1024]{1,0:T(8,128)(2,1)} %get-tuple-element.184.refs_1_, bf16[2048,1024]{1,0:T(8,128)(2,1)} %get-tuple-element.187.refs_2_, ...), custom_call_target="tpu_custom_call" | custom-call | bytes 251658240 | tf_op jit(solution)/shard_map/product_scatter/pallas_call | solution.py:538
  406.0 45.6 %plane_gather.7 = (bf16[2048,2048]{1,0:T(8,128)(2,1)}, bf16[1024,2048]{1,0:T(8,128)(2,1)}, bf16[1024,2048]{1,0:T(8,128)(2,1)}, bf16[1024,2048]{1,0:T(8,128)(2,1)}) custom-call(bf16[256,2048]{1,0:T(8,128)(2,1)} %get-tuple-element.189.own_ref, bf16[2048,512]{1,0:T(8,128)(2,1)} %get-tuple-element.190.refs_0_, bf16[2048,512]{1,0:T(8,128)(2,1)} %get-tuple-element.191.refs_1_, ...), custom_call_target="tpu_custom_call" | custom-call | bytes 4194304 | tf_op jit(solution)/shard_map/plane_gather/pallas_call | solution.py:239
  451.8 7.2 %collective-permute-done.14 = bf16[1024,2048]{1,0:T(8,128)(2,1)S(1)} collective-permute-done((bf16[1024,2048]{1,0:T(8,128)(2,1)}, bf16[1024,2048]{1,0:T(8,128)(2,1)S(1)}, u32[]{:S(2)}, u32[]{:S(2)}) %collective-permute-start.14) | collective-permute-done | bytes 4194336 | tf_op jit(solution)/shard_map/ppermute | solution.py:750
  459.1 4.5 add_convert_fusion
  469.7 52.1 %attention_backward.1 = (bf16[2048,384]{1,0:T(8,128)(2,1)}, bf16[256,2048]{1,0:T(8,128)(2,1)}) custom-call(s32[8]{0:T(128)} %and_select_fusion.first_ref, bf16[2048,256]{1,0:T(8,128)(2,1)} %get-tuple-element.163.query_ref, bf16[2048,256]{1,0:T(8,128)(2,1)} %get-tuple-element.164.key_ref, bf16[64,2048]{1,0:T(8,128)(2,1)} %get-tuple-element.165.key_columns_ref, ...), custom_call_target="tpu_custom_call" | custom-call | bytes 524288 | tf_op jit(solution)/shard_map/attention_backward/pallas_call | solution.py:1198
  524.1 4.2 all-to-all-start
  528.4 9.5 %convolution_convert_fusion.1 = bf16[2048,384]{1,0:T(8,128)(2,1)} fusion(bf16[2048,2048]{1,0:T(8,128)(2,1)} %plane_gather.4.normed_ref, bf16[2048,384]{1,0:T(8,128)(2,1)} %get-tuple-element.212.refs_0_), kind=kOutput, calls=%fused_computation.8 | convolution fusion | flops 3222011904 | bytes 11534336 | tf_op jit(solution)/shard_map/dot_general | solution.py:39
  547.4 4.5 collective-permute-done.19.refs_5_
  561.4 52.3 %product_scatter.5 = f32[256,2048]{1,0:T(8,128)} custom-call(bf16[2048,384]{1,0:T(8,128)(2,1)} %get-tuple-element.212.refs_0_, bf16[2048,640]{1,0:T(8,128)(2,1)} %all-gather.8.cloned.1.call-done.weight_ref.value_ref.refs_1_), custom_call_target="tpu_custom_call" | custom-call | bytes 4194304 | tf_op jit(solution)/shard_map/product_scatter/pallas_call | solution.py:538
  620.6 4.7 collective-permute-done.28.refs_13_
  631.1 4.2 units_together.1
  636.9 17.3 %finale.1 = (bf16[8,64,640]{2,1,0:T(8,128)(2,1)}, f32[8,128]{1,0:T(8,128)}) custom-call(bf16[512,640]{1,0:T(8,128)(2,1)} %reduce-scatter.9.cloned.1.call-done.packed_ref, f32[8,8,128]{2,1,0:T(8,128)} %pad.4.part_ref), custom_call_target="tpu_custom_call" | custom-call | bytes 40000000 | tf_op jit(solution)/shard_map/finale/pallas_call | solution.py:653
  (223 shorter events, 100.8 us)
Async XLA Ops:
  7.2 33.6 %all-gather.6.cloned.1.call-start = ((), (), s32[]{:S(2)}) async-start(), calls=%async_computation.5 | async-start | bytes 1310720 | tf_op jit(solution)/shard_map/all_gather | solution.py:1260
  9.0 87.8 %all-gather.8.cloned.1.call-start = ((), (), s32[]{:S(2)}) async-start(), calls=%async_computation.6 | async-start | bytes 3276800 | tf_op jit(solution)/shard_map/all_gather | solution.py:1260
  25.6 186.6 %all-gather.10.cloned.1.call-start = ((), (), s32[]{:S(2)}) async-start(), calls=%async_computation.7 | async-start | bytes 3932160 | tf_op jit(solution)/shard_map/all_gather | solution.py:1260
  80.1 213.7 %all-gather.12.cloned.1.call-start = ((), (), s32[]{:S(2)}) async-start(), calls=%async_computation.8 | async-start | bytes 5242880 | tf_op jit(solution)/shard_map/all_gather | solution.py:1260
  112.0 44.9 %collective-permute-start.2 = (bf16[256,256]{1,0:T(8,128)(2,1)}, bf16[256,256]{1,0:T(8,128)(2,1)S(1)}, u32[]{:S(2)}, u32[]{:S(2)}) collective-permute-start(bf16[256,256]{1,0:T(8,128)(2,1)} %get-tuple-element.140), channel_id=1, source_target_pairs={{0,3},{1,2},{2,1},{3,0},{4,7},{5,6},{6,5},{7,4},{8,11},{9,10},{10,... | collective-permute-start | bytes 393224 | tf_op jit(solution)/shard_map/ppermute | solution.py:740
  113.2 43.7 %collective-permute-start.3 = (bf16[256,256]{1,0:T(8,128)(2,1)}, bf16[256,256]{1,0:T(8,128)(2,1)S(1)}, u32[]{:S(2)}, u32[]{:S(2)}) collective-permute-start(bf16[256,256]{1,0:T(8,128)(2,1)} %get-tuple-element.141), channel_id=1, source_target_pairs={{0,4},{1,5},{2,6},{3,7},{4,0},{5,1},{6,2},{7,3},{8,12},{9,13},{10,... | collective-permute-start | bytes 393224 | tf_op jit(solution)/shard_map/ppermute | solution.py:740
  114.2 42.8 %collective-permute-start.4 = (bf16[256,256]{1,0:T(8,128)(2,1)}, bf16[256,256]{1,0:T(8,128)(2,1)S(1)}, u32[]{:S(2)}, u32[]{:S(2)}) collective-permute-start(bf16[256,256]{1,0:T(8,128)(2,1)} %get-tuple-element.142), channel_id=1, source_target_pairs={{0,5},{1,4},{2,7},{3,6},{4,1},{5,0},{6,3},{7,2},{8,13},{9,12},{10,... | collective-permute-start | bytes 393224 | tf_op jit(solution)/shard_map/ppermute | solution.py:740
  114.6 42.4 %collective-permute-start.5 = (bf16[256,256]{1,0:T(8,128)(2,1)}, bf16[256,256]{1,0:T(8,128)(2,1)S(1)}, u32[]{:S(2)}, u32[]{:S(2)}) collective-permute-start(bf16[256,256]{1,0:T(8,128)(2,1)} %get-tuple-element.143), channel_id=1, source_target_pairs={{0,6},{1,7},{2,4},{3,5},{4,2},{5,3},{6,0},{7,1},{8,14},{9,15},{10,... | collective-permute-start | bytes 393224 | tf_op jit(solution)/shard_map/ppermute | solution.py:740
  115.7 41.2 %collective-permute-start.6 = (bf16[256,256]{1,0:T(8,128)(2,1)}, bf16[256,256]{1,0:T(8,128)(2,1)S(1)}, u32[]{:S(2)}, u32[]{:S(2)}) collective-permute-start(bf16[256,256]{1,0:T(8,128)(2,1)} %get-tuple-element.144), channel_id=1, source_target_pairs={{0,7},{1,6},{2,5},{3,4},{4,3},{5,2},{6,1},{7,0},{8,15},{9,14},{10,... | collective-permute-start | bytes 393224 | tf_op jit(solution)/shard_map/ppermute | solution.py:740
  160.8 167.1 %all-gather.14.cloned.1.call-start = ((), (), s32[]{:S(2)}) async-start(), calls=%async_computation.9 | async-start | bytes 5242880 | tf_op jit(solution)/shard_map/all_gather | solution.py:1260
  161.4 244.7 %reduce-scatter.5.cloned.1.call-start = ((), (), s32[]{:S(2)}) async-start(), calls=%async_computation.10 | async-start | bytes 5242880 | tf_op jit(solution)/shard_map/reduce_scatter | solution.py:1256
  327.3 228.3 %reduce-scatter.11.cloned.1.call-start = ((), (), s32[]{:S(2)}) async-start(), calls=%async_computation.13 | async-start | bytes 5242880 | tf_op jit(solution)/shard_map/reduce_scatter | solution.py:1256
  400.8 219.8 %reduce-scatter.7.cloned.1.call-start = ((), (), s32[]{:S(2)}) async-start(), calls=%async_computation.11 | async-start | bytes 5242880 | tf_op jit(solution)/shard_map/reduce_scatter | solution.py:1256
  463.6 88.3 %collective-permute-start.22 = (bf16[512,2048]{1,0:T(8,128)(2,1)}, bf16[512,2048]{1,0:T(8,128)(2,1)}, u32[]{:S(2)}, u32[]{:S(2)}) collective-permute-start(bf16[512,2048]{1,0:T(8,128)(2,1)} %get-tuple-element.268), channel_id=1, source_target_pairs={{0,4},{1,3},{2,6},{3,1},{4,0},{5,7},{6,2},{7,5},{8,12},{9,11},{10,... | collective-permute-start | bytes 6291464 | tf_op jit(solution)/shard_map/ppermute | solution.py:750
  466.8 71.1 %collective-permute-start.15 = (bf16[64,1024]{1,0:T(8,128)(2,1)}, bf16[64,1024]{1,0:T(8,128)(2,1)S(1)}, u32[]{:S(2)}, u32[]{:S(2)}) collective-permute-start(bf16[64,1024]{1,0:T(8,128)(2,1)} %get-tuple-element.201), channel_id=1, source_target_pairs={{0,1},{1,0},{2,3},{3,2},{4,5},{5,4},{6,7},{7,6},{8,9},{9,8},{10,11... | collective-permute-start | bytes 393224 | tf_op jit(solution)/shard_map/ppermute | solution.py:740
  466.8 72.8 %collective-permute-start.16 = (bf16[64,1024]{1,0:T(8,128)(2,1)}, bf16[64,1024]{1,0:T(8,128)(2,1)S(1)}, u32[]{:S(2)}, u32[]{:S(2)}) collective-permute-start(bf16[64,1024]{1,0:T(8,128)(2,1)} %get-tuple-element.202), channel_id=1, source_target_pairs={{0,2},{1,3},{2,0},{3,1},{4,6},{5,7},{6,4},{7,5},{8,10},{9,11},{10,... | collective-permute-start | bytes 393224 | tf_op jit(solution)/shard_map/ppermute | solution.py:740
  467.8 73.2 %collective-permute-start.17 = (bf16[64,1024]{1,0:T(8,128)(2,1)}, bf16[64,1024]{1,0:T(8,128)(2,1)S(1)}, u32[]{:S(2)}, u32[]{:S(2)}) collective-permute-start(bf16[64,1024]{1,0:T(8,128)(2,1)} %get-tuple-element.203), channel_id=1, source_target_pairs={{0,3},{1,2},{2,1},{3,0},{4,7},{5,6},{6,5},{7,4},{8,11},{9,10},{10,... | collective-permute-start | bytes 393224 | tf_op jit(solution)/shard_map/ppermute | solution.py:740
  468.6 78.8 %collective-permute-start.18 = (bf16[64,1024]{1,0:T(8,128)(2,1)}, bf16[64,1024]{1,0:T(8,128)(2,1)}, u32[]{:S(2)}, u32[]{:S(2)}) collective-permute-start(bf16[64,1024]{1,0:T(8,128)(2,1)} %get-tuple-element.204), channel_id=1, source_target_pairs={{0,4},{1,5},{2,6},{3,7},{4,0},{5,1},{6,2},{7,3},{8,12},{9,13},{10,... | collective-permute-start | bytes 393224 | tf_op jit(solution)/shard_map/ppermute | solution.py:740
  528.4 108.5 %reduce-scatter.9.cloned.1.call-start = ((), (), s32[]{:S(2)}) async-start(), calls=%async_computation.12 | async-start | bytes 3276800 | tf_op jit(solution)/shard_map/reduce_scatter | solution.py:1256
  554.9 60.4 %collective-permute-start.23 = (bf16[256,2048]{1,0:T(8,128)(2,1)}, bf16[256,2048]{1,0:T(8,128)(2,1)}, u32[]{:S(2)}, u32[]{:S(2)}) collective-permute-start(bf16[256,2048]{1,0:T(8,128)(2,1)} %add_convert_fusion.3), channel_id=1, source_target_pairs={{0,2},{1,5},{2,0},{3,7},{4,6},{5,1},{6,4},{7,3},{8,10},{9,13},{10,... | collective-permute-start | bytes 3145736 | tf_op jit(solution)/shard_map/ppermute | solution.py:750
  557.9 55.8 %collective-permute-start.24 = (bf16[64,1024]{1,0:T(8,128)(2,1)}, bf16[64,1024]{1,0:T(8,128)(2,1)S(1)}, u32[]{:S(2)}, u32[]{:S(2)}) collective-permute-start(bf16[64,1024]{1,0:T(8,128)(2,1)} %get-tuple-element.232), channel_id=1, source_target_pairs={{0,1},{1,0},{2,3},{3,2},{4,5},{5,4},{6,7},{7,6},{8,9},{9,8},{10,11... | collective-permute-start | bytes 393224 | tf_op jit(solution)/shard_map/ppermute | solution.py:740
  557.9 55.9 %collective-permute-start.25 = (bf16[64,1024]{1,0:T(8,128)(2,1)}, bf16[64,1024]{1,0:T(8,128)(2,1)S(1)}, u32[]{:S(2)}, u32[]{:S(2)}) collective-permute-start(bf16[64,1024]{1,0:T(8,128)(2,1)} %get-tuple-element.233), channel_id=1, source_target_pairs={{0,2},{1,3},{2,0},{3,1},{4,6},{5,7},{6,4},{7,5},{8,10},{9,11},{10,... | collective-permute-start | bytes 393224 | tf_op jit(solution)/shard_map/ppermute | solution.py:740
  559.9 60.6 %collective-permute-start.26 = (bf16[64,1024]{1,0:T(8,128)(2,1)}, bf16[64,1024]{1,0:T(8,128)(2,1)S(1)}, u32[]{:S(2)}, u32[]{:S(2)}) collective-permute-start(bf16[64,1024]{1,0:T(8,128)(2,1)} %get-tuple-element.234), channel_id=1, source_target_pairs={{0,3},{1,2},{2,1},{3,0},{4,7},{5,6},{6,5},{7,4},{8,11},{9,10},{10,... | collective-permute-start | bytes 393224 | tf_op jit(solution)/shard_map/ppermute | solution.py:740
  560.5 60.1 %collective-permute-start.27 = (bf16[64,1024]{1,0:T(8,128)(2,1)}, bf16[64,1024]{1,0:T(8,128)(2,1)}, u32[]{:S(2)}, u32[]{:S(2)}) collective-permute-start(bf16[64,1024]{1,0:T(8,128)(2,1)} %get-tuple-element.235), channel_id=1, source_target_pairs={{0,4},{1,5},{2,6},{3,7},{4,0},{5,1},{6,2},{7,3},{8,12},{9,13},{10,... | collective-permute-start | bytes 393224 | tf_op jit(solution)/shard_map/ppermute | solution.py:740
  (57 other events, 935.4 us)
Sparse Core Ops, SparseCore 0:
  10.2 30.6 all-gather.5
  42.4 54.2 all-gather.7
  98.3 62.2 all-gather.9
  162.6 79.6 all-gather.11
  243.7 79.2 all-gather.13
  327.5 77.8 reduce-scatter.4
  407.7 77.2 reduce-scatter.10
  487.3 77.2 reduce-scatter.6
  567.0 52.6 reduce-scatter.8

commit v5 on v4

--- a/solution.py
+++ b/solution.py
@@ -75,7 +75,8 @@
 def gather_kernel(member_count, in_order, count, own_ref, *refs):
     operands = refs[: count + 2] if count else ()
     refs = refs[len(operands) :]
-    all_ref, results, refs = refs[0], refs[1 : 4 if count else 1], refs[4 if count else 1 :]
+    extra = 4 if count else 1
+    all_ref, results, refs = refs[0], refs[1:extra], refs[extra:]
     link_send, link_recv, core_send, core_recv, local_sem = refs[:5]
     group = lax.axis_index("dp")
     member = lax.axis_index("fsdp")
@@ -126,60 +127,77 @@
         core_copy(0, part).start()
     tiles = []
     if count:
-        helds = refs[5 : 7 + count]
-        down_grad, out_sibling, out_own, turned = refs[7 + count : 11 + count]
-        load_sem, store_sem = refs[11 + count :]
-        hiddens, gradient, down = helds[:count], helds[count], helds[count + 1]
-        units = hiddens[0].shape[1]
+        hidden, gradient, down, down_grad, out_sibling, out_own, turned, out_arrived = refs[5:13]
+        load_sem, store_sem, out_send, out_recv = refs[13:]
+        units = operands[0].shape[1]
+        targets = [hidden.at[:, pl.ds(number * units, units)] for number in range(count)]
         loads = [
             pltpu.make_async_copy(source, target, load_sem.at[number])
-            for number, (source, target) in enumerate(zip(operands, helds))
+            for number, (source, target) in enumerate(zip(operands, (*targets, gradient, down)))
         ]
+        half = out_own.shape[0]
+        finished = (
+            down_grad,
+            out_own.at[pl.ds(half // 2, half // 2)],
+            out_own.at[pl.ds(0, half // 2)],
+        )
         stores = [
             pltpu.make_async_copy(source, target, store_sem.at[number])
-            for number, (source, target) in enumerate(
-                zip((down_grad, out_sibling, out_own), results)
-            )
+            for number, (source, target) in enumerate(zip(finished, results))
         ]
         for load in loads:
             load.start()
-        half = out_own.shape[0]
         width = 256
 
-        def out_tile(target, base, column):
-            total = None
-            for number in range(count):
-                term = dot_nn(
-                    hiddens[number][base : base + half, :],
-                    down[number * units : (number + 1) * units, column : column + width],
-                )
-                total = term if total is None else total + term
-            target[:, column : column + width] = total.astype(BF16)
+        def out_copy(column):
+            where = pl.ds(column, width)
+            return pltpu.make_async_remote_copy(
+                out_sibling.at[:, where],
+                out_arrived.at[:, where],
+                out_send.at[column // width],
+                out_recv.at[column // width],
+                device_id=(group, flip(member, 1)),
+                device_id_type=MESH,
+            )
+
+        def sibling_tile(column):
+            out_sibling[:, column : column + width] = dot_nn(
+                hidden[half:, :], down[:, column : column + width]
+            ).astype(BF16)
+            out_copy(column).start()
+
+        def own_tile(column):
+            product = dot_nn(hidden[:half, :], down[:, column : column + width])
+            out_copy(column).wait()
+            out_own[:, column : column + width] = (
+                product + out_arrived[:, column : column + width].astype(F32)
+            ).astype(BF16)
 
         def turn_tile(number):
-            turned[...] = jnp.transpose(hiddens[number][...])
-
-        def grad_tile(number, column):
-            down_grad[number * units : (number + 1) * units, column : column + width] = dot_nn(
+            part = slice(number * units, (number + 1) * units)
+            turned[part, :] = jnp.transpose(hidden[:, part])
+
+        def grad_tile(column):
+            down_grad[:, column : column + width] = dot_nn(
                 turned[...], gradient[:, column : column + width]
             ).astype(BF16)
 
         for load in loads[:count] + loads[count + 1 :]:
             tiles.append(load.wait)
-        for target, base, store in (
-            (out_sibling, half, stores[1]),
-            (out_own, 0, stores[2]),
-        ):
-            for column in range(0, down.shape[1], width):
-                tiles.append(functools.partial(out_tile, target, base, column))
-            tiles.append(store.start)
+        starts = range(0, down.shape[1], width)
+        for column in starts:
+            tiles.append(functools.partial(sibling_tile, column))
+        for column in starts:
+            tiles.append(functools.partial(own_tile, column))
+        tiles += [stores[1].start, stores[2].start]
         tiles.append(loads[count].wait)
         for number in range(count):
             tiles.append(functools.partial(turn_tile, number))
-            for column in range(0, down.shape[1], width):
-                tiles.append(functools.partial(grad_tile, number, column))
+        for column in starts:
+            tiles.append(functools.partial(grad_tile, column))
         tiles.append(stores[0].start)
-    shares = [1 << step for step in range(steps) for part in range(PIECES)]
+    shares = [4] * PIECES + [2, 1, 0, 0] * max(1, steps - 1)
+    shares = shares[: steps * PIECES]
     ends = [-(-len(tiles) * sum(shares[: n + 1]) // sum(shares)) for n in range(len(shares))]
 
     turn = 0
@@ -227,15 +245,29 @@
         hiddens, gradient, down = extras
         count = len(hiddens)
         operands += [*hiddens, gradient, down]
-        scratch += [pltpu.VMEM(value.shape, BF16) for value in operands[1:]]
+        units = down.shape[0]
+        scratch += [
+            pltpu.VMEM((total, units), BF16),
+            pltpu.VMEM(gradient.shape, BF16),
+            pltpu.VMEM(down.shape, BF16),
+        ]
         out_shape += [
             jax.ShapeDtypeStruct((down.shape[0], gradient.shape[1]), BF16),
-            jax.ShapeDtypeStruct((total // 2, down.shape[1]), BF16),
-            jax.ShapeDtypeStruct((total // 2, down.shape[1]), BF16),
+            jax.ShapeDtypeStruct((total // 4, down.shape[1]), BF16),
+            jax.ShapeDtypeStruct((total // 4, down.shape[1]), BF16),
         ]
-        scratch += [pltpu.VMEM(value.shape, BF16) for value in out_shape[1:]]
-        scratch.append(pltpu.VMEM(hiddens[0].shape[::-1], BF16))
-        scratch += [pltpu.SemaphoreType.DMA((count + 2,)), pltpu.SemaphoreType.DMA((3,))]
+        out_half = pltpu.VMEM((total // 2, down.shape[1]), BF16)
+        scratch += [
+            pltpu.VMEM(out_shape[1].shape, BF16),
+            out_half,
+            out_half,
+            pltpu.VMEM((units, total), BF16),
+            out_half,
+            pltpu.SemaphoreType.DMA((count + 2,)),
+            pltpu.SemaphoreType.DMA((3,)),
+            pltpu.SemaphoreType.DMA((down.shape[1] // 256,)),
+            pltpu.SemaphoreType.DMA((down.shape[1] // 256,)),
+        ]
     result = pl.pallas_call(
         functools.partial(gather_kernel, member_count, in_order, count),
         out_shape=out_shape,
@@ -323,7 +355,9 @@
         held_other, held_grad, other_sem, grad_sem = refs[-4:]
         refs = refs[1 : 2 * count + 2] + refs[2 * count + 3 : -4]
     lefts, rights, sum_ref = refs[:count], refs[count : 2 * count], refs[2 * count]
-    held_lefts, held_rights = refs[2 * count + 1 : 3 * count + 1], refs[3 * count + 1 : 4 * count + 1]
+    held_left, held_right = refs[2 * count + 1 : 2 * count + 3]
+    depths = [left.shape[1] for left in lefts]
+    offsets = [sum(depths[:number]) for number in range(count)]
     (
         outgoing,
         core_buffer,
@@ -335,7 +369,7 @@
         link_recv,
         core_send,
         core_recv,
-    ) = refs[4 * count + 1 :]
+    ) = refs[2 * count + 3 :]
     group = lax.axis_index("dp")
     member = lax.axis_index("fsdp")
     sibling = flip(member, 1)
@@ -350,37 +384,48 @@
         block = walk(owner, subset, masks) if in_order else subset + side * blocks
         return pltpu.make_async_copy(
             lefts[number].at[pl.ds(pl.multiple_of(block * rows, rows), rows)],
-            held_lefts[number].at[pl.ds((side * blocks + subset) * rows, rows)],
+            held_left.at[
+                pl.ds((side * blocks + subset) * rows, rows), pl.ds(offsets[number], depths[number])
+            ],
             left_sem.at[number, side, subset],
         )
 
-    def right_copy(number):
-        source = rights[number]
-        if transposed and source.shape[1] != held_rights[number].shape[1]:
-            source = source.at[:, pl.ds(0, held_rights[number].shape[1])]
-        return pltpu.make_async_copy(source, held_rights[number], right_sem.at[number])
-
-    for number in range(count):
-        right_copy(number).start()
-        for side in (1, 0):
+    def right_copy(number, index):
+        where = pl.ds(pl.multiple_of(index * piece, piece), piece)
+        source, there = rights[number], pl.ds(offsets[number], depths[number])
+        if transposed:
+            return pltpu.make_async_copy(
+                source.at[where, pl.ds(0, depths[number])],
+                held_right.at[where, there],
+                right_sem.at[number, index],
+            )
+        return pltpu.make_async_copy(
+            source.at[:, where], held_right.at[there, where], right_sem.at[number, index]
+        )
+
+    def load_side(side):
+        for number in range(count):
             for subset in range(blocks):
                 left_copy(number, side, subset).start()
-    if with_grad:
-        other_copy = pltpu.make_async_copy(other_ref, held_other, other_sem)
-        other_copy.start()
+
+    def wait_side(side):
+        for number in range(count):
+            for subset in range(blocks):
+                left_copy(number, side, subset).wait()
+
+    def load_right(index):
+        for number in range(count):
+            right_copy(number, index).start()
+
+    load_side(1)
+    load_right(0)
     greet(group, member, masks)
 
     def part(side, subset, where):
-        where_rows = pl.ds((side * blocks + subset) * rows, rows)
-        total = None
-        for number in range(count):
-            left = held_lefts[number][where_rows, :]
-            if transposed:
-                term = dot_nt(left, held_rights[number][where, :])
-            else:
-                term = dot_nn(left, held_rights[number][:, where])
-            total = term if total is None else total + term
-        return total
+        left = held_left[pl.ds((side * blocks + subset) * rows, rows), :]
+        if transposed:
+            return dot_nt(left, held_right[where, :])
+        return dot_nn(left, held_right[:, where])
 
     def columns(index):
         return pl.ds(pl.multiple_of(index * piece, piece), piece)
@@ -411,14 +456,11 @@
 
     order = sorted(range(blocks), key=lambda s: (-(s & 1), -s))
 
-    for number in range(count):
-        right_copy(number).wait()
-        for side in (1, 0):
-            for subset in range(blocks):
-                left_copy(number, side, subset).wait()
-
     def for_sibling(index):
         where = columns(index)
+        for number in range(count):
+            right_copy(number, index).wait()
+        pl.when(index + 1 < pieces)(lambda: load_right(index + 1))
         for subset in range(blocks):
             outgoing[pl.ds(subset * rows, rows), where] = part(1, subset, where).astype(BF16)
         core_copy(index).start()
@@ -441,7 +483,13 @@
         for_links(index - 1)
         return carried
 
+    wait_side(1)
+    load_side(0)
     for_sibling(0)
+    wait_side(0)
+    if with_grad:
+        other_copy = pltpu.make_async_copy(other_ref, held_other, other_sem)
+        other_copy.start()
     lax.fori_loop(1, pieces, for_both, 0)
     for_links(pieces - 1)
     if with_grad:
@@ -451,7 +499,10 @@
 
     def grad_tile(index):
         where = pl.ds(pl.multiple_of(index * units, units), units)
-        turned = dot_tn(held_lefts[-1][:, where], held_other[...])
+        turned = dot_tn(
+            held_left[:, pl.ds(pl.multiple_of(offsets[-1] + index * units, units), units)],
+            held_other[...],
+        )
         held_grad[:, where] = jnp.transpose(turned.astype(BF16))
 
     for step in range(steps):
@@ -503,10 +554,9 @@
     blocks = 1 << len(plane_masks(member_count))
     depth = sum(left.shape[1] for left in lefts)
     scratch = (
-        [pltpu.VMEM(left.shape, BF16) for left in lefts]
-        + [
-            pltpu.VMEM((right.shape[0], left.shape[1]) if transposed else right.shape, BF16)
-            for left, right in zip(lefts, rights)
+        [
+            pltpu.VMEM((total, depth), BF16),
+            pltpu.VMEM((width, depth) if transposed else (depth, width), BF16),
         ]
         + [
             pltpu.VMEM((blocks * rows, width), BF16),
@@ -514,7 +564,7 @@
             pltpu.VMEM((blocks * rows, width), BF16),
             pltpu.VMEM(((blocks - 1) * rows, width), BF16),
             pltpu.SemaphoreType.DMA((count, 2, blocks)),
-            pltpu.SemaphoreType.DMA((count,)),
+            pltpu.SemaphoreType.DMA((count, SCATTER_PIECES)),
             pltpu.SemaphoreType.DMA((blocks - 1, SCATTER_PIECES)),
             pltpu.SemaphoreType.DMA((blocks - 1, SCATTER_PIECES)),
             pltpu.SemaphoreType.DMA((SCATTER_PIECES,)),
@@ -797,7 +847,7 @@
     return local_call(kernel, "units_apart", [shape] * member_count, member, gate, up, gain)
 
 
-def units_together(member, chunk_blocks, gain, member_count, group_count):
+def units_together(member, chunk_blocks, gain, down, member_count, group_count):
     chunks = len(chunk_blocks)
     shard, columns = chunk_blocks[0][0].shape
     per = columns * chunks // (2 * group_count)
@@ -817,10 +867,11 @@
                             result, piece.astype(F32) * gain, base + other * per, 1
                         )
             results.append(result)
-        return results
-
-    def kernel(member_ref, gain_ref, *refs):
+        return *results, down.astype(F32)
+
+    def kernel(member_ref, gain_ref, down_ref, *refs):
         outs = refs[len(blocks) :]
+        outs[2][...] = down_ref[...].astype(F32)
         for away in range(member_count):
             other = member_ref[0] ^ away
             for chunk, side, column, base in strips:
@@ -829,7 +880,8 @@
                 outs[side][:, where] = piece.astype(F32) * gain_ref[...]
 
     shape = jax.ShapeDtypeStruct((shard, width), F32)
-    return local_call(kernel, "units_together", [shape] * 2, member, gain, *blocks)
+    shapes = [shape, shape, jax.ShapeDtypeStruct(down.shape, F32)]
+    return local_call(kernel, "units_together", shapes, member, gain, down, *blocks)
 
 
 def heads_together(member, arrived, gain, heads):
@@ -1235,6 +1287,33 @@
     )(first, query, keys, key_columns, values, mixed, grad, weight, lse, start, table)
 
 
+def projection_grad(normed, grad, out_grad):
+    tokens, model = normed.shape
+    columns, more = grad.shape[1], out_grad.shape[1]
+    tile = 512
+
+    def kernel(normed_ref, grad_ref, out_grad_ref, result_ref):
+        result_ref[:, :columns] = dot_tn(normed_ref[...], grad_ref[...]).astype(BF16)
+        result_ref[:, columns:] = out_grad_ref[...]
+
+    return pl.pallas_call(
+        kernel,
+        grid=(model // tile,),
+        in_specs=[
+            pl.BlockSpec((tokens, tile), lambda i: (0, i)),
+            pl.BlockSpec((tokens, columns), lambda i: (0, 0)),
+            pl.BlockSpec((tile, more), lambda i: (i, 0)),
+        ],
+        out_specs=pl.BlockSpec((tile, columns + more), lambda i: (i, 0)),
+        out_shape=jax.ShapeDtypeStruct((model, columns + more), BF16),
+        compiler_params=pltpu.CompilerParams(vmem_limit_bytes=VMEM_BYTES),
+        cost_estimate=pl.CostEstimate(
+            flops=2 * tokens * model * columns, bytes_accessed=2 * tokens * model, transcendentals=0
+        ),
+        name="projection_grad",
+    )(normed, grad, out_grad)
+
+
 def token_starts(lengths_row, group_tokens):
     count = lengths_row.shape[0]
     order = jnp.arange(count, dtype=jnp.int32)
@@ -1312,26 +1391,6 @@
     packed_in = packed_in.reshape(members * shard, columns + out_columns)
     inputs = tokens.astype(F32)
     inverse_one = inverse_norm(inputs)
-    early = model // 4
-    down_early = gather_groups(down_weight[:, :early])
-    normed_one = plane_gather(
-        after((inputs * inverse_one).astype(BF16), packed_in, down_early), members, 0, True
-    )
-    packed = gather_groups(packed_in)
-    upstream = cotangent.astype(F32)
-    down_rest = gather_groups(after(down_weight[:, early:], normed_one))
-    gate_up = exchanged(
-        units_apart(
-            member,
-            after(gate_weight, normed_one),
-            up_weight,
-            gain_two,
-            members,
-            groups,
-            CHUNKS,
-        )
-    )
-
     start, place = token_starts(lengths[0], group_tokens)
     first = start[::BLOCK] // BLOCK
     frequency = ROPE_BASE ** (-(2.0 * jnp.arange(HALF, dtype=F32)) / HD)
@@ -1339,27 +1398,38 @@
     table = jnp.concatenate([jnp.cos(angles), jnp.sin(angles)], axis=1)
     start = start[None, :]
 
+    gate_up = exchanged(
+        units_apart(
+            member, after(gate_weight, packed_in), up_weight, gain_two, members, groups, CHUNKS
+        )
+    )
+    packed = gather_groups(packed_in)
+    down_all = gather_groups(down_weight)
+    normed_one = plane_gather(
+        after((inputs * inverse_one).astype(BF16), packed_in), members, 0, True
+    )
+    upstream = cotangent.astype(F32)
+    grad_two = (RESIDUAL_SCALE * upstream).astype(BF16)
+    grad_two, down_all, table, first, start, _ = lax.optimization_barrier(
+        (grad_two, down_all, table, first, start, normed_one)
+    )
+    grad_two = plane_gather(grad_two, members, 9, False)
+    gate_up, grad_two = lax.optimization_barrier((gate_up, grad_two))
+    gate_up_parts = rows_together(member, gate_up, CHUNKS)
+    gate_up_chunks = [gather_groups(part) for part in gate_up_parts]
+    packed, gate_up_parts = lax.optimization_barrier((packed, gate_up_parts))
+
     out_blocks = exchanged(rows_apart(member, packed, members, columns))
     query, keys, key_columns, values, mixed, lse = attention_forward(
         first, normed_one, packed, table, start, heads
     )
-    mixed_then, out_blocks, gate_up = lax.optimization_barrier((mixed, out_blocks, gate_up))
-    gate_up_chunks = [
-        gather_groups(part) for part in rows_together(member, gate_up, CHUNKS)
-    ]
+    mixed_then, out_blocks = lax.optimization_barrier((mixed, out_blocks))
     out_piece = columns_together(member, out_blocks)
     branch_one = product_scatter([mixed_then], [out_piece], False, members, 2, True)
     residual = inputs + RESIDUAL_SCALE * branch_one
 
     inverse_two = inverse_norm(residual)
-    normed_two, down_rest = lax.optimization_barrier(
-        ((residual * inverse_two).astype(BF16), down_rest)
-    )
-    normed_two = plane_gather(normed_two, members, 3, False)
-    grad_two = plane_gather(
-        after((RESIDUAL_SCALE * upstream).astype(BF16), normed_two), members, 9, False
-    )
-    down_all = jnp.concatenate([down_early, after(down_rest, grad_two)], axis=1)
+    normed_two = plane_gather((residual * inverse_two).astype(BF16), members, 3, False)
     fused = group_tokens <= 2048
     hiddens = []
     grad_boths = []
@@ -1389,34 +1459,25 @@
     )
     gain_term_two = jnp.sum(weighted_two * residual * inverse_two, axis=0)
 
-    grad_one, gate_up_grads[0] = lax.optimization_barrier(
-        ((RESIDUAL_SCALE * grad_residual).astype(BF16), gate_up_grads[0])
-    )
-    grad_one, down_grad, out_sibling, out_own = plane_gather(
-        grad_one, members, 5, True, (hiddens, grad_two, down_all)
+    grad_one, down_grad, out_high, out_kept = plane_gather(
+        (RESIDUAL_SCALE * grad_residual).astype(BF16),
+        members,
+        5,
+        True,
+        (hiddens, grad_two, down_all),
     )
     down_grad = sum_over_groups(down_grad)
-    half_rows = group_tokens // 2
-    out_sibling = send_to(out_sibling, members, lambda m: m ^ 1)
-    gate_up_grads[0] = exchanged(rows_apart(member, gate_up_grads[0], members))
-    grad_one, out_own, out_sibling = lax.optimization_barrier(
-        (grad_one, out_own, out_sibling)
+    gate_up_grads[0] = exchanged(
+        rows_apart(member, after(gate_up_grads[0], grad_one), members)
     )
     steps = len(plane_masks(members))
-    half_rows //= 2
-    out_sent = send_to(
-        added(out_own[half_rows:], out_sibling[half_rows:]).astype(BF16),
-        members,
-        hopped(steps - 1, members),
-    )
-    out_kept = added(out_own[:half_rows], out_sibling[:half_rows]).astype(BF16)
+    half_rows = group_tokens // 4
+    out_sent = send_to(out_high, members, hopped(steps - 1, members))
     grad_projected, out_grad = attention_backward(
         first, query, keys, key_columns, values, mixed, grad_one, out_piece, lse, start, table
     )
     out_grad = lax.all_to_all(out_grad, "fsdp", split_axis=1, concat_axis=0, tiled=True)
-    packed_grad = jnp.concatenate(
-        [dot_tn(normed_one, grad_projected).astype(BF16), out_grad], axis=1
-    )
+    packed_grad = projection_grad(normed_one, grad_projected, out_grad)
     gate_up_grads[1:] = [
         exchanged(rows_apart(member, part, members))
         for part in after(gate_up_grads[1:], grad_projected)
@@ -1453,8 +1514,8 @@
     )
     output = (residual + RESIDUAL_SCALE * added(out_kept, out_sent)).astype(BF16)
 
-    gate_grad, up_grad = units_together(
-        member, after(gate_up_grads, weighted_one), gain_two, members, groups
+    gate_grad, up_grad, down_grad = units_together(
+        member, after(gate_up_grads, weighted_one), gain_two, down_grad, members, groups
     )
     arrived, gains = finale(packed_grad, gains, groups, 8)
     query_grad, key_grad, value_grad, out_grad = heads_together(member, arrived, gain_one, heads)
@@ -1469,7 +1530,7 @@
         out_grad,
         gate_grad,
         up_grad,
-        down_grad.astype(F32),
+        down_grad,
         gains[0] / gain_one[:, 0],
         gains[1] / gain_two[:, 0],
     )

time: 676 us -> 644 us (0.953)
  waiting for transfers between devices: 42.1 us -> 29.8 us
  other arithmetic: 41 us -> 30.8 us
  Pallas kernels: 493 us -> 503 us
  matrix products: 23.5 us -> 14 us
  local copies, waits for them, and re-layouts: 16.2 us -> 8.28 us
    pallas_call x3, Pallas kernels: 148 us -> 138 us  [product_scatter(): pl.pallas_call(functools.partial(product_scatter_kernel, member_count, in...]
    pallas_call x4, Pallas kernels: 163 us -> 173 us  [plane_gather(): pl.pallas_call(functools.partial(gather_kernel, member_count, in_order, c...]
    dot_general x2 -> x1, matrix products: 23.5 us -> 14 us  [dot_tn(): lax.dot_general(left, right, (((0,), (0,)), ((), ())), preferred_element_...]
    pallas_call x0 -> x1, Pallas kernels: none -> 8.84 us  [projection_grad(): pl.pallas_call(kernel, grid=(model // tile,), in_specs=[pl.BlockSpec((tok...]
    convert_element_type x3 -> x1, other arithmetic: 8.62 us -> 1.22 us  [body(): grad_two = (RESIDUAL_SCALE * upstream).astype(BF16)]
    ppermute x28, waiting for transfers between devices: 20.1 us -> 13 us  [exchanged(): lax.ppermute(blocks[away], 'fsdp', [(m, m ^ away) for m in range(len(bloc...]
  transfers between devices with their start and end apart: 41 -> 39, of which waited for: 8 -> 7; matrix products, arithmetic and copies ran while one was open for 11% -> 8% of each run, Pallas kernels for 71% -> 77%
where the time goes in v5:
time: 644 us; the launch traced here: 635 us
  Pallas kernels  503 us (78%)
  starting transfers between devices  34.1 us (5%)
  other arithmetic  30.8 us (5%)
  waiting for transfers between devices  29.8 us (5%)
  between operations  15.2 us (2%)
  matrix products  14 us (2%)
  local copies, waits for them, and re-layouts  8.28 us (1%)
    pallas_call x4, Pallas kernels, plane_gather(): pl.pallas_call(functools.partial(gather_kernel, member_count, in_order, c...  173 us
    pallas_call x3, Pallas kernels, product_scatter(): pl.pallas_call(functools.partial(product_scatter_kernel, member_count, in...  138 us
    pallas_call x1, Pallas kernels, attention_backward(): pl.pallas_call(functools.partial(backward_kernel, heads), grid_spec=pltpu...  54.6 us
    pallas_call x1, Pallas kernels, attention_forward(): pl.pallas_call(functools.partial(forward_kernel, heads), grid_spec=pltpu....  41.6 us
    pallas_call x2, Pallas kernels, hidden_units(): pl.pallas_call(units_kernel, grid=(tokens // tile,), in_specs=[by_tile, b...  39.2 us
    ppermute x28, starting transfers between devices, exchanged(): lax.ppermute(blocks[away], 'fsdp', [(m, m ^ away) for m in range(len(bloc...  27.3 us
    pallas_call x8, Pallas kernels, local_call(): pl.pallas_call(kernel, grid_spec=pltpu.PrefetchScalarGridSpec(num_scalar_...  23.8 us
    dot_general x1, matrix products, dot_tn(): lax.dot_general(left, right, (((0,), (0,)), ((), ())), preferred_element_...  14 us
  transfers between devices with their start and end apart: 39, of which 7 were waited for; matrix products, arithmetic and copies ran while one was open for 8% of the time, Pallas kernels for 77%

profile of v5, /device:TPU:0, one launch (start us, length us, event | category | flops | bytes accessed | tf_op | source)
XLA Modules:
  0.0 635.4 jit_solution(14471511615572301102)
XLA Ops:
  12.6 11.9 %plane_swap.1 = bf16[8,64,640]{2,1,0:T(8,128)(2,1)} custom-call(bf16[8,64,640]{2,1,0:T(8,128)(2,1)} %pad_maximum_fusion.1.refs_0_), custom_call_target="tpu_custom_call" | custom-call | bytes 19660800 | tf_op jit(solution)/shard_map/plane_swap/pallas_call | solution.py:332
  25.3 3.3 units_apart.1
  35.2 3.7 multiply_cosine_fusion
  42.9 50.2 %plane_gather.4.normed_ref = bf16[2048,2048]{1,0:T(8,128)(2,1)} custom-call(bf16[256,2048]{1,0:T(8,128)(2,1)} %fusion.3.own_ref), custom_call_target="tpu_custom_call" | custom-call | bytes 251658240 | tf_op jit(solution)/shard_map/plane_gather/pallas_call | solution.py:271
  94.5 39.6 %plane_gather.5.gradient_ref.refs_2_ = bf16[2048,2048]{1,0:T(8,128)(2,1)} custom-call(bf16[256,2048]{1,0:T(8,128)(2,1)} %fusion.own_ref), custom_call_target="tpu_custom_call" | custom-call | bytes 251658240 | tf_op jit(solution)/shard_map/plane_gather/pallas_call | solution.py:271
  134.1 3.0 rows_together.1
  137.7 10.3 %all-gather.7.cloned.1.call-done.weight_ref.value_ref.refs_1_ = bf16[2048,640]{1,0:T(8,128)(2,1)} async-done(((bf16[512,640]{1,0:T(8,128)(2,1)}), bf16[2048,640]{1,0:T(8,128)(2,1)}) %all-gather.7.cloned.1.call-update) | async-done | bytes 2621456 | tf_op jit(solution)/shard_map/all_gather | solution.py:1339
  158.6 41.6 %attention_forward.1 = (bf16[2048,256]{1,0:T(8,128)(2,1)}, bf16[2048,256]{1,0:T(8,128)(2,1)}, bf16[64,2048]{1,0:T(8,128)(2,1)}, bf16[2048,256]{1,0:T(8,128)(2,1)...) custom-call(s32[8]{0:T(128)} %and_select_fusion.first_ref, bf16[2048,2048]{1,0:T(8,128)(2,1)} %plane_gather.4.normed_ref, ...), custom_call_target="tpu_custom_call" | custom-call | flops 8589934592 | bytes 4194304 | tf_op jit(solution)/shard_map/attention_forward/pallas_call | solution.py:1103
  203.4 43.1 %product_scatter.3 = f32[256,2048]{1,0:T(8,128)} custom-call(bf16[2048,256]{1,0:T(8,128)(2,1)} %get-tuple-element.168.refs_0_.mixed_ref, bf16[256,2048]{1,0:T(8,128)(2,1)} %columns_together.1.refs_1_.weight_ref), custom_call_target="tpu_custom_call" | custom-call | bytes 251658240 | tf_op jit(solution)/shard_map/product_scatter/pallas_call | solution.py:588
  249.8 39.1 %plane_gather.6.normed_ref.refs_0_ = bf16[2048,2048]{1,0:T(8,128)(2,1)} custom-call(bf16[256,2048]{1,0:T(8,128)(2,1)} %multiply_convert_fusion.1.own_ref), custom_call_target="tpu_custom_call" | custom-call | bytes 251658240 | tf_op jit(solution)/shard_map/plane_gather/pallas_call | solution.py:271
  288.9 19.4 %hidden_units.2 = (bf16[2048,512]{1,0:T(8,128)(2,1)}, bf16[2048,1024]{1,0:T(8,128)(2,1)}) custom-call(bf16[2048,2048]{1,0:T(8,128)(2,1)} %plane_gather.6.normed_ref.refs_0_, bf16[2048,2048]{1,0:T(8,128)(2,1)} %plane_gather.5.gradient_ref.refs_2_, bf16[2048,1024]{1,0:T(8,128)(2,1)} %all-gather.9.cloned.1.call-done.both_ref.refs_3_, ...), custom_call_target="tpu_custom_call" | custom-call | flops 12884901888 | bytes 23068672 | tf_op jit(solution)/shard_map/hidden_units/pallas_call | solution.py:950
  308.3 14.0 %convolution_convert_fusion = bf16[2048,1024]{1,0:T(8,128)(2,1)} fusion(bf16[2048,2048]{1,0:T(8,128)(2,1)} %plane_gather.6.normed_ref.refs_0_, bf16[2048,1024]{1,0:T(8,128)(2,1)} %get-tuple-element.186.refs_1_), kind=kOutput, calls=%fused_computation.5 | convolution fusion | flops 8592031744 | bytes 16777216 | tf_op jit(solution)/shard_map/dot_general | solution.py:39
  322.4 19.8 %hidden_units.3 = (bf16[2048,512]{1,0:T(8,128)(2,1)}, bf16[2048,1024]{1,0:T(8,128)(2,1)}) custom-call(bf16[2048,2048]{1,0:T(8,128)(2,1)} %plane_gather.6.normed_ref.refs_0_, bf16[2048,2048]{1,0:T(8,128)(2,1)} %plane_gather.5.gradient_ref.refs_2_, bf16[2048,1024]{1,0:T(8,128)(2,1)} %all-gather.11.cloned.1.call-done.both_ref.refs_4_, ...), custom_call_target="tpu_custom_call" | custom-call | flops 12884901888 | bytes 23068672 | tf_op jit(solution)/shard_map/hidden_units/pallas_call | solution.py:950
  342.2 51.6 %product_scatter.4 = (f32[256,2048]{1,0:T(8,128)}, bf16[2048,1024]{1,0:T(8,128)(2,1)}) custom-call(bf16[2048,2048]{1,0:T(8,128)(2,1)} %plane_gather.6.normed_ref.refs_0_, bf16[2048,1024]{1,0:T(8,128)(2,1)} %get-tuple-element.186.refs_1_, bf16[2048,1024]{1,0:T(8,128)(2,1)} %get-tuple-element.188.refs_2_, ...), custom_call_target="tpu_custom_call" | custom-call | bytes 251658240 | tf_op jit(solution)/shard_map/product_scatter/pallas_call | solution.py:588
  398.8 44.1 %plane_gather.7 = (bf16[2048,2048]{1,0:T(8,128)(2,1)}, bf16[1024,2048]{1,0:T(8,128)(2,1)}, bf16[512,2048]{1,0:T(8,128)(2,1)}, bf16[512,2048]{1,0:T(8,128)(2,1)}) custom-call(bf16[256,2048]{1,0:T(8,128)(2,1)} %get-tuple-element.261.own_ref, bf16[2048,512]{1,0:T(8,128)(2,1)} %get-tuple-element.190.refs_0_, bf16[2048,512]{1,0:T(8,128)(2,1)} %get-tuple-element.191.refs_1_, ...), custom_call_target="tpu_custom_call" | custom-call | bytes 4194304 | tf_op jit(solution)/shard_map/plane_gather/pallas_call | solution.py:271
  443.4 54.6 %attention_backward.1 = (bf16[2048,384]{1,0:T(8,128)(2,1)}, bf16[256,2048]{1,0:T(8,128)(2,1)}) custom-call(s32[8]{0:T(128)} %and_select_fusion.first_ref, bf16[2048,256]{1,0:T(8,128)(2,1)} %get-tuple-element.177.query_ref, bf16[2048,256]{1,0:T(8,128)(2,1)} %get-tuple-element.178.key_ref, bf16[64,2048]{1,0:T(8,128)(2,1)} %get-tuple-element.179.key_columns_ref, ...), custom_call_target="tpu_custom_call" | custom-call | bytes 524288 | tf_op jit(solution)/shard_map/attention_backward/pallas_call | solution.py:1250
  500.3 4.2 all-to-all-start
  513.6 8.7 %collective-permute-done.15.refs_2_ = bf16[64,1024]{1,0:T(8,128)(2,1)S(1)} collective-permute-done((bf16[64,1024]{1,0:T(8,128)(2,1)}, bf16[64,1024]{1,0:T(8,128)(2,1)S(1)}, u32[]{:S(2)}, u32[]{:S(2)}) %collective-permute-start.15) | collective-permute-done | bytes 131104 | tf_op jit(solution)/shard_map/ppermute | solution.py:790
  522.6 8.8 %projection_grad.1 = bf16[2048,640]{1,0:T(8,128)(2,1)} custom-call(bf16[2048,2048]{1,0:T(8,128)(2,1)} %plane_gather.4.normed_ref, bf16[2048,384]{1,0:T(8,128)(2,1)} %get-tuple-element.209.grad_ref.refs_0_, bf16[2048,256]{1,0:T(8,128)(2,1)} %bitcast.12.out_grad_ref), custom_call_target="tpu_custom_call" | custom-call | flops 3221225472 | bytes 8388608 | tf_op jit(solution)/shard_map/projection_grad/pallas_call | solution.py:1299
  542.3 43.1 %product_scatter.5 = f32[256,2048]{1,0:T(8,128)} custom-call(bf16[2048,384]{1,0:T(8,128)(2,1)} %get-tuple-element.209.grad_ref.refs_0_, bf16[2048,640]{1,0:T(8,128)(2,1)} %all-gather.7.cloned.1.call-done.weight_ref.value_ref.refs_1_), custom_call_target="tpu_custom_call" | custom-call | bytes 4194304 | tf_op jit(solution)/shard_map/product_scatter/pallas_call | solution.py:588
  595.0 5.3 units_together.1
  600.2 3.3 fusion.6
  605.7 3.1 add_convert_fusion
  611.8 12.5 %finale.1 = (bf16[8,64,640]{2,1,0:T(8,128)(2,1)}, f32[8,128]{1,0:T(8,128)}) custom-call(bf16[512,640]{1,0:T(8,128)(2,1)} %reduce-scatter.9.cloned.1.call-done.packed_ref, f32[8,8,128]{2,1,0:T(8,128)} %pad.4.part_ref), custom_call_target="tpu_custom_call" | custom-call | bytes 40000000 | tf_op jit(solution)/shard_map/finale/pallas_call | solution.py:703
  (177 shorter events, 81.8 us)
Async XLA Ops:
  7.2 87.3 %all-gather.5.cloned.1.call-start = ((), (), s32[]{:S(2)}) async-start(), calls=%async_computation.5 | async-start | bytes 5242880 | tf_op jit(solution)/shard_map/all_gather | solution.py:1339
  7.9 140.1 %all-gather.7.cloned.1.call-start = ((), (), s32[]{:S(2)}) async-start(), calls=%async_computation.6 | async-start | bytes 3276800 | tf_op jit(solution)/shard_map/all_gather | solution.py:1339
  24.6 264.3 %all-gather.9.cloned.1.call-start = ((), (), s32[]{:S(2)}) async-start(), calls=%async_computation.7 | async-start | bytes 5242880 | tf_op jit(solution)/shard_map/all_gather | solution.py:1339
  31.0 103.1 %collective-permute-start.2 = (bf16[64,2048]{1,0:T(8,128)(2,1)}, bf16[64,2048]{1,0:T(8,128)(2,1)}, u32[]{:S(2)}, u32[]{:S(2)}) collective-permute-start(bf16[64,2048]{1,0:T(8,128)(2,1)} %get-tuple-element.140), channel_id=1, source_target_pairs={{0,3},{1,2},{2,1},{3,0},{4,7},{5,6},{6,5},{7,4},{8,11},{9,10},{10,... | collective-permute-start | bytes 786440 | tf_op jit(solution)/shard_map/ppermute | solution.py:790
  31.2 102.8 %collective-permute-start.3 = (bf16[64,2048]{1,0:T(8,128)(2,1)}, bf16[64,2048]{1,0:T(8,128)(2,1)}, u32[]{:S(2)}, u32[]{:S(2)}) collective-permute-start(bf16[64,2048]{1,0:T(8,128)(2,1)} %get-tuple-element.141), channel_id=1, source_target_pairs={{0,4},{1,5},{2,6},{3,7},{4,0},{5,1},{6,2},{7,3},{8,12},{9,13},{10,... | collective-permute-start | bytes 786440 | tf_op jit(solution)/shard_map/ppermute | solution.py:790
  32.6 101.4 %collective-permute-start.4 = (bf16[64,2048]{1,0:T(8,128)(2,1)}, bf16[64,2048]{1,0:T(8,128)(2,1)}, u32[]{:S(2)}, u32[]{:S(2)}) collective-permute-start(bf16[64,2048]{1,0:T(8,128)(2,1)} %get-tuple-element.142), channel_id=1, source_target_pairs={{0,5},{1,4},{2,7},{3,6},{4,1},{5,0},{6,3},{7,2},{8,13},{9,12},{10,... | collective-permute-start | bytes 786440 | tf_op jit(solution)/shard_map/ppermute | solution.py:790
  40.2 93.9 %collective-permute-start.5 = (bf16[64,2048]{1,0:T(8,128)(2,1)}, bf16[64,2048]{1,0:T(8,128)(2,1)}, u32[]{:S(2)}, u32[]{:S(2)}) collective-permute-start(bf16[64,2048]{1,0:T(8,128)(2,1)} %get-tuple-element.143), channel_id=1, source_target_pairs={{0,6},{1,7},{2,4},{3,5},{4,2},{5,3},{6,0},{7,1},{8,14},{9,15},{10,... | collective-permute-start | bytes 786440 | tf_op jit(solution)/shard_map/ppermute | solution.py:790
  42.2 91.9 %collective-permute-start.6 = (bf16[64,2048]{1,0:T(8,128)(2,1)}, bf16[64,2048]{1,0:T(8,128)(2,1)}, u32[]{:S(2)}, u32[]{:S(2)}) collective-permute-start(bf16[64,2048]{1,0:T(8,128)(2,1)} %get-tuple-element.144), channel_id=1, source_target_pairs={{0,7},{1,6},{2,5},{3,4},{4,3},{5,2},{6,1},{7,0},{8,15},{9,14},{10,... | collective-permute-start | bytes 786440 | tf_op jit(solution)/shard_map/ppermute | solution.py:790
  137.1 185.2 %all-gather.11.cloned.1.call-start = ((), (), s32[]{:S(2)}) async-start(), calls=%async_computation.8 | async-start | bytes 5242880 | tf_op jit(solution)/shard_map/all_gather | solution.py:1339
  137.7 367.2 %reduce-scatter.5.cloned.1.call-start = ((), (), s32[]{:S(2)}) async-start(), calls=%async_computation.9 | async-start | bytes 5242880 | tf_op jit(solution)/shard_map/reduce_scatter | solution.py:1335
  152.3 47.9 %collective-permute-start.9 = (bf16[256,256]{1,0:T(8,128)(2,1)}, bf16[256,256]{1,0:T(8,128)(2,1)S(1)}, u32[]{:S(2)}, u32[]{:S(2)}) collective-permute-start(bf16[256,256]{1,0:T(8,128)(2,1)} %get-tuple-element.163), channel_id=1, source_target_pairs={{0,3},{1,2},{2,1},{3,0},{4,7},{5,6},{6,5},{7,4},{8,11},{9,10},{10,... | collective-permute-start | bytes 393224 | tf_op jit(solution)/shard_map/ppermute | solution.py:790
  152.7 47.6 %collective-permute-start.10 = (bf16[256,256]{1,0:T(8,128)(2,1)}, bf16[256,256]{1,0:T(8,128)(2,1)S(1)}, u32[]{:S(2)}, u32[]{:S(2)}) collective-permute-start(bf16[256,256]{1,0:T(8,128)(2,1)} %get-tuple-element.164), channel_id=1, source_target_pairs={{0,4},{1,5},{2,6},{3,7},{4,0},{5,1},{6,2},{7,3},{8,12},{9,13},{10,... | collective-permute-start | bytes 393224 | tf_op jit(solution)/shard_map/ppermute | solution.py:790
  154.1 46.1 %collective-permute-start.11 = (bf16[256,256]{1,0:T(8,128)(2,1)}, bf16[256,256]{1,0:T(8,128)(2,1)S(1)}, u32[]{:S(2)}, u32[]{:S(2)}) collective-permute-start(bf16[256,256]{1,0:T(8,128)(2,1)} %get-tuple-element.165), channel_id=1, source_target_pairs={{0,5},{1,4},{2,7},{3,6},{4,1},{5,0},{6,3},{7,2},{8,13},{9,12},{10,... | collective-permute-start | bytes 393224 | tf_op jit(solution)/shard_map/ppermute | solution.py:790
  154.3 46.0 %collective-permute-start.12 = (bf16[256,256]{1,0:T(8,128)(2,1)}, bf16[256,256]{1,0:T(8,128)(2,1)S(1)}, u32[]{:S(2)}, u32[]{:S(2)}) collective-permute-start(bf16[256,256]{1,0:T(8,128)(2,1)} %get-tuple-element.166), channel_id=1, source_target_pairs={{0,6},{1,7},{2,4},{3,5},{4,2},{5,3},{6,0},{7,1},{8,14},{9,15},{10,... | collective-permute-start | bytes 393224 | tf_op jit(solution)/shard_map/ppermute | solution.py:790
  157.3 43.0 %collective-permute-start.13 = (bf16[256,256]{1,0:T(8,128)(2,1)}, bf16[256,256]{1,0:T(8,128)(2,1)S(1)}, u32[]{:S(2)}, u32[]{:S(2)}) collective-permute-start(bf16[256,256]{1,0:T(8,128)(2,1)} %get-tuple-element.167), channel_id=1, source_target_pairs={{0,7},{1,6},{2,5},{3,4},{4,3},{5,2},{6,1},{7,0},{8,15},{9,14},{10,... | collective-permute-start | bytes 393224 | tf_op jit(solution)/shard_map/ppermute | solution.py:790
  322.3 210.1 %reduce-scatter.11.cloned.1.call-start = ((), (), s32[]{:S(2)}) async-start(), calls=%async_computation.12 | async-start | bytes 5242880 | tf_op jit(solution)/shard_map/reduce_scatter | solution.py:1335
  393.8 191.6 %reduce-scatter.7.cloned.1.call-start = ((), (), s32[]{:S(2)}) async-start(), calls=%async_computation.10 | async-start | bytes 5242880 | tf_op jit(solution)/shard_map/reduce_scatter | solution.py:1335
  443.0 67.9 %collective-permute-start.21 = (bf16[512,2048]{1,0:T(8,128)(2,1)}, bf16[512,2048]{1,0:T(8,128)(2,1)}, u32[]{:S(2)}, u32[]{:S(2)}) collective-permute-start(bf16[512,2048]{1,0:T(8,128)(2,1)} %get-tuple-element.205), channel_id=1, source_target_pairs={{0,4},{1,3},{2,6},{3,1},{4,0},{5,7},{6,2},{7,5},{8,12},{9,11},{10,... | collective-permute-start | bytes 6291464 | tf_op jit(solution)/shard_map/ppermute | solution.py:800
  504.6 107.2 %reduce-scatter.9.cloned.1.call-start = ((), (), s32[]{:S(2)}) async-start(), calls=%async_computation.11 | async-start | bytes 3276800 | tf_op jit(solution)/shard_map/reduce_scatter | solution.py:1335
  534.6 50.9 %collective-permute-start.23 = (bf16[64,1024]{1,0:T(8,128)(2,1)}, bf16[64,1024]{1,0:T(8,128)(2,1)S(1)}, u32[]{:S(2)}, u32[]{:S(2)}) collective-permute-start(bf16[64,1024]{1,0:T(8,128)(2,1)} %get-tuple-element.230), channel_id=1, source_target_pairs={{0,1},{1,0},{2,3},{3,2},{4,5},{5,4},{6,7},{7,6},{8,9},{9,8},{10,11... | collective-permute-start | bytes 393224 | tf_op jit(solution)/shard_map/ppermute | solution.py:790
  535.8 51.2 %collective-permute-start.24 = (bf16[64,1024]{1,0:T(8,128)(2,1)}, bf16[64,1024]{1,0:T(8,128)(2,1)S(1)}, u32[]{:S(2)}, u32[]{:S(2)}) collective-permute-start(bf16[64,1024]{1,0:T(8,128)(2,1)} %get-tuple-element.231), channel_id=1, source_target_pairs={{0,2},{1,3},{2,0},{3,1},{4,6},{5,7},{6,4},{7,5},{8,10},{9,11},{10,... | collective-permute-start | bytes 393224 | tf_op jit(solution)/shard_map/ppermute | solution.py:790
  537.3 49.9 %collective-permute-start.25 = (bf16[64,1024]{1,0:T(8,128)(2,1)}, bf16[64,1024]{1,0:T(8,128)(2,1)}, u32[]{:S(2)}, u32[]{:S(2)}) collective-permute-start(bf16[64,1024]{1,0:T(8,128)(2,1)} %get-tuple-element.232), channel_id=1, source_target_pairs={{0,3},{1,2},{2,1},{3,0},{4,7},{5,6},{6,5},{7,4},{8,11},{9,10},{10,... | collective-permute-start | bytes 393224 | tf_op jit(solution)/shard_map/ppermute | solution.py:790
  537.3 53.1 %collective-permute-start.26 = (bf16[64,1024]{1,0:T(8,128)(2,1)}, bf16[64,1024]{1,0:T(8,128)(2,1)}, u32[]{:S(2)}, u32[]{:S(2)}) collective-permute-start(bf16[64,1024]{1,0:T(8,128)(2,1)} %get-tuple-element.233), channel_id=1, source_target_pairs={{0,4},{1,5},{2,6},{3,7},{4,0},{5,1},{6,2},{7,3},{8,12},{9,13},{10,... | collective-permute-start | bytes 393224 | tf_op jit(solution)/shard_map/ppermute | solution.py:790
  537.9 52.6 %collective-permute-start.27 = (bf16[64,1024]{1,0:T(8,128)(2,1)}, bf16[64,1024]{1,0:T(8,128)(2,1)}, u32[]{:S(2)}, u32[]{:S(2)}) collective-permute-start(bf16[64,1024]{1,0:T(8,128)(2,1)} %get-tuple-element.234), channel_id=1, source_target_pairs={{0,5},{1,4},{2,7},{3,6},{4,1},{5,0},{6,3},{7,2},{8,13},{9,12},{10,... | collective-permute-start | bytes 393224 | tf_op jit(solution)/shard_map/ppermute | solution.py:790
  (38 other events, 501.0 us)
Sparse Core Ops, SparseCore 0:
  9.6 83.4 all-gather.4
  94.7 53.3 all-gather.6
  150.2 79.5 all-gather.8
  231.2 79.2 all-gather.10
  322.4 75.1 reduce-scatter.4
  399.8 77.2 reduce-scatter.10
  479.4 77.2 reduce-scatter.6
  559.2 52.5 reduce-scatter.8

commit v6 on v5

--- a/solution.py
+++ b/solution.py
@@ -996,14 +996,15 @@
     return (row == HD + column % HD).astype(F32)
 
 
-def exact(left, right, dims):
-    return lax.dot_general(
-        left,
-        right,
-        (dims, ((), ())),
-        precision=lax.Precision.HIGHEST,
-        preferred_element_type=F32,
-    )
+def split(value):
+    high = value.astype(BF16)
+    return high, (value - high.astype(F32)).astype(BF16)
+
+
+def exact(value, choice):
+    high, low = split(value)
+    choice = choice.astype(BF16)
+    return dot_nn(high, choice) + dot_nn(low, choice)
 
 
 def tables(table, width):
@@ -1011,8 +1012,8 @@
     row = lax.broadcasted_iota(jnp.int32, (2 * HALF, half), 0)
     column = lax.broadcasted_iota(jnp.int32, (2 * HALF, half), 1) % HALF
     return (
-        exact(table, (row == column).astype(F32), ((1,), (0,))),
-        exact(table, (row == column + HALF).astype(F32), ((1,), (0,))),
+        exact(table, row == column),
+        exact(table, row == column + HALF),
     )
 
 
@@ -1046,16 +1047,16 @@
     start = start_ref[...]
     cosine, sine = tables(table_ref[...], width)
     projected = dot_nn(normed_ref[...], weight_ref[:, : width + 2 * HD])
-    query = turn(projected[:, :width], cosine, sine).astype(BF16)
+    query = turn(projected[:, :width], cosine, sine).astype(BF16) * ATTENTION_SCALE
     pair = projected[:, width:]
-    keys_here = turn(exact(pair, spread_keys(width), ((1,), (0,))), cosine, sine).astype(BF16)
+    keys_here = turn(exact(pair, spread_keys(width)), cosine, sine).astype(BF16)
     own_rows = pl.ds(pl.multiple_of(step * BLOCK, BLOCK), BLOCK)
     query_ref[...] = query
     key_ref[own_rows, :] = keys_here
     turned_keys = jnp.transpose(keys_here.astype(F32)).astype(BF16)
     key_columns_ref[:HALF, :] = turned_keys[:HALF, :]
     key_columns_ref[HALF:, :] = turned_keys[width // 2 : width // 2 + HALF, :]
-    value_ref[...] = exact(pair, spread_values(width), ((1,), (0,))).astype(BF16)
+    value_ref[...] = dot_nn(pair.astype(BF16), spread_values(width).astype(BF16)).astype(BF16)
     value_columns[:, own_rows] = jnp.transpose(pair)[HD:, :].astype(BF16)
     token = step * BLOCK + lax.broadcasted_iota(jnp.int32, (BLOCK, BLOCK), 1)
     within = lax.broadcasted_iota(jnp.int32, (BLOCK, BLOCK), 0)
@@ -1072,7 +1073,7 @@
         visible = (place >= start) & (place <= token)
         for head in range(heads):
             own_keys = jnp.where(lane_head == head, keys, jnp.zeros_like(keys))
-            scores = jnp.where(visible, dot_nt(own_keys, query) * ATTENTION_SCALE, MASKED)
+            scores = jnp.where(visible, dot_nt(own_keys, query), MASKED)
             old = top[head : head + 1, :]
             new = jnp.maximum(old, jnp.max(scores, axis=0, keepdims=True))
             weights = jnp.exp(scores - new)
@@ -1173,8 +1174,9 @@
     chooser = (
         lax.broadcasted_iota(jnp.int32, (8, width), 0)
         == lax.broadcasted_iota(jnp.int32, (8, width), 1) // HD
-    ).astype(F32)
-    correction = exact(chooser, product, ((1,), (1,)))
+    ).astype(BF16)
+    high, low = split(product)
+    correction = dot_nt(chooser, high) + dot_nt(chooser, low)
 
     @pl.when(step == 0)
     def _():
@@ -1198,7 +1200,7 @@
         for head in range(heads):
             own_keys = jnp.where(half_head == head, keys, zero)
             own_values = jnp.where(full_head == head, values, zero)
-            scores = dot_nt(own_keys, query) * ATTENTION_SCALE
+            scores = dot_nt(own_keys, query)
             probs = jnp.where(visible, jnp.exp(scores - lse_ref[head : head + 1, :]), 0.0)
             pressure = dot_nt(own_values, grad)
             dscores = (probs * (pressure - correction[head : head + 1, :])).astype(BF16)
@@ -1227,7 +1229,7 @@
         def fold(block, carried):
             rows = pl.ds(pl.multiple_of(block * BLOCK, BLOCK), BLOCK)
             cosine, sine = tables(table_ref[rows, :], width)
-            turned = turn(dkey[rows, :], cosine, -sine) * ATTENTION_SCALE
+            turned = turn(dkey[rows, :], cosine, -sine)
             out_ref[rows, width:] = (
                 dot_nt(turned.astype(BF16), spread_keys(width).astype(BF16))
                 + dot_nt(dvalue[rows, :].astype(BF16), spread_values(width).astype(BF16))

time: 644 us -> 641 us (level)
  Pallas kernels: 503 us -> 486 us
  waiting for transfers between devices: 29.8 us -> 42.2 us
    reduce_scatter x4, waiting for transfers between devices: 3 us -> 15.5 us  [sum_over_groups(): return lax.psum_scatter(value, 'dp', scatter_dimension=0, tiled=True)]
    pallas_call x1, Pallas kernels: 54.6 us -> 46 us  [attention_backward(): pl.pallas_call(functools.partial(backward_kernel, heads), grid_spec=pltpu...]
    pallas_call x1, Pallas kernels: 41.6 us -> 33.8 us  [attention_forward(): pl.pallas_call(functools.partial(forward_kernel, heads), grid_spec=pltpu....]
  transfers between devices with their start and end apart: 39 -> 39, of which waited for: 7 -> 7; matrix products, arithmetic and copies ran while one was open for 8% -> 8% of each run, Pallas kernels for 77% -> 75%
where the time goes in v6:
time: 641 us; the launch traced here: 632 us
  Pallas kernels  486 us (76%)
  waiting for transfers between devices  42.2 us (7%)
  starting transfers between devices  34.8 us (5%)
  other arithmetic  30.9 us (5%)
  between operations  15.2 us (2%)
  matrix products  14 us (2%)
  local copies, waits for them, and re-layouts  8.61 us (1%)
    pallas_call x4, Pallas kernels, plane_gather(): pl.pallas_call(functools.partial(gather_kernel, member_count, in_order, c...  173 us
    pallas_call x3, Pallas kernels, product_scatter(): pl.pallas_call(functools.partial(product_scatter_kernel, member_count, in...  138 us
    pallas_call x1, Pallas kernels, attention_backward(): pl.pallas_call(functools.partial(backward_kernel, heads), grid_spec=pltpu...  46 us
    pallas_call x2, Pallas kernels, hidden_units(): pl.pallas_call(units_kernel, grid=(tokens // tile,), in_specs=[by_tile, b...  38.8 us
    pallas_call x1, Pallas kernels, attention_forward(): pl.pallas_call(functools.partial(forward_kernel, heads), grid_spec=pltpu....  33.8 us
    ppermute x28, starting transfers between devices, exchanged(): lax.ppermute(blocks[away], 'fsdp', [(m, m ^ away) for m in range(len(bloc...  27.3 us
    pallas_call x8, Pallas kernels, local_call(): pl.pallas_call(kernel, grid_spec=pltpu.PrefetchScalarGridSpec(num_scalar_...  23.8 us
    reduce_scatter x4, waiting for transfers between devices, sum_over_groups(): return lax.psum_scatter(value, 'dp', scatter_dimension=0, tiled=True)  15.5 us
  transfers between devices with their start and end apart: 39, of which 7 were waited for; matrix products, arithmetic and copies ran while one was open for 8% of the time, Pallas kernels for 75%

profile of v6, /device:TPU:0, one launch (start us, length us, event | category | flops | bytes accessed | tf_op | source)
XLA Modules:
  0.0 632.1 jit_solution(8581241832849553647)
XLA Ops:
  12.6 11.9 %plane_swap.1 = bf16[8,64,640]{2,1,0:T(8,128)(2,1)} custom-call(bf16[8,64,640]{2,1,0:T(8,128)(2,1)} %pad_maximum_fusion.1.refs_0_), custom_call_target="tpu_custom_call" | custom-call | bytes 19660800 | tf_op jit(solution)/shard_map/plane_swap/pallas_call | solution.py:332
  25.3 3.3 units_apart.1
  35.2 3.7 multiply_cosine_fusion
  42.9 50.2 %plane_gather.4.normed_ref = bf16[2048,2048]{1,0:T(8,128)(2,1)} custom-call(bf16[256,2048]{1,0:T(8,128)(2,1)} %fusion.3.own_ref), custom_call_target="tpu_custom_call" | custom-call | bytes 251658240 | tf_op jit(solution)/shard_map/plane_gather/pallas_call | solution.py:271
  94.5 39.6 %plane_gather.5.gradient_ref.refs_2_ = bf16[2048,2048]{1,0:T(8,128)(2,1)} custom-call(bf16[256,2048]{1,0:T(8,128)(2,1)} %fusion.own_ref), custom_call_target="tpu_custom_call" | custom-call | bytes 251658240 | tf_op jit(solution)/shard_map/plane_gather/pallas_call | solution.py:271
  138.0 10.1 %all-gather.7.cloned.1.call-done.weight_ref.value_ref.refs_1_ = bf16[2048,640]{1,0:T(8,128)(2,1)} async-done(((bf16[512,640]{1,0:T(8,128)(2,1)}), bf16[2048,640]{1,0:T(8,128)(2,1)}) %all-gather.7.cloned.1.call-update) | async-done | bytes 2621456 | tf_op jit(solution)/shard_map/all_gather | solution.py:1341
  158.6 33.8 %attention_forward.1 = (bf16[2048,256]{1,0:T(8,128)(2,1)}, bf16[2048,256]{1,0:T(8,128)(2,1)}, bf16[64,2048]{1,0:T(8,128)(2,1)}, bf16[2048,256]{1,0:T(8,128)(2,1)...) custom-call(s32[8]{0:T(128)} %and_select_fusion.first_ref, bf16[2048,2048]{1,0:T(8,128)(2,1)} %plane_gather.4.normed_ref, ...), custom_call_target="tpu_custom_call" | custom-call | flops 8589934592 | bytes 4194304 | tf_op jit(solution)/shard_map/attention_forward/pallas_call | solution.py:1104
  195.6 43.2 %product_scatter.3 = f32[256,2048]{1,0:T(8,128)} custom-call(bf16[2048,256]{1,0:T(8,128)(2,1)} %get-tuple-element.168.refs_0_.mixed_ref, bf16[256,2048]{1,0:T(8,128)(2,1)} %columns_together.1.refs_1_.weight_ref), custom_call_target="tpu_custom_call" | custom-call | bytes 251658240 | tf_op jit(solution)/shard_map/product_scatter/pallas_call | solution.py:588
  242.2 39.0 %plane_gather.6.normed_ref.refs_0_ = bf16[2048,2048]{1,0:T(8,128)(2,1)} custom-call(bf16[256,2048]{1,0:T(8,128)(2,1)} %multiply_convert_fusion.1.own_ref), custom_call_target="tpu_custom_call" | custom-call | bytes 251658240 | tf_op jit(solution)/shard_map/plane_gather/pallas_call | solution.py:271
  281.2 19.4 %hidden_units.2 = (bf16[2048,512]{1,0:T(8,128)(2,1)}, bf16[2048,1024]{1,0:T(8,128)(2,1)}) custom-call(bf16[2048,2048]{1,0:T(8,128)(2,1)} %plane_gather.6.normed_ref.refs_0_, bf16[2048,2048]{1,0:T(8,128)(2,1)} %plane_gather.5.gradient_ref.refs_2_, bf16[2048,1024]{1,0:T(8,128)(2,1)} %all-gather.9.cloned.1.call-done.both_ref.refs_3_, ...), custom_call_target="tpu_custom_call" | custom-call | flops 12884901888 | bytes 23068672 | tf_op jit(solution)/shard_map/hidden_units/pallas_call | solution.py:950
  300.7 14.0 %convolution_convert_fusion = bf16[2048,1024]{1,0:T(8,128)(2,1)} fusion(bf16[2048,2048]{1,0:T(8,128)(2,1)} %plane_gather.6.normed_ref.refs_0_, bf16[2048,1024]{1,0:T(8,128)(2,1)} %get-tuple-element.186.refs_1_), kind=kOutput, calls=%fused_computation.5 | convolution fusion | flops 8592031744 | bytes 16777216 | tf_op jit(solution)/shard_map/dot_general | solution.py:39
  315.2 19.4 %hidden_units.3 = (bf16[2048,512]{1,0:T(8,128)(2,1)}, bf16[2048,1024]{1,0:T(8,128)(2,1)}) custom-call(bf16[2048,2048]{1,0:T(8,128)(2,1)} %plane_gather.6.normed_ref.refs_0_, bf16[2048,2048]{1,0:T(8,128)(2,1)} %plane_gather.5.gradient_ref.refs_2_, bf16[2048,1024]{1,0:T(8,128)(2,1)} %all-gather.11.cloned.1.call-done.both_ref.refs_4_, ...), custom_call_target="tpu_custom_call" | custom-call | flops 12884901888 | bytes 23068672 | tf_op jit(solution)/shard_map/hidden_units/pallas_call | solution.py:950
  334.5 51.7 %product_scatter.4 = (f32[256,2048]{1,0:T(8,128)}, bf16[2048,1024]{1,0:T(8,128)(2,1)}) custom-call(bf16[2048,2048]{1,0:T(8,128)(2,1)} %plane_gather.6.normed_ref.refs_0_, bf16[2048,1024]{1,0:T(8,128)(2,1)} %get-tuple-element.186.refs_1_, bf16[2048,1024]{1,0:T(8,128)(2,1)} %get-tuple-element.188.refs_2_, ...), custom_call_target="tpu_custom_call" | custom-call | bytes 251658240 | tf_op jit(solution)/shard_map/product_scatter/pallas_call | solution.py:588
  391.3 44.0 %plane_gather.7 = (bf16[2048,2048]{1,0:T(8,128)(2,1)}, bf16[1024,2048]{1,0:T(8,128)(2,1)}, bf16[512,2048]{1,0:T(8,128)(2,1)}, bf16[512,2048]{1,0:T(8,128)(2,1)}) custom-call(bf16[256,2048]{1,0:T(8,128)(2,1)} %get-tuple-element.261.own_ref, bf16[2048,512]{1,0:T(8,128)(2,1)} %get-tuple-element.190.refs_0_, bf16[2048,512]{1,0:T(8,128)(2,1)} %get-tuple-element.191.refs_1_, ...), custom_call_target="tpu_custom_call" | custom-call | bytes 4194304 | tf_op jit(solution)/shard_map/plane_gather/pallas_call | solution.py:271
  435.9 46.0 %attention_backward.1 = (bf16[2048,384]{1,0:T(8,128)(2,1)}, bf16[256,2048]{1,0:T(8,128)(2,1)}) custom-call(s32[8]{0:T(128)} %and_select_fusion.first_ref, bf16[2048,256]{1,0:T(8,128)(2,1)} %get-tuple-element.177.query_ref, bf16[2048,256]{1,0:T(8,128)(2,1)} %get-tuple-element.178.key_ref, bf16[64,2048]{1,0:T(8,128)(2,1)} %get-tuple-element.179.key_columns_ref, ...), custom_call_target="tpu_custom_call" | custom-call | bytes 524288 | tf_op jit(solution)/shard_map/attention_backward/pallas_call | solution.py:1252
  484.5 4.2 all-to-all-start
  497.8 8.7 %collective-permute-done.15.refs_2_ = bf16[64,1024]{1,0:T(8,128)(2,1)S(1)} collective-permute-done((bf16[64,1024]{1,0:T(8,128)(2,1)}, bf16[64,1024]{1,0:T(8,128)(2,1)S(1)}, u32[]{:S(2)}, u32[]{:S(2)}) %collective-permute-start.15) | collective-permute-done | bytes 131104 | tf_op jit(solution)/shard_map/ppermute | solution.py:790
  506.8 8.9 %projection_grad.1 = bf16[2048,640]{1,0:T(8,128)(2,1)} custom-call(bf16[2048,2048]{1,0:T(8,128)(2,1)} %plane_gather.4.normed_ref, bf16[2048,384]{1,0:T(8,128)(2,1)} %get-tuple-element.209.grad_ref.refs_0_, bf16[2048,256]{1,0:T(8,128)(2,1)} %bitcast.12.out_grad_ref), custom_call_target="tpu_custom_call" | custom-call | flops 3221225472 | bytes 8388608 | tf_op jit(solution)/shard_map/projection_grad/pallas_call | solution.py:1301
  526.4 43.1 %product_scatter.5 = f32[256,2048]{1,0:T(8,128)} custom-call(bf16[2048,384]{1,0:T(8,128)(2,1)} %get-tuple-element.209.grad_ref.refs_0_, bf16[2048,640]{1,0:T(8,128)(2,1)} %all-gather.7.cloned.1.call-done.weight_ref.value_ref.refs_1_), custom_call_target="tpu_custom_call" | custom-call | bytes 4194304 | tf_op jit(solution)/shard_map/product_scatter/pallas_call | solution.py:588
  579.1 5.3 units_together.1
  584.4 3.2 fusion.6
  589.9 3.1 add_convert_fusion
  593.0 15.5 %reduce-scatter.9.cloned.1.call-done.packed_ref = bf16[512,640]{1,0:T(8,128)(2,1)} async-done(((bf16[2048,640]{1,0:T(8,128)(2,1)}), bf16[512,640]{1,0:T(8,128)(2,1)}) %reduce-scatter.9.cloned.1.call-update) | async-done | bytes 655376 | tf_op jit(solution)/shard_map/reduce_scatter | solution.py:1337
  608.5 12.5 %finale.1 = (bf16[8,64,640]{2,1,0:T(8,128)(2,1)}, f32[8,128]{1,0:T(8,128)}) custom-call(bf16[512,640]{1,0:T(8,128)(2,1)} %reduce-scatter.9.cloned.1.call-done.packed_ref, f32[8,8,128]{2,1,0:T(8,128)} %pad.4.part_ref), custom_call_target="tpu_custom_call" | custom-call | bytes 40000000 | tf_op jit(solution)/shard_map/finale/pallas_call | solution.py:703
  (177 shorter events, 83.2 us)
Async XLA Ops:
  7.2 87.3 %all-gather.5.cloned.1.call-start = ((), (), s32[]{:S(2)}) async-start(), calls=%async_computation.5 | async-start | bytes 5242880 | tf_op jit(solution)/shard_map/all_gather | solution.py:1341
  7.9 140.1 %all-gather.7.cloned.1.call-start = ((), (), s32[]{:S(2)}) async-start(), calls=%async_computation.6 | async-start | bytes 3276800 | tf_op jit(solution)/shard_map/all_gather | solution.py:1341
  24.6 256.6 %all-gather.9.cloned.1.call-start = ((), (), s32[]{:S(2)}) async-start(), calls=%async_computation.7 | async-start | bytes 5242880 | tf_op jit(solution)/shard_map/all_gather | solution.py:1341
  31.0 103.1 %collective-permute-start.2 = (bf16[64,2048]{1,0:T(8,128)(2,1)}, bf16[64,2048]{1,0:T(8,128)(2,1)}, u32[]{:S(2)}, u32[]{:S(2)}) collective-permute-start(bf16[64,2048]{1,0:T(8,128)(2,1)} %get-tuple-element.140), channel_id=1, source_target_pairs={{0,3},{1,2},{2,1},{3,0},{4,7},{5,6},{6,5},{7,4},{8,11},{9,10},{10,... | collective-permute-start | bytes 786440 | tf_op jit(solution)/shard_map/ppermute | solution.py:790
  31.2 102.8 %collective-permute-start.3 = (bf16[64,2048]{1,0:T(8,128)(2,1)}, bf16[64,2048]{1,0:T(8,128)(2,1)}, u32[]{:S(2)}, u32[]{:S(2)}) collective-permute-start(bf16[64,2048]{1,0:T(8,128)(2,1)} %get-tuple-element.141), channel_id=1, source_target_pairs={{0,4},{1,5},{2,6},{3,7},{4,0},{5,1},{6,2},{7,3},{8,12},{9,13},{10,... | collective-permute-start | bytes 786440 | tf_op jit(solution)/shard_map/ppermute | solution.py:790
  32.6 101.4 %collective-permute-start.4 = (bf16[64,2048]{1,0:T(8,128)(2,1)}, bf16[64,2048]{1,0:T(8,128)(2,1)}, u32[]{:S(2)}, u32[]{:S(2)}) collective-permute-start(bf16[64,2048]{1,0:T(8,128)(2,1)} %get-tuple-element.142), channel_id=1, source_target_pairs={{0,5},{1,4},{2,7},{3,6},{4,1},{5,0},{6,3},{7,2},{8,13},{9,12},{10,... | collective-permute-start | bytes 786440 | tf_op jit(solution)/shard_map/ppermute | solution.py:790
  40.2 93.9 %collective-permute-start.5 = (bf16[64,2048]{1,0:T(8,128)(2,1)}, bf16[64,2048]{1,0:T(8,128)(2,1)}, u32[]{:S(2)}, u32[]{:S(2)}) collective-permute-start(bf16[64,2048]{1,0:T(8,128)(2,1)} %get-tuple-element.143), channel_id=1, source_target_pairs={{0,6},{1,7},{2,4},{3,5},{4,2},{5,3},{6,0},{7,1},{8,14},{9,15},{10,... | collective-permute-start | bytes 786440 | tf_op jit(solution)/shard_map/ppermute | solution.py:790
  42.2 91.9 %collective-permute-start.6 = (bf16[64,2048]{1,0:T(8,128)(2,1)}, bf16[64,2048]{1,0:T(8,128)(2,1)}, u32[]{:S(2)}, u32[]{:S(2)}) collective-permute-start(bf16[64,2048]{1,0:T(8,128)(2,1)} %get-tuple-element.144), channel_id=1, source_target_pairs={{0,7},{1,6},{2,5},{3,4},{4,3},{5,2},{6,1},{7,0},{8,15},{9,14},{10,... | collective-permute-start | bytes 786440 | tf_op jit(solution)/shard_map/ppermute | solution.py:790
  137.1 178.0 %all-gather.11.cloned.1.call-start = ((), (), s32[]{:S(2)}) async-start(), calls=%async_computation.8 | async-start | bytes 5242880 | tf_op jit(solution)/shard_map/all_gather | solution.py:1341
  137.7 351.4 %reduce-scatter.5.cloned.1.call-start = ((), (), s32[]{:S(2)}) async-start(), calls=%async_computation.9 | async-start | bytes 5242880 | tf_op jit(solution)/shard_map/reduce_scatter | solution.py:1337
  152.3 40.1 %collective-permute-start.9 = (bf16[256,256]{1,0:T(8,128)(2,1)}, bf16[256,256]{1,0:T(8,128)(2,1)S(1)}, u32[]{:S(2)}, u32[]{:S(2)}) collective-permute-start(bf16[256,256]{1,0:T(8,128)(2,1)} %get-tuple-element.163), channel_id=1, source_target_pairs={{0,3},{1,2},{2,1},{3,0},{4,7},{5,6},{6,5},{7,4},{8,11},{9,10},{10,... | collective-permute-start | bytes 393224 | tf_op jit(solution)/shard_map/ppermute | solution.py:790
  152.7 39.8 %collective-permute-start.10 = (bf16[256,256]{1,0:T(8,128)(2,1)}, bf16[256,256]{1,0:T(8,128)(2,1)S(1)}, u32[]{:S(2)}, u32[]{:S(2)}) collective-permute-start(bf16[256,256]{1,0:T(8,128)(2,1)} %get-tuple-element.164), channel_id=1, source_target_pairs={{0,4},{1,5},{2,6},{3,7},{4,0},{5,1},{6,2},{7,3},{8,12},{9,13},{10,... | collective-permute-start | bytes 393224 | tf_op jit(solution)/shard_map/ppermute | solution.py:790
  154.1 38.3 %collective-permute-start.11 = (bf16[256,256]{1,0:T(8,128)(2,1)}, bf16[256,256]{1,0:T(8,128)(2,1)S(1)}, u32[]{:S(2)}, u32[]{:S(2)}) collective-permute-start(bf16[256,256]{1,0:T(8,128)(2,1)} %get-tuple-element.165), channel_id=1, source_target_pairs={{0,5},{1,4},{2,7},{3,6},{4,1},{5,0},{6,3},{7,2},{8,13},{9,12},{10,... | collective-permute-start | bytes 393224 | tf_op jit(solution)/shard_map/ppermute | solution.py:790
  154.3 38.1 %collective-permute-start.12 = (bf16[256,256]{1,0:T(8,128)(2,1)}, bf16[256,256]{1,0:T(8,128)(2,1)S(1)}, u32[]{:S(2)}, u32[]{:S(2)}) collective-permute-start(bf16[256,256]{1,0:T(8,128)(2,1)} %get-tuple-element.166), channel_id=1, source_target_pairs={{0,6},{1,7},{2,4},{3,5},{4,2},{5,3},{6,0},{7,1},{8,14},{9,15},{10,... | collective-permute-start | bytes 393224 | tf_op jit(solution)/shard_map/ppermute | solution.py:790
  157.3 35.2 %collective-permute-start.13 = (bf16[256,256]{1,0:T(8,128)(2,1)}, bf16[256,256]{1,0:T(8,128)(2,1)S(1)}, u32[]{:S(2)}, u32[]{:S(2)}) collective-permute-start(bf16[256,256]{1,0:T(8,128)(2,1)} %get-tuple-element.167), channel_id=1, source_target_pairs={{0,7},{1,6},{2,5},{3,4},{4,3},{5,2},{6,1},{7,0},{8,15},{9,14},{10,... | collective-permute-start | bytes 393224 | tf_op jit(solution)/shard_map/ppermute | solution.py:790
  314.7 201.9 %reduce-scatter.11.cloned.1.call-start = ((), (), s32[]{:S(2)}) async-start(), calls=%async_computation.12 | async-start | bytes 5242880 | tf_op jit(solution)/shard_map/reduce_scatter | solution.py:1337
  386.3 183.3 %reduce-scatter.7.cloned.1.call-start = ((), (), s32[]{:S(2)}) async-start(), calls=%async_computation.10 | async-start | bytes 5242880 | tf_op jit(solution)/shard_map/reduce_scatter | solution.py:1337
  435.3 59.8 %collective-permute-start.21 = (bf16[512,2048]{1,0:T(8,128)(2,1)}, bf16[512,2048]{1,0:T(8,128)(2,1)}, u32[]{:S(2)}, u32[]{:S(2)}) collective-permute-start(bf16[512,2048]{1,0:T(8,128)(2,1)} %get-tuple-element.205), channel_id=1, source_target_pairs={{0,4},{1,3},{2,6},{3,1},{4,0},{5,7},{6,2},{7,5},{8,12},{9,11},{10,... | collective-permute-start | bytes 6291464 | tf_op jit(solution)/shard_map/ppermute | solution.py:800
  488.8 119.7 %reduce-scatter.9.cloned.1.call-start = ((), (), s32[]{:S(2)}) async-start(), calls=%async_computation.11 | async-start | bytes 3276800 | tf_op jit(solution)/shard_map/reduce_scatter | solution.py:1337
  518.8 50.7 %collective-permute-start.23 = (bf16[64,1024]{1,0:T(8,128)(2,1)}, bf16[64,1024]{1,0:T(8,128)(2,1)S(1)}, u32[]{:S(2)}, u32[]{:S(2)}) collective-permute-start(bf16[64,1024]{1,0:T(8,128)(2,1)} %get-tuple-element.230), channel_id=1, source_target_pairs={{0,1},{1,0},{2,3},{3,2},{4,5},{5,4},{6,7},{7,6},{8,9},{9,8},{10,11... | collective-permute-start | bytes 393224 | tf_op jit(solution)/shard_map/ppermute | solution.py:790
  520.0 51.2 %collective-permute-start.24 = (bf16[64,1024]{1,0:T(8,128)(2,1)}, bf16[64,1024]{1,0:T(8,128)(2,1)S(1)}, u32[]{:S(2)}, u32[]{:S(2)}) collective-permute-start(bf16[64,1024]{1,0:T(8,128)(2,1)} %get-tuple-element.231), channel_id=1, source_target_pairs={{0,2},{1,3},{2,0},{3,1},{4,6},{5,7},{6,4},{7,5},{8,10},{9,11},{10,... | collective-permute-start | bytes 393224 | tf_op jit(solution)/shard_map/ppermute | solution.py:790
  521.5 49.8 %collective-permute-start.25 = (bf16[64,1024]{1,0:T(8,128)(2,1)}, bf16[64,1024]{1,0:T(8,128)(2,1)}, u32[]{:S(2)}, u32[]{:S(2)}) collective-permute-start(bf16[64,1024]{1,0:T(8,128)(2,1)} %get-tuple-element.232), channel_id=1, source_target_pairs={{0,3},{1,2},{2,1},{3,0},{4,7},{5,6},{6,5},{7,4},{8,11},{9,10},{10,... | collective-permute-start | bytes 393224 | tf_op jit(solution)/shard_map/ppermute | solution.py:790
  521.5 53.1 %collective-permute-start.26 = (bf16[64,1024]{1,0:T(8,128)(2,1)}, bf16[64,1024]{1,0:T(8,128)(2,1)}, u32[]{:S(2)}, u32[]{:S(2)}) collective-permute-start(bf16[64,1024]{1,0:T(8,128)(2,1)} %get-tuple-element.233), channel_id=1, source_target_pairs={{0,4},{1,5},{2,6},{3,7},{4,0},{5,1},{6,2},{7,3},{8,12},{9,13},{10,... | collective-permute-start | bytes 393224 | tf_op jit(solution)/shard_map/ppermute | solution.py:790
  522.1 52.5 %collective-permute-start.27 = (bf16[64,1024]{1,0:T(8,128)(2,1)}, bf16[64,1024]{1,0:T(8,128)(2,1)}, u32[]{:S(2)}, u32[]{:S(2)}) collective-permute-start(bf16[64,1024]{1,0:T(8,128)(2,1)} %get-tuple-element.234), channel_id=1, source_target_pairs={{0,5},{1,4},{2,7},{3,6},{4,1},{5,0},{6,3},{7,2},{8,13},{9,12},{10,... | collective-permute-start | bytes 393224 | tf_op jit(solution)/shard_map/ppermute | solution.py:790
  (38 other events, 498.1 us)
Sparse Core Ops, SparseCore 0:
  9.6 83.4 all-gather.4
  94.7 53.3 all-gather.6
  150.2 79.5 all-gather.8
  231.2 79.2 all-gather.10
  314.8 79.4 reduce-scatter.4
  396.5 77.2 reduce-scatter.10
  476.1 77.2 reduce-scatter.6
  555.8 52.6 reduce-scatter.8

commit v7 on v6

--- a/solution.py
+++ b/solution.py
@@ -1289,14 +1289,16 @@
     )(first, query, keys, key_columns, values, mixed, grad, weight, lse, start, table)
 
 
-def projection_grad(normed, grad, out_grad):
+def projection_grad(normed, grad, out_grad=None):
     tokens, model = normed.shape
-    columns, more = grad.shape[1], out_grad.shape[1]
+    beside = () if out_grad is None else (out_grad,)
+    columns, more = grad.shape[1], sum(value.shape[1] for value in beside)
     tile = 512
 
-    def kernel(normed_ref, grad_ref, out_grad_ref, result_ref):
-        result_ref[:, :columns] = dot_tn(normed_ref[...], grad_ref[...]).astype(BF16)
-        result_ref[:, columns:] = out_grad_ref[...]
+    def kernel(normed_ref, grad_ref, *refs):
+        refs[-1][:, :columns] = dot_tn(normed_ref[...], grad_ref[...]).astype(BF16)
+        if more:
+            refs[-1][:, columns:] = refs[0][...]
 
     return pl.pallas_call(
         kernel,
@@ -1304,8 +1306,8 @@
         in_specs=[
             pl.BlockSpec((tokens, tile), lambda i: (0, i)),
             pl.BlockSpec((tokens, columns), lambda i: (0, 0)),
-            pl.BlockSpec((tile, more), lambda i: (i, 0)),
-        ],
+        ]
+        + [pl.BlockSpec((tile, more), lambda i: (i, 0))] * len(beside),
         out_specs=pl.BlockSpec((tile, columns + more), lambda i: (i, 0)),
         out_shape=jax.ShapeDtypeStruct((model, columns + more), BF16),
         compiler_params=pltpu.CompilerParams(vmem_limit_bytes=VMEM_BYTES),
@@ -1313,7 +1315,7 @@
             flops=2 * tokens * model * columns, bytes_accessed=2 * tokens * model, transcendentals=0
         ),
         name="projection_grad",
-    )(normed, grad, out_grad)
+    )(normed, grad, *beside)
 
 
 def token_starts(lengths_row, group_tokens):
@@ -1442,7 +1444,7 @@
         hiddens.append(hidden)
         grad_boths.append(grad_both)
         if chunk < CHUNKS - 1 or not fused:
-            gate_up_grad = dot_tn(normed_two, grad_both).astype(BF16)
+            gate_up_grad = projection_grad(normed_two, grad_both)
             gate_up_grads.append(sum_over_groups(gate_up_grad))
             normed_two, grad_two, hiddens, grad_boths, _ = lax.optimization_barrier(
                 (normed_two, grad_two, hiddens, grad_boths, gate_up_grad)

time: 641 us -> 639 us (level)
  Pallas kernels: 486 us -> 509 us
  matrix products: 14 us -> 0 us
  waiting for transfers between devices: 42.2 us -> 33.4 us
    dot_general x1 -> x0, matrix products: 14 us -> none  [dot_tn(): lax.dot_general(left, right, (((0,), (0,)), ((), ())), preferred_element_...]
    pallas_call x1 -> x2, Pallas kernels: 8.86 us -> 22.2 us  [projection_grad(): pl.pallas_call(kernel, grid=(model // tile,), in_specs=[pl.BlockSpec((tok...]
    reduce_scatter x4, waiting for transfers between devices: 15.5 us -> 6.67 us  [sum_over_groups(): return lax.psum_scatter(value, 'dp', scatter_dimension=0, tiled=True)]
  transfers between devices with their start and end apart: 39 -> 39, of which waited for: 7 -> 7; matrix products, arithmetic and copies ran while one was open for 8% -> 6% of each run, Pallas kernels for 75% -> 78%
where the time goes in v7:
time: 639 us; the launch traced here: 631 us
  Pallas kernels  509 us (80%)
  starting transfers between devices  34.7 us (5%)
  waiting for transfers between devices  33.4 us (5%)
  other arithmetic  30.7 us (5%)
  between operations  15.2 us (2%)
  local copies, waits for them, and re-layouts  8.3 us (1%)
    pallas_call x4, Pallas kernels, plane_gather(): pl.pallas_call(functools.partial(gather_kernel, member_count, in_order, c...  173 us
    pallas_call x3, Pallas kernels, product_scatter(): pl.pallas_call(functools.partial(product_scatter_kernel, member_count, in...  138 us
    pallas_call x1, Pallas kernels, attention_backward(): pl.pallas_call(functools.partial(backward_kernel, heads), grid_spec=pltpu...  51 us
    pallas_call x2, Pallas kernels, hidden_units(): pl.pallas_call(units_kernel, grid=(tokens // tile,), in_specs=[by_tile, b...  38.8 us
    pallas_call x1, Pallas kernels, attention_forward(): pl.pallas_call(functools.partial(forward_kernel, heads), grid_spec=pltpu....  38.2 us
    ppermute x28, starting transfers between devices, exchanged(): lax.ppermute(blocks[away], 'fsdp', [(m, m ^ away) for m in range(len(bloc...  27.4 us
    pallas_call x8, Pallas kernels, local_call(): pl.pallas_call(kernel, grid_spec=pltpu.PrefetchScalarGridSpec(num_scalar_...  23.8 us
    pallas_call x2, Pallas kernels, projection_grad(): pl.pallas_call(kernel, grid=(model // tile,), in_specs=[pl.BlockSpec((tok...  22.2 us
  transfers between devices with their start and end apart: 39, of which 7 were waited for; matrix products, arithmetic and copies ran while one was open for 6% of the time, Pallas kernels for 78%

profile of v7, /device:TPU:0, one launch (start us, length us, event | category | flops | bytes accessed | tf_op | source)
XLA Modules:
  0.0 631.3 jit_solution(186481077350242408)
XLA Ops:
  12.6 11.9 %plane_swap.1 = bf16[8,64,640]{2,1,0:T(8,128)(2,1)} custom-call(bf16[8,64,640]{2,1,0:T(8,128)(2,1)} %pad_maximum_fusion.1.refs_0_), custom_call_target="tpu_custom_call" | custom-call | bytes 19660800 | tf_op jit(solution)/shard_map/plane_swap/pallas_call | solution.py:332
  25.3 3.3 units_apart.1
  35.2 3.7 multiply_cosine_fusion
  42.9 50.2 %plane_gather.4.normed_ref = bf16[2048,2048]{1,0:T(8,128)(2,1)} custom-call(bf16[256,2048]{1,0:T(8,128)(2,1)} %fusion.3.own_ref), custom_call_target="tpu_custom_call" | custom-call | bytes 251658240 | tf_op jit(solution)/shard_map/plane_gather/pallas_call | solution.py:271
  94.5 39.6 %plane_gather.5.gradient_ref.refs_2_ = bf16[2048,2048]{1,0:T(8,128)(2,1)} custom-call(bf16[256,2048]{1,0:T(8,128)(2,1)} %fusion.own_ref), custom_call_target="tpu_custom_call" | custom-call | bytes 251658240 | tf_op jit(solution)/shard_map/plane_gather/pallas_call | solution.py:271
  138.0 10.1 %all-gather.7.cloned.1.call-done.weight_ref.value_ref.refs_1_ = bf16[2048,640]{1,0:T(8,128)(2,1)} async-done(((bf16[512,640]{1,0:T(8,128)(2,1)}), bf16[2048,640]{1,0:T(8,128)(2,1)}) %all-gather.7.cloned.1.call-update) | async-done | bytes 2621456 | tf_op jit(solution)/shard_map/all_gather | solution.py:1343
  158.6 38.2 %attention_forward.1 = (bf16[2048,256]{1,0:T(8,128)(2,1)}, bf16[2048,256]{1,0:T(8,128)(2,1)}, bf16[64,2048]{1,0:T(8,128)(2,1)}, bf16[2048,256]{1,0:T(8,128)(2,1)...) custom-call(s32[8]{0:T(128)} %and_select_fusion.first_ref, bf16[2048,2048]{1,0:T(8,128)(2,1)} %plane_gather.4.normed_ref, ...), custom_call_target="tpu_custom_call" | custom-call | flops 8589934592 | bytes 4194304 | tf_op jit(solution)/shard_map/attention_forward/pallas_call | solution.py:1104
  200.1 43.2 %product_scatter.3 = f32[256,2048]{1,0:T(8,128)} custom-call(bf16[2048,256]{1,0:T(8,128)(2,1)} %get-tuple-element.168.refs_0_.mixed_ref, bf16[256,2048]{1,0:T(8,128)(2,1)} %columns_together.1.refs_1_.weight_ref), custom_call_target="tpu_custom_call" | custom-call | bytes 251658240 | tf_op jit(solution)/shard_map/product_scatter/pallas_call | solution.py:588
  246.4 39.0 %plane_gather.6.normed_ref.refs_0_ = bf16[2048,2048]{1,0:T(8,128)(2,1)} custom-call(bf16[256,2048]{1,0:T(8,128)(2,1)} %multiply_convert_fusion.1.own_ref), custom_call_target="tpu_custom_call" | custom-call | bytes 251658240 | tf_op jit(solution)/shard_map/plane_gather/pallas_call | solution.py:271
  285.4 19.4 %hidden_units.2 = (bf16[2048,512]{1,0:T(8,128)(2,1)}, bf16[2048,1024]{1,0:T(8,128)(2,1)}) custom-call(bf16[2048,2048]{1,0:T(8,128)(2,1)} %plane_gather.6.normed_ref.refs_0_, bf16[2048,2048]{1,0:T(8,128)(2,1)} %plane_gather.5.gradient_ref.refs_2_, bf16[2048,1024]{1,0:T(8,128)(2,1)} %all-gather.9.cloned.1.call-done.both_ref.refs_3_, ...), custom_call_target="tpu_custom_call" | custom-call | flops 12884901888 | bytes 23068672 | tf_op jit(solution)/shard_map/hidden_units/pallas_call | solution.py:950
  304.8 13.3 %projection_grad.2 = bf16[2048,1024]{1,0:T(8,128)(2,1)} custom-call(bf16[2048,2048]{1,0:T(8,128)(2,1)} %plane_gather.6.normed_ref.refs_0_, bf16[2048,1024]{1,0:T(8,128)(2,1)} %get-tuple-element.186.grad_ref.refs_1_), custom_call_target="tpu_custom_call" | custom-call | flops 8589934592 | bytes 8388608 | tf_op jit(solution)/shard_map/projection_grad/pallas_call | solution.py:1303
  318.6 19.4 %hidden_units.3 = (bf16[2048,512]{1,0:T(8,128)(2,1)}, bf16[2048,1024]{1,0:T(8,128)(2,1)}) custom-call(bf16[2048,2048]{1,0:T(8,128)(2,1)} %plane_gather.6.normed_ref.refs_0_, bf16[2048,2048]{1,0:T(8,128)(2,1)} %plane_gather.5.gradient_ref.refs_2_, bf16[2048,1024]{1,0:T(8,128)(2,1)} %all-gather.11.cloned.1.call-done.both_ref.refs_4_, ...), custom_call_target="tpu_custom_call" | custom-call | flops 12884901888 | bytes 23068672 | tf_op jit(solution)/shard_map/hidden_units/pallas_call | solution.py:950
  338.0 51.7 %product_scatter.4 = (f32[256,2048]{1,0:T(8,128)}, bf16[2048,1024]{1,0:T(8,128)(2,1)}) custom-call(bf16[2048,2048]{1,0:T(8,128)(2,1)} %plane_gather.6.normed_ref.refs_0_, bf16[2048,1024]{1,0:T(8,128)(2,1)} %get-tuple-element.186.grad_ref.refs_1_, bf16[2048,1024]{1,0:T(8,128)(2,1)} %get-tuple-element.188.refs_2_, ...), custom_call_target="tpu_custom_call" | custom-call | bytes 251658240 | tf_op jit(solution)/shard_map/product_scatter/pallas_call | solution.py:588
  394.7 44.1 %plane_gather.7 = (bf16[2048,2048]{1,0:T(8,128)(2,1)}, bf16[1024,2048]{1,0:T(8,128)(2,1)}, bf16[512,2048]{1,0:T(8,128)(2,1)}, bf16[512,2048]{1,0:T(8,128)(2,1)}) custom-call(bf16[256,2048]{1,0:T(8,128)(2,1)} %get-tuple-element.261.own_ref, bf16[2048,512]{1,0:T(8,128)(2,1)} %get-tuple-element.190.refs_0_, bf16[2048,512]{1,0:T(8,128)(2,1)} %get-tuple-element.191.refs_1_, ...), custom_call_target="tpu_custom_call" | custom-call | bytes 4194304 | tf_op jit(solution)/shard_map/plane_gather/pallas_call | solution.py:271
  439.3 51.0 %attention_backward.1 = (bf16[2048,384]{1,0:T(8,128)(2,1)}, bf16[256,2048]{1,0:T(8,128)(2,1)}) custom-call(s32[8]{0:T(128)} %and_select_fusion.first_ref, bf16[2048,256]{1,0:T(8,128)(2,1)} %get-tuple-element.177.query_ref, bf16[2048,256]{1,0:T(8,128)(2,1)} %get-tuple-element.178.key_ref, bf16[64,2048]{1,0:T(8,128)(2,1)} %get-tuple-element.179.key_columns_ref, ...), custom_call_target="tpu_custom_call" | custom-call | bytes 524288 | tf_op jit(solution)/shard_map/attention_backward/pallas_call | solution.py:1252
  492.5 4.2 all-to-all-start
  505.8 8.7 %collective-permute-done.15.refs_2_ = bf16[64,1024]{1,0:T(8,128)(2,1)S(1)} collective-permute-done((bf16[64,1024]{1,0:T(8,128)(2,1)}, bf16[64,1024]{1,0:T(8,128)(2,1)S(1)}, u32[]{:S(2)}, u32[]{:S(2)}) %collective-permute-start.15) | collective-permute-done | bytes 131104 | tf_op jit(solution)/shard_map/ppermute | solution.py:790
  514.8 8.9 %projection_grad.3 = bf16[2048,640]{1,0:T(8,128)(2,1)} custom-call(bf16[2048,2048]{1,0:T(8,128)(2,1)} %plane_gather.4.normed_ref, bf16[2048,384]{1,0:T(8,128)(2,1)} %get-tuple-element.209.grad_ref.refs_0_, bf16[2048,256]{1,0:T(8,128)(2,1)} %bitcast.12.refs_0_), custom_call_target="tpu_custom_call" | custom-call | flops 3221225472 | bytes 8388608 | tf_op jit(solution)/shard_map/projection_grad/pallas_call | solution.py:1303
  534.5 43.2 %product_scatter.5 = f32[256,2048]{1,0:T(8,128)} custom-call(bf16[2048,384]{1,0:T(8,128)(2,1)} %get-tuple-element.209.grad_ref.refs_0_, bf16[2048,640]{1,0:T(8,128)(2,1)} %all-gather.7.cloned.1.call-done.weight_ref.value_ref.refs_1_), custom_call_target="tpu_custom_call" | custom-call | bytes 4194304 | tf_op jit(solution)/shard_map/product_scatter/pallas_call | solution.py:588
  587.3 5.3 units_together.1
  592.6 3.2 fusion.6
  598.0 3.1 add_convert_fusion
  601.2 6.6 %reduce-scatter.9.cloned.1.call-done.packed_ref = bf16[512,640]{1,0:T(8,128)(2,1)} async-done(((bf16[2048,640]{1,0:T(8,128)(2,1)}), bf16[512,640]{1,0:T(8,128)(2,1)}) %reduce-scatter.9.cloned.1.call-update) | async-done | bytes 655376 | tf_op jit(solution)/shard_map/reduce_scatter | solution.py:1339
  607.8 12.5 %finale.1 = (bf16[8,64,640]{2,1,0:T(8,128)(2,1)}, f32[8,128]{1,0:T(8,128)}) custom-call(bf16[512,640]{1,0:T(8,128)(2,1)} %reduce-scatter.9.cloned.1.call-done.packed_ref, f32[8,8,128]{2,1,0:T(8,128)} %pad.4.part_ref), custom_call_target="tpu_custom_call" | custom-call | bytes 40000000 | tf_op jit(solution)/shard_map/finale/pallas_call | solution.py:703
  (177 shorter events, 82.6 us)
Async XLA Ops:
  7.2 87.3 %all-gather.5.cloned.1.call-start = ((), (), s32[]{:S(2)}) async-start(), calls=%async_computation.5 | async-start | bytes 5242880 | tf_op jit(solution)/shard_map/all_gather | solution.py:1343
  7.9 140.1 %all-gather.7.cloned.1.call-start = ((), (), s32[]{:S(2)}) async-start(), calls=%async_computation.6 | async-start | bytes 3276800 | tf_op jit(solution)/shard_map/all_gather | solution.py:1343
  24.6 260.9 %all-gather.9.cloned.1.call-start = ((), (), s32[]{:S(2)}) async-start(), calls=%async_computation.7 | async-start | bytes 5242880 | tf_op jit(solution)/shard_map/all_gather | solution.py:1343
  31.0 103.1 %collective-permute-start.2 = (bf16[64,2048]{1,0:T(8,128)(2,1)}, bf16[64,2048]{1,0:T(8,128)(2,1)}, u32[]{:S(2)}, u32[]{:S(2)}) collective-permute-start(bf16[64,2048]{1,0:T(8,128)(2,1)} %get-tuple-element.140), channel_id=1, source_target_pairs={{0,3},{1,2},{2,1},{3,0},{4,7},{5,6},{6,5},{7,4},{8,11},{9,10},{10,... | collective-permute-start | bytes 786440 | tf_op jit(solution)/shard_map/ppermute | solution.py:790
  31.2 102.8 %collective-permute-start.3 = (bf16[64,2048]{1,0:T(8,128)(2,1)}, bf16[64,2048]{1,0:T(8,128)(2,1)}, u32[]{:S(2)}, u32[]{:S(2)}) collective-permute-start(bf16[64,2048]{1,0:T(8,128)(2,1)} %get-tuple-element.141), channel_id=1, source_target_pairs={{0,4},{1,5},{2,6},{3,7},{4,0},{5,1},{6,2},{7,3},{8,12},{9,13},{10,... | collective-permute-start | bytes 786440 | tf_op jit(solution)/shard_map/ppermute | solution.py:790
  32.6 101.4 %collective-permute-start.4 = (bf16[64,2048]{1,0:T(8,128)(2,1)}, bf16[64,2048]{1,0:T(8,128)(2,1)}, u32[]{:S(2)}, u32[]{:S(2)}) collective-permute-start(bf16[64,2048]{1,0:T(8,128)(2,1)} %get-tuple-element.142), channel_id=1, source_target_pairs={{0,5},{1,4},{2,7},{3,6},{4,1},{5,0},{6,3},{7,2},{8,13},{9,12},{10,... | collective-permute-start | bytes 786440 | tf_op jit(solution)/shard_map/ppermute | solution.py:790
  40.2 93.9 %collective-permute-start.5 = (bf16[64,2048]{1,0:T(8,128)(2,1)}, bf16[64,2048]{1,0:T(8,128)(2,1)}, u32[]{:S(2)}, u32[]{:S(2)}) collective-permute-start(bf16[64,2048]{1,0:T(8,128)(2,1)} %get-tuple-element.143), channel_id=1, source_target_pairs={{0,6},{1,7},{2,4},{3,5},{4,2},{5,3},{6,0},{7,1},{8,14},{9,15},{10,... | collective-permute-start | bytes 786440 | tf_op jit(solution)/shard_map/ppermute | solution.py:790
  42.2 91.9 %collective-permute-start.6 = (bf16[64,2048]{1,0:T(8,128)(2,1)}, bf16[64,2048]{1,0:T(8,128)(2,1)}, u32[]{:S(2)}, u32[]{:S(2)}) collective-permute-start(bf16[64,2048]{1,0:T(8,128)(2,1)} %get-tuple-element.144), channel_id=1, source_target_pairs={{0,7},{1,6},{2,5},{3,4},{4,3},{5,2},{6,1},{7,0},{8,15},{9,14},{10,... | collective-permute-start | bytes 786440 | tf_op jit(solution)/shard_map/ppermute | solution.py:790
  137.1 181.5 %all-gather.11.cloned.1.call-start = ((), (), s32[]{:S(2)}) async-start(), calls=%async_computation.8 | async-start | bytes 5242880 | tf_op jit(solution)/shard_map/all_gather | solution.py:1343
  137.7 359.4 %reduce-scatter.5.cloned.1.call-start = ((), (), s32[]{:S(2)}) async-start(), calls=%async_computation.9 | async-start | bytes 5242880 | tf_op jit(solution)/shard_map/reduce_scatter | solution.py:1339
  152.3 44.6 %collective-permute-start.9 = (bf16[256,256]{1,0:T(8,128)(2,1)}, bf16[256,256]{1,0:T(8,128)(2,1)S(1)}, u32[]{:S(2)}, u32[]{:S(2)}) collective-permute-start(bf16[256,256]{1,0:T(8,128)(2,1)} %get-tuple-element.163), channel_id=1, source_target_pairs={{0,3},{1,2},{2,1},{3,0},{4,7},{5,6},{6,5},{7,4},{8,11},{9,10},{10,... | collective-permute-start | bytes 393224 | tf_op jit(solution)/shard_map/ppermute | solution.py:790
  152.7 44.2 %collective-permute-start.10 = (bf16[256,256]{1,0:T(8,128)(2,1)}, bf16[256,256]{1,0:T(8,128)(2,1)S(1)}, u32[]{:S(2)}, u32[]{:S(2)}) collective-permute-start(bf16[256,256]{1,0:T(8,128)(2,1)} %get-tuple-element.164), channel_id=1, source_target_pairs={{0,4},{1,5},{2,6},{3,7},{4,0},{5,1},{6,2},{7,3},{8,12},{9,13},{10,... | collective-permute-start | bytes 393224 | tf_op jit(solution)/shard_map/ppermute | solution.py:790
  154.1 42.8 %collective-permute-start.11 = (bf16[256,256]{1,0:T(8,128)(2,1)}, bf16[256,256]{1,0:T(8,128)(2,1)S(1)}, u32[]{:S(2)}, u32[]{:S(2)}) collective-permute-start(bf16[256,256]{1,0:T(8,128)(2,1)} %get-tuple-element.165), channel_id=1, source_target_pairs={{0,5},{1,4},{2,7},{3,6},{4,1},{5,0},{6,3},{7,2},{8,13},{9,12},{10,... | collective-permute-start | bytes 393224 | tf_op jit(solution)/shard_map/ppermute | solution.py:790
  154.3 42.6 %collective-permute-start.12 = (bf16[256,256]{1,0:T(8,128)(2,1)}, bf16[256,256]{1,0:T(8,128)(2,1)S(1)}, u32[]{:S(2)}, u32[]{:S(2)}) collective-permute-start(bf16[256,256]{1,0:T(8,128)(2,1)} %get-tuple-element.166), channel_id=1, source_target_pairs={{0,6},{1,7},{2,4},{3,5},{4,2},{5,3},{6,0},{7,1},{8,14},{9,15},{10,... | collective-permute-start | bytes 393224 | tf_op jit(solution)/shard_map/ppermute | solution.py:790
  157.3 39.6 %collective-permute-start.13 = (bf16[256,256]{1,0:T(8,128)(2,1)}, bf16[256,256]{1,0:T(8,128)(2,1)S(1)}, u32[]{:S(2)}, u32[]{:S(2)}) collective-permute-start(bf16[256,256]{1,0:T(8,128)(2,1)} %get-tuple-element.167), channel_id=1, source_target_pairs={{0,7},{1,6},{2,5},{3,4},{4,3},{5,2},{6,1},{7,0},{8,15},{9,14},{10,... | collective-permute-start | bytes 393224 | tf_op jit(solution)/shard_map/ppermute | solution.py:790
  318.1 206.4 %reduce-scatter.11.cloned.1.call-start = ((), (), s32[]{:S(2)}) async-start(), calls=%async_computation.12 | async-start | bytes 5242880 | tf_op jit(solution)/shard_map/reduce_scatter | solution.py:1339
  389.7 188.0 %reduce-scatter.7.cloned.1.call-start = ((), (), s32[]{:S(2)}) async-start(), calls=%async_computation.10 | async-start | bytes 5242880 | tf_op jit(solution)/shard_map/reduce_scatter | solution.py:1339
  438.8 64.3 %collective-permute-start.21 = (bf16[512,2048]{1,0:T(8,128)(2,1)}, bf16[512,2048]{1,0:T(8,128)(2,1)}, u32[]{:S(2)}, u32[]{:S(2)}) collective-permute-start(bf16[512,2048]{1,0:T(8,128)(2,1)} %get-tuple-element.205), channel_id=1, source_target_pairs={{0,4},{1,3},{2,6},{3,1},{4,0},{5,7},{6,2},{7,5},{8,12},{9,11},{10,... | collective-permute-start | bytes 6291464 | tf_op jit(solution)/shard_map/ppermute | solution.py:800
  496.8 111.0 %reduce-scatter.9.cloned.1.call-start = ((), (), s32[]{:S(2)}) async-start(), calls=%async_computation.11 | async-start | bytes 3276800 | tf_op jit(solution)/shard_map/reduce_scatter | solution.py:1339
  526.8 50.9 %collective-permute-start.23 = (bf16[64,1024]{1,0:T(8,128)(2,1)}, bf16[64,1024]{1,0:T(8,128)(2,1)S(1)}, u32[]{:S(2)}, u32[]{:S(2)}) collective-permute-start(bf16[64,1024]{1,0:T(8,128)(2,1)} %get-tuple-element.230), channel_id=1, source_target_pairs={{0,1},{1,0},{2,3},{3,2},{4,5},{5,4},{6,7},{7,6},{8,9},{9,8},{10,11... | collective-permute-start | bytes 393224 | tf_op jit(solution)/shard_map/ppermute | solution.py:790
  528.1 51.2 %collective-permute-start.24 = (bf16[64,1024]{1,0:T(8,128)(2,1)}, bf16[64,1024]{1,0:T(8,128)(2,1)S(1)}, u32[]{:S(2)}, u32[]{:S(2)}) collective-permute-start(bf16[64,1024]{1,0:T(8,128)(2,1)} %get-tuple-element.231), channel_id=1, source_target_pairs={{0,2},{1,3},{2,0},{3,1},{4,6},{5,7},{6,4},{7,5},{8,10},{9,11},{10,... | collective-permute-start | bytes 393224 | tf_op jit(solution)/shard_map/ppermute | solution.py:790
  529.6 49.9 %collective-permute-start.25 = (bf16[64,1024]{1,0:T(8,128)(2,1)}, bf16[64,1024]{1,0:T(8,128)(2,1)}, u32[]{:S(2)}, u32[]{:S(2)}) collective-permute-start(bf16[64,1024]{1,0:T(8,128)(2,1)} %get-tuple-element.232), channel_id=1, source_target_pairs={{0,3},{1,2},{2,1},{3,0},{4,7},{5,6},{6,5},{7,4},{8,11},{9,10},{10,... | collective-permute-start | bytes 393224 | tf_op jit(solution)/shard_map/ppermute | solution.py:790
  529.6 53.1 %collective-permute-start.26 = (bf16[64,1024]{1,0:T(8,128)(2,1)}, bf16[64,1024]{1,0:T(8,128)(2,1)}, u32[]{:S(2)}, u32[]{:S(2)}) collective-permute-start(bf16[64,1024]{1,0:T(8,128)(2,1)} %get-tuple-element.233), channel_id=1, source_target_pairs={{0,4},{1,5},{2,6},{3,7},{4,0},{5,1},{6,2},{7,3},{8,12},{9,13},{10,... | collective-permute-start | bytes 393224 | tf_op jit(solution)/shard_map/ppermute | solution.py:790
  530.1 52.6 %collective-permute-start.27 = (bf16[64,1024]{1,0:T(8,128)(2,1)}, bf16[64,1024]{1,0:T(8,128)(2,1)}, u32[]{:S(2)}, u32[]{:S(2)}) collective-permute-start(bf16[64,1024]{1,0:T(8,128)(2,1)} %get-tuple-element.234), channel_id=1, source_target_pairs={{0,5},{1,4},{2,7},{3,6},{4,1},{5,0},{6,3},{7,2},{8,13},{9,12},{10,... | collective-permute-start | bytes 393224 | tf_op jit(solution)/shard_map/ppermute | solution.py:790
  (38 other events, 498.3 us)
Sparse Core Ops, SparseCore 0:
  9.6 83.4 all-gather.4
  94.7 53.3 all-gather.6
  150.2 79.5 all-gather.8
  231.2 79.2 all-gather.10
  318.3 75.2 reduce-scatter.4
  395.8 77.2 reduce-scatter.10
  475.4 77.2 reduce-scatter.6
  555.1 52.5 reduce-scatter.8
